TPU v7x, 32 devices: a whole 2x2x4 slice. The times are simulated.
32 devices in a mesh: dp: 8 (over z, y), expert: 4 (over x, core).
Axes of the slice: x: 2, y: 2, z: 4, core: 2. Of those that a mesh axis runs over, the one named last changes fastest.
Arguments:
- tokens: bfloat16 [1024, 7168], P('dp', 'expert'), may hold values from -6 to 6
- cotangent: bfloat16 [1024, 7168], P('dp', 'expert'), may hold values from -6 to 6
- gates: bfloat16 [1024, 2], P('dp'), may hold values from 0.19921875 to 2.5
- expert_ids: int32 [1024, 2], P('dp'), may hold values from 0 to 8, as said below
- w_gate: bfloat16 [8, 7168, 2048], P('dp', None, 'expert'), may hold values from -0.0625 to 0.0625
- w_up: bfloat16 [8, 7168, 2048], P('dp', None, 'expert'), may hold values from -0.0625 to 0.0625
- w_down: bfloat16 [8, 2048, 7168], P('dp', 'expert'), may hold values from -0.125 to 0.125
Outputs:
- grad_tokens: bfloat16 [1024, 7168], P('dp', 'expert')
- gate_grads: float32 [1024, 2], P('dp')
- grad_gate: bfloat16 [8, 7168, 2048], P('dp', None, 'expert')
- grad_up: bfloat16 [8, 7168, 2048], P('dp', None, 'expert')
- grad_down: bfloat16 [8, 2048, 7168], P('dp', 'expert')
Inputs may be any that keep to these rules, and one draw needn't show every extreme that they name: `expert_ids`: column 0 names one of the experts 0 to half of 8 minus 1 and column 1 one of the others, or the value 8 for a choice outside this window. The 128 tokens of one index of dp route at most 8 tokens to one expert; in each column one expert, the same for every index of dp, receives exactly 8 tokens from every index of dp.
All inputs are finite; a program needn't handle non-finite values.
Results may differ from a plain program's by a relative error of at most 0.024.
Values may be sent and summed in bfloat16 or wider, within the bound.
No kernel may reach another device: no remote copies, remote signals or barrier semaphores. Data moves between devices by JAX's collectives and lax.ppermute only.
A program may use at most 128 MiB of HBM per device.

v0:
```python
import jax
import jax.numpy as jnp
from jax import lax
from jax.sharding import PartitionSpec as P

CAP = 8


def per_device(tokens, cotangent, gates, expert_ids, w_gate, w_up, w_down):
    experts = lax.axis_size("dp")
    labels = jnp.arange(experts, dtype=jnp.int32)
    first = expert_ids[:, 0:1] == labels[None, :]
    second = expert_ids[:, 1:2] == labels[None, :]
    member = jnp.logical_or(first, second)
    gate_f = gates.astype(jnp.float32)
    route = jnp.where(first, gate_f[:, 0:1], 0.0) + jnp.where(second, gate_f[:, 1:2], 0.0)
    places = jnp.cumsum(member.astype(jnp.int32), axis=0) - 1
    slot_ids = jnp.arange(CAP, dtype=jnp.int32)
    picker = jnp.logical_and(member.T[:, None, :], places.T[:, None, :] == slot_ids[None, :, None])
    picker_low = picker.astype(jnp.bfloat16)
    slot_gates = jnp.sum(jnp.where(picker, route.T[:, None, :], 0.0), axis=2).astype(jnp.bfloat16)
    slot_x = jnp.einsum(
        "est,tf->esf", picker_low, tokens, preferred_element_type=jnp.float32
    ).astype(jnp.bfloat16)
    slot_d = jnp.einsum(
        "est,tf->esf", picker_low, cotangent, preferred_element_type=jnp.float32
    ).astype(jnp.bfloat16)
    slot_x, slot_d, slot_g = (
        lax.all_to_all(slot_x, "dp", split_axis=0, concat_axis=0, tiled=True),
        lax.all_to_all(slot_d, "dp", split_axis=0, concat_axis=0, tiled=True),
        lax.all_to_all(slot_gates, "dp", split_axis=0, concat_axis=0, tiled=True),
    )
    slot_x, slot_d = (
        lax.all_gather(slot_x, "expert", axis=2, tiled=True),
        lax.all_gather(slot_d, "expert", axis=2, tiled=True),
    )
    total_rows = experts * CAP
    x_all = slot_x.reshape(total_rows, slot_x.shape[2])
    d_all = slot_d.reshape(total_rows, slot_d.shape[2])
    g_all = slot_g.reshape(total_rows).astype(jnp.float32)[:, None]
    gate_m = w_gate[0]
    up_m = w_up[0]
    down_m = w_down[0]
    pre_gate = jnp.dot(x_all, gate_m, preferred_element_type=jnp.float32)
    pre_up = jnp.dot(x_all, up_m, preferred_element_type=jnp.float32)
    sig = jax.nn.sigmoid(pre_gate)
    act = pre_gate * sig
    hidden = (act * pre_up).astype(jnp.bfloat16)
    back = lax.dot_general(
        d_all, down_m, (((1,), (1,)), ((), ())), preferred_element_type=jnp.float32
    )
    gate_part = jnp.sum(back * hidden.astype(jnp.float32), axis=1)
    dhid = g_all * back
    scaled = (g_all * d_all.astype(jnp.float32)).astype(jnp.bfloat16)
    grad_down = lax.dot_general(
        hidden, scaled, (((0,), (0,)), ((), ())), preferred_element_type=jnp.float32
    ).astype(jnp.bfloat16)
    d_gate = (dhid * pre_up * sig * (1.0 + pre_gate * (1.0 - sig))).astype(jnp.bfloat16)
    d_up = (dhid * act).astype(jnp.bfloat16)
    grad_gate = lax.dot_general(
        x_all, d_gate, (((0,), (0,)), ((), ())), preferred_element_type=jnp.float32
    ).astype(jnp.bfloat16)
    grad_up = lax.dot_general(
        x_all, d_up, (((0,), (0,)), ((), ())), preferred_element_type=jnp.float32
    ).astype(jnp.bfloat16)
    term = lax.dot_general(
        gate_m, d_gate, (((1,), (1,)), ((), ())), preferred_element_type=jnp.float32
    )
    feat_sums = lax.psum_scatter(
        (
            term
            + lax.dot_general(
                up_m, d_up, (((1,), (1,)), ((), ())), preferred_element_type=jnp.float32
            )
        ).astype(jnp.bfloat16),
        "expert",
        scatter_dimension=0,
        tiled=True,
    ).astype(jnp.float32)
    feat_sums = feat_sums.reshape(feat_sums.shape[0], experts, CAP)
    gate_back = lax.psum(gate_part, "expert").reshape(1, experts, CAP)
    feat_back, gate_back = (
        lax.all_to_all(
            feat_sums.astype(jnp.bfloat16), "dp", split_axis=1, concat_axis=1, tiled=True
        ).astype(feat_sums.dtype),
        lax.all_to_all(
            gate_back.astype(jnp.bfloat16), "dp", split_axis=1, concat_axis=1, tiled=True
        ).astype(gate_back.dtype),
    )
    slot_rows = feat_back.reshape(feat_back.shape[0], total_rows).T
    gate_flat = gate_back.reshape(total_rows)
    inside = expert_ids < experts
    safe_ids = jnp.where(inside, expert_ids, 0)
    slot_place = jnp.take_along_axis(places, safe_ids, axis=1)
    slot_index = safe_ids * CAP + jnp.maximum(slot_place, 0)
    first_rows = jnp.where(inside[:, 0:1], slot_rows[slot_index[:, 0]], 0.0)
    second_rows = jnp.where(inside[:, 1:2], slot_rows[slot_index[:, 1]], 0.0)
    grad_tokens = (first_rows + second_rows).astype(jnp.bfloat16)
    gate_grads = jnp.where(inside, gate_flat[slot_index], 0.0)
    return (grad_tokens, gate_grads, grad_gate[None], grad_up[None], grad_down[None])


def solution(mesh):
    in_specs = (
        P("dp", "expert"),
        P("dp", "expert"),
        P("dp", None),
        P("dp", None),
        P("dp", None, "expert"),
        P("dp", None, "expert"),
        P("dp", "expert", None),
    )
    out_specs = (
        P("dp", "expert"),
        P("dp", None),
        P("dp", None, "expert"),
        P("dp", None, "expert"),
        P("dp", "expert", None),
    )
    return jax.shard_map(
        per_device, mesh=mesh, in_specs=in_specs, out_specs=out_specs, check_vma=False
    )
```

profile of v0, /device:TPU:0, one launch (start us, length us, event | category | flops | bytes accessed | tf_op | source)
XLA Modules:
  0.0 127.5 jit_solution(7503397581649159755)
XLA Ops:
  7.2 0.8 slice_bitcast_fusion.3
  8.1 0.7 convert_element_type.94
  9.1 0.6 copy.23
  9.7 7.3 %all-to-all-start = ((bf16[8,1,8]{2,1,0:T(2,128)(2,1)}), bf16[8,1,8]{2,1,0:T(2,128)(2,1)S(1)}, u32[]{:S(2)}, u32[]{:S(2)}) async-start(bf16[8,1,8]{2,1,0:T(2,128)(2,1)} %copy.23), calls=%async_computation | async-start | bytes 8192 | tf_op jit(solution)/shard_map/all_to_all | solution.py:31
  17.0 0.9 convolution_convert_fusion.3
  17.9 5.5 %all-to-all-done = bf16[8,1,8]{2,1,0:T(2,128)(2,1)S(1)} async-done(((bf16[8,1,8]{2,1,0:T(2,128)(2,1)}), bf16[8,1,8]{2,1,0:T(2,128)(2,1)S(1)}, u32[]{:S(2)}, u32[]{:S(2)}) %all-to-all-start) | async-done | bytes 160 | tf_op jit(solution)/shard_map/all_to_all | solution.py:31
  23.4 3.4 %all-to-all-start.2 = ((bf16[8,8,1792]{2,1,0:T(8,128)(2,1)}), bf16[8,8,1792]{2,1,0:T(8,128)(2,1)S(1)}, u32[]{:S(2)}, u32[]{:S(2)}) async-start(bf16[8,8,1792]{2,1,0:T(8,128)(2,1)} %convolution_convert_fusion.3), calls=%async_computation.2 | async-start | bytes 458752 | tf_op jit(solution)/shard_map/all_to_all | solution.py:29
  26.8 1.9 %convolution_convert_fusion.4 = bf16[8,8,1792]{2,1,0:T(8,128)(2,1)} fusion(bf16[128,1792]{1,0:T(8,128)(2,1)} %param.8, s32[8,128]{1,0:T(8,128)S(1)} %copy.22, pred[8,128]{1,0:T(8,128)(4,1)S(1)} %fusion.35), kind=kOutput, calls=%fused_computation.23 | convolution fusion | flops 29491200 | bytes 693248 | tf_op jit(solution)/shard_map/est,tf->esf/dot_general | solution.py:25
  28.8 5.9 %all-to-all-done.2 = bf16[8,8,1792]{2,1,0:T(8,128)(2,1)S(1)} async-done(((bf16[8,8,1792]{2,1,0:T(8,128)(2,1)}), bf16[8,8,1792]{2,1,0:T(8,128)(2,1)S(1)}, u32[]{:S(2)}, u32[]{:S(2)}) %all-to-all-start.2) | async-done | bytes 229408 | tf_op jit(solution)/shard_map/all_to_all | solution.py:29
  34.7 3.4 %all-to-all-start.1 = ((bf16[8,8,1792]{2,1,0:T(8,128)(2,1)}), bf16[8,8,1792]{2,1,0:T(8,128)(2,1)S(1)}, u32[]{:S(2)}, u32[]{:S(2)}) async-start(bf16[8,8,1792]{2,1,0:T(8,128)(2,1)} %convolution_convert_fusion.4), calls=%async_computation.1 | async-start | bytes 458752 | tf_op jit(solution)/shard_map/all_to_all | solution.py:30
  38.2 9.4 %all_gather.7 = bf16[8,8,7168]{2,1,0:T(8,128)(2,1)S(1)} all-gather(bf16[8,8,1792]{2,1,0:T(8,128)(2,1)S(1)} %all-to-all-done.2), channel_id=1, replica_groups=mesh['dp'=8,'expert'=4] {'expert'}, dimensions={2}, use_global_device_ids=true | all-gather | bytes 1146880 | tf_op jit(solution)/shard_map/all_gather | solution.py:34
  47.6 4.6 %fusion.7 = f32[64,512]{1,0:T(8,128)S(1)} fusion(bf16[1,7168,512]{2,1,0:T(8,128)(2,1)} %param.11, bf16[8,8,7168]{2,1,0:T(8,128)(2,1)S(1)} %all_gather.7), kind=kOutput, calls=%fused_computation.15 | convolution fusion | flops 469762048 | bytes 8388608 | tf_op jit(solution)/shard_map/dot_general | solution.py:44
  52.3 1.4 %fusion.10 = f32[64,512]{1,0:T(8,128)S(1)} fusion(bf16[1,7168,512]{2,1,0:T(8,128)(2,1)S(1)} %bitcast.76, bf16[8,8,7168]{2,1,0:T(8,128)(2,1)S(1)} %all_gather.7), kind=kOutput, calls=%fused_computation.18 | convolution fusion | flops 469762048 | bytes 8388608 | tf_op jit(solution)/shard_map/dot_general | solution.py:45
  53.6 9.4 %all_gather.6 = bf16[8,8,7168]{2,1,0:T(8,128)(2,1)S(1)} all-gather(bf16[8,8,1792]{2,1,0:T(8,128)(2,1)S(1)} %all-to-all-done.1), channel_id=1, replica_groups=mesh['dp'=8,'expert'=4] {'expert'}, dimensions={2}, use_global_device_ids=true | all-gather | bytes 1146880 | tf_op jit(solution)/shard_map/all_gather | solution.py:35
  63.1 5.7 %multiply_reduce_fusion = (f32[64]{0:T(128)S(1)}, bf16[64,512]{1,0:T(8,128)(2,1)S(1)}, bf16[64,512]{1,0:T(8,128)(2,1)S(1)}, bf16[64,512]{1,0:T(8,128)(2,1)S(1)}) fusion(f32[64,512]{1,0:T(8,128)S(1)} %fusion.10, f32[64,512]{1,0:T(8,128)S(1)} %fusion.7, f32[64]{0:T(128)S(1)} %reshape.179, bf16[1,512,7168]{2,1,0:T(8,128)(2,1)} %param.13, ...), kind=kOutput, calls=%fused_computation.40 | convolution fusion | flops 470384576 | bytes 8716800 | tf_op jit(solution)/shard_map/dot_general | solution.py:49
  68.8 5.5 %fusion.5 = f32[64,7168]{1,0:T(8,128)S(1)} fusion(bf16[64,512]{1,0:T(8,128)(2,1)S(1)} %get-tuple-element.30, bf16[1,7168,512]{2,1,0:T(8,128)(2,1)} %param.11), kind=kOutput, calls=%fused_computation.13 | convolution fusion | flops 469762048 | bytes 9240576 | tf_op jit(solution)/shard_map/dot_general | solution.py:66
  74.4 3.3 %fusion.4 = bf16[7168,64]{0,1:T(8,128)(2,1)} fusion(f32[64,7168]{1,0:T(8,128)S(1)} %fusion.5, bf16[64,512]{1,0:T(8,128)(2,1)S(1)} %get-tuple-element.31, bf16[1,7168,512]{2,1,0:T(8,128)(2,1)S(1)} %bitcast.78), kind=kOutput, calls=%fused_computation.12 | convolution fusion | flops 470679552 | bytes 10158080 | tf_op jit(solution)/shard_map/dot_general | solution.py:72
  78.0 1.9 %gather_fusion.3 = s32[256]{0:T(256)S(1)} fusion(s32[128,8]{1,0:T(8,128)S(1)} %get-tuple-element.32, s32[256]{0:T(256)S(1)} %reshape.207), kind=kCustom, calls=%fused_computation.3 | custom fusion | bytes 4096 | tf_op jit(solution)/shard_map/jit(take_along_axis)/gather | solution.py:94
  80.3 0.2 fusion.24
  80.5 0.2 slice_reduce_fusion.1
  80.7 6.2 %psum.7 = bf16[64]{0:T(256)(128)(2,1)S(1)} all-reduce(f32[64]{0:T(128)S(1)} %get-tuple-element.26), channel_id=1, replica_groups=mesh['dp'=8,'expert'=4] {'expert'}, use_global_device_ids=true, to_apply=%region_4.5 | all-reduce | flops 64 | bytes 384 | tf_op jit(solution)/shard_map/psum | solution.py:81
  86.8 0.7 convert_element_type.117
  87.5 5.9 %all-to-all-start.4 = ((bf16[1,8,8]{2,0,1:T(2,128)(2,1)}), bf16[1,8,8]{2,0,1:T(2,128)(2,1)S(1)}, u32[]{:S(2)}, u32[]{:S(2)}) async-start(bf16[1,8,8]{2,0,1:T(2,128)(2,1)} %convert_element_type.117), calls=%async_computation.5 | async-start | bytes 8192 | tf_op jit(solution)/shard_map/all_to_all | solution.py:86
  93.4 5.2 %fusion.2 = bf16[1,512,7168]{2,1,0:T(8,128)(2,1)} fusion(bf16[64,512]{1,0:T(8,128)(2,1)S(1)} %get-tuple-element.27, bf16[8,8,7168]{2,1,0:T(8,128)(2,1)S(1)} %all_gather.6, f32[64]{0:T(128)S(1)} %reshape.179), kind=kOutput, calls=%fused_computation.9 | convolution fusion | flops 474808320 | bytes 8323328 | tf_op jit(solution)/shard_map/dot_general | solution.py:55
  98.5 5.2 %fusion.1 = bf16[1,7168,512]{2,1,0:T(8,128)(2,1)} fusion(bf16[64,512]{1,0:T(8,128)(2,1)S(1)} %get-tuple-element.31, bf16[8,8,7168]{2,1,0:T(8,128)(2,1)S(1)} %all_gather.7), kind=kOutput, calls=%fused_computation.8 | convolution fusion | flops 473432064 | bytes 8323072 | tf_op jit(solution)/shard_map/dot_general | solution.py:63
  103.7 6.0 %all-to-all-start.3 = ((bf16[1792,8,8]{0,2,1:T(8,128)(2,1)}), bf16[1792,8,8]{0,2,1:T(8,128)(2,1)S(1)}, u32[]{:S(2)}, u32[]{:S(2)}) async-start(bf16[1792,8,8]{0,2,1:T(8,128)(2,1)} %bitcast.79), calls=%async_computation.4 | async-start | bytes 458752 | tf_op jit(solution)/shard_map/all_to_all | solution.py:83
  109.7 5.1 %fusion = bf16[1,7168,512]{2,1,0:T(8,128)(2,1)} fusion(bf16[64,512]{1,0:T(8,128)(2,1)S(1)} %get-tuple-element.30, bf16[8,8,7168]{2,1,0:T(8,128)(2,1)S(1)} %all_gather.7), kind=kOutput, calls=%fused_computation.7 | convolution fusion | flops 473432064 | bytes 8323072 | tf_op jit(solution)/shard_map/dot_general | solution.py:60
  114.9 1.9 %gather_fusion.2 = f32[256]{0:T(256)S(1)} fusion(f32[64]{0:T(128)S(1)} %reshape.181, s32[1024]{0:T(1024)S(1)} %pad_clamp_fusion), kind=kCustom, calls=%fused_computation.2 | custom fusion | bytes 3072 | tf_op jit(solution)/shard_map/gather | solution.py:99
  117.0 0.6 copy.26
  117.7 1.0 gather_fusion.1
  118.7 1.0 gather_fusion
  119.7 0.9 add_convert_fusion
  (43 shorter events, 1.6 us)
Async XLA Ops:
  7.2 9.8 %copy-start = (bf16[128,1792]{1,0:T(8,128)(2,1)S(1)}, bf16[128,1792]{1,0:T(8,128)(2,1)}, u32[]{:S(2)}) copy-start(bf16[128,1792]{1,0:T(8,128)(2,1)} %param.7) | copy-start | bytes 1376260
  9.7 13.7 %all-to-all-start = ((bf16[8,1,8]{2,1,0:T(2,128)(2,1)}), bf16[8,1,8]{2,1,0:T(2,128)(2,1)S(1)}, u32[]{:S(2)}, u32[]{:S(2)}) async-start(bf16[8,1,8]{2,1,0:T(2,128)(2,1)} %copy.23), calls=%async_computation | async-start | bytes 8192 | tf_op jit(solution)/shard_map/all_to_all | solution.py:31
  23.4 11.3 %all-to-all-start.2 = ((bf16[8,8,1792]{2,1,0:T(8,128)(2,1)}), bf16[8,8,1792]{2,1,0:T(8,128)(2,1)S(1)}, u32[]{:S(2)}, u32[]{:S(2)}) async-start(bf16[8,8,1792]{2,1,0:T(8,128)(2,1)} %convolution_convert_fusion.3), calls=%async_computation.2 | async-start | bytes 458752 | tf_op jit(solution)/shard_map/all_to_all | solution.py:29
  34.7 18.9 %all-to-all-start.1 = ((bf16[8,8,1792]{2,1,0:T(8,128)(2,1)}), bf16[8,8,1792]{2,1,0:T(8,128)(2,1)S(1)}, u32[]{:S(2)}, u32[]{:S(2)}) async-start(bf16[8,8,1792]{2,1,0:T(8,128)(2,1)} %convolution_convert_fusion.4), calls=%async_computation.1 | async-start | bytes 458752 | tf_op jit(solution)/shard_map/all_to_all | solution.py:30
  38.1 65.6 %reduce-scatter.2.cloned.1.call-start = ((), (), s32[]{:S(2)}) async-start(), calls=%async_computation.6 | async-start | bytes 1146880 | tf_op jit(solution)/shard_map/reduce_scatter | solution.py:69
  38.2 14.1 %slice-start = ((s8[7340032]{0:T(1024)(128)(4,1)}), s8[4194304]{0:T(1024)(128)(4,1)S(1)}, s32[]{:S(2)}) async-start(s8[7340032]{0:T(1024)(128)(4,1)} %bitcast.75), calls=%async_computation.7 | async-start | bytes 8388608
  47.6 4.6 %slice-start.1 = ((s8[7340032]{0:T(1024)(128)(4,1)}), s8[3145728]{0:T(1024)(128)(4,1)S(1)}, s32[]{:S(2)}) async-start(s8[7340032]{0:T(1024)(128)(4,1)} %bitcast.75), calls=%async_computation.8 | async-start | bytes 6291456
  63.1 11.3 %slice-start.2 = ((s8[7340032]{0:T(1024)(128)(4,1)}), s8[4194304]{0:T(1024)(128)(4,1)S(1)}, s32[]{:S(2)}) async-start(s8[7340032]{0:T(1024)(128)(4,1)} %bitcast.77), calls=%async_computation.9 | async-start | bytes 8388608
  68.8 5.6 %slice-start.3 = ((s8[7340032]{0:T(1024)(128)(4,1)}), s8[3145728]{0:T(1024)(128)(4,1)S(1)}, s32[]{:S(2)}) async-start(s8[7340032]{0:T(1024)(128)(4,1)} %bitcast.77), calls=%async_computation.10 | async-start | bytes 6291456
  74.4 3.3 %copy-start.1 = (s32[128,2]{0,1:T(2,128)S(1)}, s32[128,2]{0,1:T(2,128)}, u32[]{:S(2)}) copy-start(s32[128,2]{0,1:T(2,128)} %param.10) | copy-start | bytes 3076
  87.5 16.2 %all-to-all-start.4 = ((bf16[1,8,8]{2,0,1:T(2,128)(2,1)}), bf16[1,8,8]{2,0,1:T(2,128)(2,1)S(1)}, u32[]{:S(2)}, u32[]{:S(2)}) async-start(bf16[1,8,8]{2,0,1:T(2,128)(2,1)} %convert_element_type.117), calls=%async_computation.5 | async-start | bytes 8192 | tf_op jit(solution)/shard_map/all_to_all | solution.py:86
  103.7 14.0 %all-to-all-start.3 = ((bf16[1792,8,8]{0,2,1:T(8,128)(2,1)}), bf16[1792,8,8]{0,2,1:T(8,128)(2,1)S(1)}, u32[]{:S(2)}, u32[]{:S(2)}) async-start(bf16[1792,8,8]{0,2,1:T(8,128)(2,1)} %bitcast.79), calls=%async_computation.4 | async-start | bytes 458752 | tf_op jit(solution)/shard_map/all_to_all | solution.py:83
Sparse Core Ops, SparseCore 0:
  77.8 24.4 reduce-scatter.1
where the time goes:
time: 128 us
  matrix products  38.8 us (30%)
  starting transfers between devices  26 us (20%)
  blocking collectives  25 us (20%)
  between operations  14.3 us (11%)
  waiting for transfers between devices  11.5 us (9%)
  local copies, waits for them, and re-layouts  9.56 us (7%)
  other arithmetic  2.36 us (2%)
    all_gather x1, blocking collectives, per_device(): lax.all_gather(slot_x, 'expert', axis=2, tiled=True)  9.44 us
    all_gather x1, blocking collectives, per_device(): lax.all_gather(slot_d, 'expert', axis=2, tiled=True)  9.43 us
    all_to_all x1, starting transfers between devices, per_device(): lax.all_to_all(slot_gates, 'dp', split_axis=0, concat_axis=0, tiled=True)  7.28 us
    psum x1, blocking collectives, per_device(): gate_back = lax.psum(gate_part, 'expert').reshape(1, experts, CAP)  6.16 us
    all_to_all x1, starting transfers between devices, per_device(): lax.all_to_all(feat_sums.astype(jnp.bfloat16), 'dp', split_axis=1, concat...  5.99 us
    all_to_all x1, waiting for transfers between devices, per_device(): lax.all_to_all(slot_x, 'dp', split_axis=0, concat_axis=0, tiled=True)  5.92 us
    all_to_all x1, starting transfers between devices, per_device(): lax.all_to_all(gate_back.astype(jnp.bfloat16), 'dp', split_axis=1, concat...  5.87 us
    dot_general x1, matrix products, per_device(): lax.dot_general(d_all, down_m, (((1,), (1,)), ((), ())), preferred_elemen...  5.7 us
  transfers between devices with their start and end apart: 6, of which 3 were waited for; matrix products, arithmetic and copies ran while one was open for 24% of the time, Pallas kernels for 0%

commit v1 on v0

v1 whole, which is shorter than its diff:
```python
import functools

import jax
import jax.numpy as jnp
from jax import lax
from jax.experimental import pallas as pl
from jax.experimental.pallas import tpu as pltpu
from jax.sharding import PartitionSpec as P

CAP = 8
LANES = 128
F32 = jnp.float32
BF16 = jnp.bfloat16
VMEM = pl.BlockSpec(memory_space=pltpu.VMEM)
SMEM = pl.BlockSpec(memory_space=pltpu.SMEM)


def keep(array):
    return pltpu.with_memory_space_constraint(array, pltpu.VMEM)


def swap(value, axis, mask):
    size = lax.axis_size(axis)
    return lax.ppermute(value, axis, [(i, i ^ mask) for i in range(size)])


def reorder(shards, me):
    size = len(shards)
    mask = 1
    while mask < size:
        flip = (me & mask) != 0
        shards = [jnp.where(flip, shards[i ^ mask], shards[i]) for i in range(size)]
        mask *= 2
    return shards


def gather_far(own, axis):
    size = lax.axis_size(axis)
    held = {0: own}
    mask = size // 2
    while mask > 1:
        for rel in list(held):
            held[rel ^ mask] = swap(held[rel], axis, mask)
        mask //= 2
    return held


def gather_near(held, axis):
    size = lax.axis_size(axis)
    if size > 1:
        held = {**held, **{rel ^ 1: swap(held[rel], axis, 1) for rel in held}}
    return [held[i] for i in range(size)]


def gather_shards(own, axis):
    return gather_near(gather_far(own, axis), axis)


def add(held, arrived):
    return (held.astype(F32) + arrived.astype(F32)).astype(BF16)


def sum_far(held, axis):
    size = lax.axis_size(axis)
    total = None
    mask = 2
    while mask < size:
        arrived = {rel ^ mask: swap(held.pop(rel), axis, mask) for rel in list(held) if rel & mask}
        for rel, value in arrived.items():
            if rel:
                held[rel] = add(held[rel], value)
            else:
                total = value if total is None else add(total, value)
        mask *= 2
    return total


def sum_all(value, axis):
    size = lax.axis_size(axis)
    arrived = jnp.zeros_like(value)
    mask = 1
    while mask < size:
        if mask > 1:
            value = add(value, arrived)
        arrived = swap(value, axis, mask)
        mask *= 2
    return value, arrived


def one_hot(ids, gates, expert, experts):
    rows, tokens = expert.shape
    row = lax.broadcasted_iota(jnp.int32, (rows, tokens), 0)
    low = expert < experts // 2
    member = jnp.where(low, ids[0:1, :], ids[1:2, :]) == expert
    gate = jnp.where(low, gates[0:1, :], gates[1:2, :])
    earlier = lax.broadcasted_iota(jnp.int32, (tokens, tokens), 0) < lax.broadcasted_iota(
        jnp.int32, (tokens, tokens), 1
    )
    before = jnp.dot(
        member.astype(F32).astype(BF16), earlier.astype(F32).astype(BF16), preferred_element_type=F32
    )
    pick = jnp.logical_and(member, before == (row & (CAP - 1)).astype(F32))
    return jnp.where(pick, 1.0, 0.0), jnp.where(pick, gate, 0.0)


def row_blocks(experts, tokens):
    return lax.broadcasted_iota(jnp.int32, (experts * CAP, tokens), 0) // CAP


def pack_kernel(experts, ids_ref, gates_ref, x_ref, d_ref, slot_out, pick_out, gates_out):
    ids = ids_ref[...]
    gates = gates_ref[...].astype(F32)
    pick, pick_gate = one_hot(ids, gates, row_blocks(experts, ids.shape[1]), experts)
    pick_out[...] = pick.astype(BF16)
    gates_out[...] = gates
    slot_x = jnp.dot(pick.astype(BF16), x_ref[...], preferred_element_type=F32)
    slot_d = jnp.dot(pick_gate.astype(BF16), d_ref[...], preferred_element_type=F32)
    for i in range(experts):
        slot_out[i] = jnp.concatenate(
            [slot_x[i * CAP:(i + 1) * CAP], slot_d[i * CAP:(i + 1) * CAP]], axis=0
        ).astype(BF16)


def pack(ids, gates, tokens, cotangent, experts):
    count, feat = tokens.shape
    return pl.pallas_call(
        functools.partial(pack_kernel, experts),
        out_shape=[
            jax.ShapeDtypeStruct((experts, 2 * CAP, feat), BF16),
            jax.ShapeDtypeStruct((experts * CAP, count), BF16),
            jax.ShapeDtypeStruct((2, count), F32),
        ],
        in_specs=[VMEM] * 4,
        out_specs=[VMEM] * 3,
        cost_estimate=pl.CostEstimate(flops=10**8, bytes_accessed=2 * 10**6, transcendentals=0),
        name="pack",
    )(*[pltpu.with_memory_space_constraint(a, pltpu.HBM) for a in (ids, gates, tokens, cotangent)])


def load_kernel(count, *refs):
    sems = refs[-1]
    copies = [
        pltpu.make_async_copy(refs[i], refs[count + 1 + i], sems.at[i]) for i in range(count)
    ]
    for copy in copies:
        copy.start()
    for copy in copies:
        copy.wait()


def load(after, *arrays):
    count = len(arrays)
    total = sum(a.size * a.dtype.itemsize for a in arrays)
    return pl.pallas_call(
        functools.partial(load_kernel, count),
        out_shape=[pltpu.VMEM(a.shape, a.dtype) for a in arrays],
        in_specs=[pl.BlockSpec(memory_space=pltpu.HBM)] * count + [pl.BlockSpec(memory_space=pl.ANY)],
        out_specs=[VMEM] * count,
        scratch_shapes=[pltpu.SemaphoreType.DMA((count,))],
        cost_estimate=pl.CostEstimate(flops=0, bytes_accessed=total, transcendentals=0),
        compiler_params=pltpu.CompilerParams(vmem_limit_bytes=2**22),
        name="load",
    )(*[pltpu.with_memory_space_constraint(a, pltpu.HBM) for a in arrays], after)


def shard_at(me_ref, rel, feat):
    return pl.ds(pl.multiple_of((me_ref[0] ^ rel) * feat, feat), feat)


def products(rels, me_ref, x_refs, d_refs, gate_ref, up_ref, down_ref):
    feat = x_refs[0].shape[1]
    totals = None
    for rel, x_ref, d_ref in zip(rels, x_refs, d_refs):
        at = shard_at(me_ref, rel, feat)
        parts = (
            jnp.dot(x_ref[...], gate_ref[at, :], preferred_element_type=F32),
            jnp.dot(x_ref[...], up_ref[at, :], preferred_element_type=F32),
            lax.dot_general(
                d_ref[...], down_ref[:, at], (((1,), (1,)), ((), ())), preferred_element_type=F32
            ),
        )
        totals = parts if totals is None else tuple(a + b for a, b in zip(totals, parts))
    return totals


def early_kernel(rels, me_ref, *refs):
    count = len(rels)
    x_refs, d_refs, (gate_ref, up_ref, down_ref) = refs[:count], refs[count:2 * count], refs[2 * count:-3]
    totals = products(rels, me_ref, x_refs, d_refs, gate_ref, up_ref, down_ref)
    for out, value in zip(refs[-3:], totals):
        out[...] = value


def early(rels, me, x, d, weights):
    rows, units = x[0].shape[0], weights[0].shape[1]
    work = 6 * rows * units * x[0].shape[1] * len(rels)
    return pl.pallas_call(
        functools.partial(early_kernel, rels),
        out_shape=[jax.ShapeDtypeStruct((rows, units), F32)] * 3,
        in_specs=[SMEM] + [VMEM] * (2 * len(rels) + 3),
        out_specs=[VMEM] * 3,
        cost_estimate=pl.CostEstimate(flops=work, bytes_accessed=work // rows, transcendentals=0),
        compiler_params=pltpu.CompilerParams(vmem_limit_bytes=2**24),
        name="early",
    )(me, *[keep(a) for a in (*x, *d, *weights)])


def partial_x_kernel(rels, me_ref, after_ref, gate_ref, up_ref, down_ref, *refs):
    x_refs, outs = refs[:-2], refs[-2:]
    feat = x_refs[0].shape[1]
    for weight_ref, out in zip((gate_ref, up_ref), outs):
        total = None
        for rel, x_ref in zip(rels, x_refs):
            part = jnp.dot(
                x_ref[...], weight_ref[shard_at(me_ref, rel, feat), :], preferred_element_type=F32
            )
            total = part if total is None else total + part
        out[...] = total


def partial_d_kernel(rels, me_ref, after_ref, gate_ref, up_ref, down_ref, *refs):
    d_refs, out = refs[:-1], refs[-1]
    feat = d_refs[0].shape[1]
    total = None
    for rel, d_ref in zip(rels, d_refs):
        part = lax.dot_general(
            d_ref[...],
            down_ref[:, shard_at(me_ref, rel, feat)],
            (((1,), (1,)), ((), ())),
            preferred_element_type=F32,
        )
        total = part if total is None else total + part
    out[...] = total


def partial(kernel, count, rels, me, after, arrays, weights):
    rows, units = arrays[0].shape[0], weights[0].shape[1]
    work = 2 * count * rows * units * arrays[0].shape[1] * len(rels)
    return pl.pallas_call(
        functools.partial(kernel, rels),
        out_shape=[jax.ShapeDtypeStruct((rows, units), F32)] * count,
        in_specs=[SMEM, pl.BlockSpec(memory_space=pl.ANY)] + [VMEM] * (3 + len(rels)),
        out_specs=[VMEM] * count,
        cost_estimate=pl.CostEstimate(flops=work, bytes_accessed=work // rows, transcendentals=0),
        compiler_params=pltpu.CompilerParams(vmem_limit_bytes=2**24),
        name="partial",
    )(me, keep(after), *[keep(a) for a in (*weights, *arrays)])


def flip(index, rel):
    mask = 1
    while mask <= rel:
        if rel & mask:
            index = index + mask * (1 - 2 * ((index // mask) % 2))
        mask *= 2
    return index


def load_early_kernel(near, far, x0, d0, x1, d1, gate_in, up_in, down_in, gate, up, down, *refs):
    sums, sems = refs[:3], refs[3]
    feat = x0.shape[1]
    me = lax.axis_index("expert")

    def copies(rel):
        at = pl.ds(pl.multiple_of(flip(me, rel) * feat, feat), feat)
        return [
            pltpu.make_async_copy(src.at[place], dst.at[place], sems.at[i, rel])
            for i, (src, dst, place) in enumerate(
                ((gate_in, gate, at), (up_in, up, at), (down_in, down, (slice(None), at)))
            )
        ]

    first = [copies(rel) for rel in near]
    rest = [copies(rel) for rel in far]
    for i in range(3):
        for group in first:
            group[i].start()
    for i in range(3):
        for group in first:
            group[i].wait()
        if i == 0:
            for group in rest:
                for copy in group:
                    copy.start()
        total = None
        for rel, x_ref, d_ref in zip(near, (x0, x1), (d0, d1)):
            at = pl.ds(pl.multiple_of(flip(me, rel) * feat, feat), feat)
            if i < 2:
                part = jnp.dot(x_ref[...], (gate, up)[i][at, :], preferred_element_type=F32)
            else:
                part = lax.dot_general(
                    d_ref[...], down[:, at], (((1,), (1,)), ((), ())), preferred_element_type=F32
                )
            total = part if total is None else total + part
        sums[i][...] = total
    for group in rest:
        for copy in group:
            copy.wait()


def load_early(x, d, weights, after):
    shards = lax.axis_size("expert")
    rows = x[0].shape[0]
    units = weights[0].shape[1]
    near, far = list(range(2)), list(range(2, shards))
    kernel = functools.partial(load_early_kernel, near, far)
    out = pl.pallas_call(
        lambda after_ref, *refs: kernel(*refs),
        out_shape=[pltpu.VMEM(a.shape, a.dtype) for a in weights]
        + [jax.ShapeDtypeStruct((rows, units), F32)] * 3,
        in_specs=[pl.BlockSpec(memory_space=pl.ANY)]
        + [VMEM] * 4
        + [pl.BlockSpec(memory_space=pltpu.HBM)] * 3,
        out_specs=[VMEM] * 6,
        scratch_shapes=[pltpu.SemaphoreType.DMA((3, shards))],
        cost_estimate=pl.CostEstimate(
            flops=6 * rows * units * x[0].shape[1],
            bytes_accessed=sum(a.size * 2 for a in weights),
            transcendentals=0,
        ),
        compiler_params=pltpu.CompilerParams(vmem_limit_bytes=2**23),
        name="load_early",
    )(
        after,
        *[keep(a) for a in (x[0], d[0], x[1], d[1])],
        *[pltpu.with_memory_space_constraint(a, pltpu.HBM) for a in weights],
    )
    return out[:3], out[3:]


def late_kernel(rels, me_ref, *refs):
    count = len(rels)
    x_refs, d_refs, refs = refs[:count], refs[count:2 * count], refs[2 * count:]
    gate_ref, up_ref, down_ref, sum_refs = refs[0], refs[1], refs[2], refs[3:-4]
    hidden_out, d_gate_out, d_up_out, cols_out = refs[-4:]
    totals = [ref[...] for ref in sum_refs[:3]]
    for i, ref in enumerate(sum_refs[3:]):
        totals[i % 3] += ref[...]
    if rels:
        parts = products(rels, me_ref, x_refs, d_refs, gate_ref, up_ref, down_ref)
        totals = [a + b for a, b in zip(totals, parts)]
    pre_gate, pre_up, dhid = totals
    sig = 1.0 / (1.0 + jnp.exp(-pre_gate))
    act = pre_gate * sig
    hidden = (act * pre_up).astype(BF16)
    hidden_out[...] = hidden
    d_gate_out[...] = (dhid * pre_up * sig * (1.0 + pre_gate * (1.0 - sig))).astype(BF16)
    d_up_out[...] = (dhid * act).astype(BF16)
    total = jnp.sum(dhid * hidden.astype(F32), axis=1, keepdims=True)
    cols_out[...] = jnp.broadcast_to(total, cols_out.shape).astype(BF16)


def late(rels, me, x, d, weights, sums):
    rows, units = sums[0].shape
    work = 6 * rows * units * max(1, sum(a.shape[1] for a in x))
    return pl.pallas_call(
        functools.partial(late_kernel, rels),
        out_shape=[jax.ShapeDtypeStruct((rows, units), BF16)] * 3
        + [jax.ShapeDtypeStruct((rows, LANES), BF16)],
        in_specs=[SMEM] + [VMEM] * (2 * len(rels) + 3 + len(sums)),
        out_specs=[VMEM] * 4,
        cost_estimate=pl.CostEstimate(
            flops=work, bytes_accessed=work // rows, transcendentals=rows * units
        ),
        compiler_params=pltpu.CompilerParams(vmem_limit_bytes=2**24),
        name="late",
    )(me, *[keep(a) for a in (*x, *d, *weights, *sums)])


def term_kernel(rels, me_ref, after_ref, last_ref, d_gate_ref, d_up_ref, gate_ref, up_ref, *outs):
    feat = outs[0].shape[1]
    dims = (((1,), (1,)), ((), ()))
    for rel, out in zip(rels, outs):
        at = shard_at(me_ref, rel, feat)
        term = lax.dot_general(d_gate_ref[...], gate_ref[at, :], dims, preferred_element_type=F32)
        term += lax.dot_general(d_up_ref[...], up_ref[at, :], dims, preferred_element_type=F32)
        out[...] = term.astype(BF16)


def terms(rels, me, after, d_gate, d_up, gate_m, up_m, feat):
    rows, units = d_gate.shape
    return pl.pallas_call(
        functools.partial(term_kernel, rels),
        out_shape=[jax.ShapeDtypeStruct((rows, feat), BF16)] * len(rels),
        in_specs=[SMEM] + [pl.BlockSpec(memory_space=pl.ANY)] * 2 + [VMEM] * 4,
        out_specs=[VMEM] * len(rels),
        cost_estimate=pl.CostEstimate(flops=10**6, bytes_accessed=10**6, transcendentals=0),
        compiler_params=pltpu.CompilerParams(vmem_limit_bytes=2**24),
        name="terms",
    )(me, *after, *[keep(a) for a in (d_gate, d_up, gate_m, up_m)])


SLOTS = 4


def stream(steps, fill, copies):
    for step in range(steps + SLOTS):
        if step >= SLOTS:
            for copy in copies(step - SLOTS, step % SLOTS):
                copy.wait()
        if step < steps:
            fill(step, step % SLOTS)
            for copy in copies(step, step % SLOTS):
                copy.start()


def places(feat, shards, block):
    me = lax.axis_index("expert") if shards > 1 else 0

    def place(step):
        rel, part = divmod(step, feat // block)
        start = flip(me, rel) * feat + part * block
        return pl.ds(pl.multiple_of(start, block) if shards > 1 else start, block)

    def source(step):
        rel, part = divmod(step, feat // block)
        return rel, slice(part * block, (part + 1) * block)

    return shards * feat // block, source, place


def outer_rows_kernel(block, shards, after_ref, *refs):
    stage, sems = refs[-2:]
    lefts, refs = refs[:shards], refs[shards:-2]
    half = len(refs) // 2
    rights, outs = refs[:half], refs[half:]
    steps, source, place = places(lefts[0].shape[1], shards, block)

    def fill(step, slot):
        rel, at = source(step)
        left = lefts[rel][:, at].astype(F32).T.astype(BF16)
        for i, right in enumerate(rights):
            stage[slot, i] = jnp.dot(left, right[...], preferred_element_type=F32).astype(BF16)

    def copies(step, slot):
        return [
            pltpu.make_async_copy(stage.at[slot, i], out.at[place(step)], sems.at[slot, i])
            for i, out in enumerate(outs)
        ]

    stream(steps, fill, copies)


def outer_rows(lefts, rights, after, block):
    rows, feat = lefts[0].shape
    tall = feat * len(lefts)
    narrow = rights[0].shape[1]
    count = len(rights)
    return pl.pallas_call(
        functools.partial(outer_rows_kernel, block, len(lefts)),
        out_shape=[jax.ShapeDtypeStruct((tall, narrow), BF16)] * count,
        in_specs=[pl.BlockSpec(memory_space=pl.ANY)] + [VMEM] * (len(lefts) + count),
        out_specs=[pl.BlockSpec(memory_space=pltpu.HBM)] * count,
        scratch_shapes=[
            pltpu.VMEM((SLOTS, count, block, narrow), BF16),
            pltpu.SemaphoreType.DMA((SLOTS, count)),
        ],
        cost_estimate=pl.CostEstimate(
            flops=2 * rows * tall * narrow * count,
            bytes_accessed=2 * tall * narrow * count,
            transcendentals=0,
        ),
        compiler_params=pltpu.CompilerParams(vmem_limit_bytes=2**24),
        name="outer_rows",
    )(pltpu.with_memory_space_constraint(after, pltpu.HBM), *[keep(a) for a in (*lefts, *rights)])


def outer_columns_kernel(block, shards, after_ref, left_ref, *refs):
    rights, (out_ref, turned, stage, sems) = refs[:shards], refs[shards:]
    turned[...] = left_ref[...].astype(F32).T.astype(BF16)
    steps, source, place = places(rights[0].shape[1], shards, block)

    def fill(step, slot):
        rel, at = source(step)
        stage[slot] = jnp.dot(turned[...], rights[rel][:, at], preferred_element_type=F32).astype(BF16)

    def copies(step, slot):
        return [pltpu.make_async_copy(stage.at[slot], out_ref.at[:, place(step)], sems.at[slot])]

    stream(steps, fill, copies)


def outer_columns(left, rights, after, block):
    rows, feat = rights[0].shape
    wide = feat * len(rights)
    tall = left.shape[1]
    return pl.pallas_call(
        functools.partial(outer_columns_kernel, block, len(rights)),
        out_shape=jax.ShapeDtypeStruct((tall, wide), BF16),
        in_specs=[pl.BlockSpec(memory_space=pl.ANY)] + [VMEM] * (1 + len(rights)),
        out_specs=pl.BlockSpec(memory_space=pltpu.HBM),
        scratch_shapes=[
            pltpu.VMEM((tall, rows), BF16),
            pltpu.VMEM((SLOTS, tall, block), BF16),
            pltpu.SemaphoreType.DMA((SLOTS,)),
        ],
        cost_estimate=pl.CostEstimate(flops=10**6, bytes_accessed=10**6, transcendentals=0),
        compiler_params=pltpu.CompilerParams(vmem_limit_bytes=2**24),
        name="outer_columns",
    )(keep(after), keep(left), *[keep(a) for a in rights])


def settle_kernel(held_ref, arrived_ref, cols_ref, more_ref, after_ref, out_ref):
    feat = held_ref.shape[1]
    total = held_ref[...].astype(F32) + arrived_ref[...].astype(F32)
    cols = cols_ref[...].astype(F32) + more_ref[...].astype(F32)
    for i in range(out_ref.shape[0]):
        out_ref[i, :, :feat] = total[i * CAP:(i + 1) * CAP].astype(BF16)
        out_ref[i, :, feat:] = cols[i * CAP:(i + 1) * CAP].astype(BF16)


def settle(own, cols, after):
    rows, feat = own[0].shape
    return pl.pallas_call(
        settle_kernel,
        out_shape=jax.ShapeDtypeStruct((rows // CAP, CAP, feat + LANES), BF16),
        in_specs=[VMEM] * 4 + [pl.BlockSpec(memory_space=pl.ANY)],
        out_specs=VMEM,
        cost_estimate=pl.CostEstimate(flops=0, bytes_accessed=10**6, transcendentals=0),
        name="settle",
    )(*[keep(a) for a in (*own, *cols)], pltpu.with_memory_space_constraint(after, pltpu.HBM))


def combine_kernel(pick_ref, gates_ref, rows_ref, grad_ref, gate_ref):
    feat = grad_ref.shape[1]
    half = pick_ref.shape[0] // 2
    pick = pick_ref[...]
    rows = rows_ref[...]
    grad_ref[...] = lax.dot_general(
        pick, rows[:, :feat], (((0,), (0,)), ((), ())), preferred_element_type=F32
    ).astype(BF16)
    terms = pick.astype(F32) * rows[:, feat:].astype(F32)
    gate_ref[0:1, :] = jnp.sum(terms[:half], axis=0, keepdims=True) / gates_ref[0:1, :]
    gate_ref[1:2, :] = jnp.sum(terms[half:], axis=0, keepdims=True) / gates_ref[1:2, :]


def combine(pick, gates, rows, feat):
    count = pick.shape[1]
    return pl.pallas_call(
        combine_kernel,
        out_shape=[
            jax.ShapeDtypeStruct((count, feat), BF16),
            jax.ShapeDtypeStruct((2, count), F32),
        ],
        in_specs=[VMEM] * 3,
        out_specs=[VMEM] * 2,
        cost_estimate=pl.CostEstimate(flops=10**8, bytes_accessed=10**6, transcendentals=0),
        name="combine",
    )(pick, gates, pltpu.with_memory_space_constraint(rows, pltpu.VMEM))


def per_device(tokens, cotangent, gates, expert_ids, w_gate, w_up, w_down):
    experts = lax.axis_size("dp")
    shards = lax.axis_size("expert")
    me = lax.axis_index("expert")
    rows = experts * CAP
    feat = tokens.shape[1]
    ids_t = expert_ids.T
    gates_t = gates.T
    me_ref = me.reshape(1)
    slots, pick, gates_f = pack(ids_t, gates_t, tokens, cotangent, experts)
    slots = lax.all_to_all(slots, "dp", split_axis=0, concat_axis=0, tiled=True)
    x = gather_far(slots[:, :CAP].reshape(rows, feat), "expert")
    d = gather_far(slots[:, CAP:].reshape(rows, feat), "expert")
    weights = [w_gate[0], w_up[0], w_down[0]]
    if feat % LANES or shards < 4:
        x, d = gather_near(x, "expert"), gather_near(d, "expert")
        x = [jnp.concatenate(reorder(x, me), axis=1)]
        d = [jnp.concatenate(reorder(d, me), axis=1)]
        weights = load(slots, *weights)
        sums = early([0], me_ref * 0, x, d, weights)
        odd = []
    else:
        x[1], d[1] = swap(x[0], "expert", 1), swap(d[0], "expert", 1)
        weights, sums = load_early(x, d, weights, slots)
        even = list(range(2, shards, 2))
        odd = list(range(3, shards, 2))
        rest, sums = lax.optimization_barrier(([x[i] for i in even], sums))
        for i, x_i in zip(even, rest):
            x[i], x[i + 1] = x_i, swap(x_i, "expert", 1)
        more = partial(partial_x_kernel, 2, even, me_ref, sums[0], rest, weights)
        rest, more = lax.optimization_barrier(([d[i] for i in even], more))
        for i, d_i in zip(even, rest):
            d[i], d[i + 1] = d_i, swap(d_i, "expert", 1)
        more = [*more, *partial(partial_d_kernel, 1, even, me_ref, more[0], rest, weights)]
        x, d = [x[i] for i in range(shards)], [d[i] for i in range(shards)]
        sums = [*sums, *more]
    hidden, d_gate, d_up, cols = late(odd, me_ref, [x[i] for i in odd], [d[i] for i in odd], weights, sums)

    def term(rels, after):
        got = terms(rels, me_ref, after, d_gate, d_up, *weights[:2], feat) if rels else []
        return dict(zip(rels, got))

    start = (keep(cols), keep(cols))
    sent = term(list(range(3, shards, 2)), start)
    arrived = {rel ^ 1: swap(part, "expert", 1) for rel, part in sent.items()}
    kept = term(list(range(2, shards, 2)), start)
    held = {rel: add(part, arrived[rel]) for rel, part in kept.items()}
    last = held[max(held)] if held else cols
    wide = feat * shards
    grad_down = outer_columns(hidden, d, last, wide // 8)
    other = sum_far(held, "expert")
    if other is None:
        other = jnp.zeros((rows, feat), BF16)
    start = (keep(other), pltpu.with_memory_space_constraint(grad_down, pltpu.HBM))
    sent = term([1] if shards > 1 else [], start)
    own = term([0], start)[0]
    for part in sent.values():
        own = add(own, swap(part, "expert", 1))
    total = settle((own, other), sum_all(cols, "expert"), grad_down)
    got = lax.all_to_all(total, "dp", split_axis=0, concat_axis=0, tiled=True)
    got = got.reshape(rows, feat + LANES)
    grad_gate, grad_up = outer_rows(x, (d_gate, d_up), total, wide // 16)
    grad_tokens, gate_grads = combine(pick, gates_f, got, feat)
    return (grad_tokens, gate_grads.T, grad_gate[None], grad_up[None], grad_down[None])


def solution(mesh):
    in_specs = (
        P("dp", "expert"),
        P("dp", "expert"),
        P("dp", None),
        P("dp", None),
        P("dp", None, "expert"),
        P("dp", None, "expert"),
        P("dp", "expert", None),
    )
    out_specs = (
        P("dp", "expert"),
        P("dp", None),
        P("dp", None, "expert"),
        P("dp", None, "expert"),
        P("dp", "expert", None),
    )
    return jax.shard_map(
        per_device, mesh=mesh, in_specs=in_specs, out_specs=out_specs, check_vma=False
    )
```

time: 128 us -> 70.1 us (0.55)
  matrix products: 38.8 us -> 0 us
  Pallas kernels: 0 us -> 32.5 us
  starting transfers between devices: 26 us -> 9.64 us
  between operations: 14.3 us -> 0.76 us
  local copies, waits for them, and re-layouts: 9.56 us -> 0.03 us
  waiting for transfers between devices: 11.5 us -> 6.13 us
  blocking collectives: 25 us -> 20.5 us
  other arithmetic: 2.36 us -> 0.12 us
    dot_general x10 -> x0, matrix products: 38.8 us -> none  [the longest x1 5.7 us: per_device(): lax.dot_general(d_all, down_m, (((1,), (1,)), ((), ())), preferred_elemen...]
    pallas_call x0 -> x13, Pallas kernels: none -> 32.5 us  [the longest x1 8.15 us: outer_rows(): pl.pallas_call(functools.partial(outer_rows_kernel, block, len(lefts)), o...]
    all_to_all x5 -> x1, starting transfers between devices: 26 us -> 3.59 us  [per_device(): got = lax.all_to_all(total, 'dp', split_axis=0, concat_axis=0, tiled=True)]
    all_to_all x0 -> x1, blocking collectives: none -> 20.5 us  [per_device(): slots = lax.all_to_all(slots, 'dp', split_axis=0, concat_axis=0, tiled=True)]
    all_gather x2 -> x0, blocking collectives: 18.9 us -> none  [the longest x1 9.44 us: per_device(): lax.all_gather(slot_x, 'expert', axis=2, tiled=True)]
    all_to_all x5 -> x1, waiting for transfers between devices: 11.5 us -> 0.06 us  [per_device(): got = lax.all_to_all(total, 'dp', split_axis=0, concat_axis=0, tiled=True)]
    gather x7 -> x0, local copies, waits for them, and re-layouts: 6.19 us -> none  [the longest x3 2.22 us: per_device(): slot_place = jnp.take_along_axis(places, safe_ids, axis=1)]
    psum x1 -> x0, blocking collectives: 6.16 us -> none  [per_device(): gate_back = lax.psum(gate_part, 'expert').reshape(1, experts, CAP)]
  transfers between devices with their start and end apart: 6 -> 12, of which waited for: 3 -> 6; matrix products, arithmetic and copies ran while one was open for 24% -> 0% of each run, Pallas kernels for 0% -> 36%
where the time goes in v1:
time: 70.1 us; the launch traced here: 69.7 us
  Pallas kernels  32.5 us (46%)
  blocking collectives  20.5 us (29%)
  starting transfers between devices  9.64 us (14%)
  waiting for transfers between devices  6.13 us (9%)
  between operations  0.76 us (1%)
    all_to_all x1, blocking collectives, per_device(): slots = lax.all_to_all(slots, 'dp', split_axis=0, concat_axis=0, tiled=True)  20.5 us
    pallas_call x1, Pallas kernels, outer_rows(): pl.pallas_call(functools.partial(outer_rows_kernel, block, len(lefts)), o...  8.15 us
    pallas_call x1, Pallas kernels, load_early(): pl.pallas_call(lambda after_ref, *refs: kernel(*refs), out_shape=[pltpu.V...  7.67 us
    ppermute x11, waiting for transfers between devices, swap(): return lax.ppermute(value, axis, [(i, i ^ mask) for i in range(size)])  6.08 us
    ppermute x11, starting transfers between devices, swap(): return lax.ppermute(value, axis, [(i, i ^ mask) for i in range(size)])  6.05 us
    pallas_call x4, Pallas kernels, terms(): pl.pallas_call(functools.partial(term_kernel, rels), out_shape=[jax.Shape...  4.89 us
    pallas_call x1, Pallas kernels, outer_columns(): pl.pallas_call(functools.partial(outer_columns_kernel, block, len(rights)...  4.02 us
    all_to_all x1, starting transfers between devices, per_device(): got = lax.all_to_all(total, 'dp', split_axis=0, concat_axis=0, tiled=True)  3.59 us
  transfers between devices with their start and end apart: 12, of which 6 were waited for; matrix products, arithmetic and copies ran while one was open for 0% of the time, Pallas kernels for 36%

profile of v1, /device:TPU:0, one launch (start us, length us, event | category | flops | bytes accessed | tf_op | source)
XLA Modules:
  0.0 69.7 jit_solution(11283650419490839351)
XLA Ops:
  0.6 2.4 %pack.1 = (bf16[8,16,1792]{2,1,0:T(8,128)(2,1)}, bf16[64,128]{1,0:T(8,128)(2,1)}, f32[2,128]{1,0:T(2,128)}) custom-call(s32[2,128]{1,0:T(2,128)} %bitcast.20, bf16[2,128]{1,0:T(2,128)(2,1)} %bitcast.21, bf16[128,1792]{1,0:T(8,128)(2,1)} %x_ref.1, bf16[128,1792]{1,0:T(8,128)(2,1)} %d_ref.1), custom_call_target="tpu_custom_call" | custom-call | flops 100000000 | bytes 2000000 | tf_op jit(solution)/shard_map/pack/pallas_call | solution.py:126
  3.0 20.5 %all_to_all.10.after_ref = bf16[8,16,1792]{2,1,0:T(8,128)(2,1)S(1)} all-to-all(bf16[8,16,1792]{2,1,0:T(8,128)(2,1)} %get-tuple-element.33), channel_id=1, replica_groups=mesh['dp'=8,'expert'=4] {'dp'}, dimensions={0} | all-to-all | bytes 917504 | tf_op jit(solution)/shard_map/all_to_all | solution.py:562
  23.5 0.1 collective-permute-start.2
  23.6 0.5 collective-permute-start.1
  24.1 1.5 %collective-permute-start = (bf16[64,1792]{1,0:T(8,128)(2,1)S(1)}, bf16[64,1792]{1,0:T(8,128)(2,1)S(1)}, u32[]{:S(2)}, u32[]{:S(2)}) collective-permute-start(bf16[64,1792]{1,0:T(8,128)(2,1)S(1)} %get-tuple-element.58.refs_0_), channel_id=1, source_target_pairs={{0,2},{1,3},{2,0},{3,1},{4,6},{5,7},{6,4},{7,5},{8,10},{9,11},{10,... | collective-permute-start | bytes 688136 | tf_op jit(solution)/shard_map/ppermute | solution.py:24
  25.6 0.5 collective-permute-start.4
  26.2 7.7 %load_early.1 = (bf16[7168,512]{1,0:T(8,128)(2,1)S(1)}, bf16[7168,512]{1,0:T(8,128)(2,1)S(1)}, bf16[512,7168]{1,0:T(8,128)(2,1)S(1)}, f32[64,512]{1,0:T(8,128)S(...) custom-call(bf16[8,16,1792]{2,1,0:T(8,128)(2,1)S(1)} %all_to_all.10.after_ref, ...), custom_call_target="tpu_custom_call" | custom-call | flops 352321536 | bytes 22020096 | tf_op jit(solution)/shard_map/load_early/pallas_call | solution.py:307
  33.8 0.1 collective-permute-start.3
  33.9 0.7 %partial.2 = (f32[64,512]{1,0:T(8,128)S(1)}, f32[64,512]{1,0:T(8,128)S(1)}) custom-call(s32[1]{0:T(128)} %bitcast.2.me_ref, f32[64,512]{1,0:T(8,128)S(1)} %get-tuple-element.38.after_ref.refs_5_, bf16[7168,512]{1,0:T(8,128)(2,1)S(1)} %get-tuple-element.39.gate_ref.refs_2_, bf16[7168,512]{1,0:T(8,128)(2,1)S(1)} %get-tuple-element.40.up_ref.refs_3_, ...), custom_call_target="tpu_custom_call" | custom-call | flops 234881024 | bytes 3670016 | tf_op jit(solution)/shard_map/partial/pallas_call | solution.py:239
  34.7 1.9 %collective-permute-done.4.refs_0_.refs_2_ = bf16[64,1792]{1,0:T(8,128)(2,1)S(1)} collective-permute-done((bf16[64,1792]{1,0:T(8,128)(2,1)S(1)}, bf16[64,1792]{1,0:T(8,128)(2,1)S(1)}, u32[]{:S(2)}, u32[]{:S(2)}) %collective-permute-start.4) | collective-permute-done | bytes 229408 | tf_op jit(solution)/shard_map/ppermute | solution.py:24
  36.6 0.7 partial.3.refs_10_
  37.3 0.8 %collective-permute-done.5.refs_1_.refs_3_ = bf16[64,1792]{1,0:T(8,128)(2,1)S(1)} collective-permute-done((bf16[64,1792]{1,0:T(8,128)(2,1)S(1)}, bf16[64,1792]{1,0:T(8,128)(2,1)S(1)}, u32[]{:S(2)}, u32[]{:S(2)}) %collective-permute-start.5) | collective-permute-done | bytes 229408 | tf_op jit(solution)/shard_map/ppermute | solution.py:24
  38.1 1.4 %late.1 = (bf16[64,512]{1,0:T(8,128)(2,1)S(1)}, bf16[64,512]{1,0:T(8,128)(2,1)S(1)}, bf16[64,512]{1,0:T(8,128)(2,1)S(1)}, bf16[64,128]{1,0:T(8,128)(2,1)S(1)}) custom-call(s32[1]{0:T(128)} %bitcast.2.me_ref, bf16[64,1792]{1,0:T(8,128)(2,1)S(1)} %collective-permute-done.3.refs_0_.refs_3_, bf16[64,1792]{1,0:T(8,128)(2,1)S(1)} %collective-permute-done.5.refs_1_.refs_3_, ...), custom_call_target="tpu_custom_call" | custom-call | flops 352321536 | bytes 5505024 | tf_op jit(solution)/shard_map/late/pallas_call | solution.py:356
  39.5 1.2 %terms.5 = bf16[64,1792]{1,0:T(8,128)(2,1)S(1)} custom-call(s32[1]{0:T(128)} %bitcast.2.me_ref, bf16[64,128]{1,0:T(8,128)(2,1)S(1)} %get-tuple-element.49.after_ref.last_ref, bf16[64,128]{1,0:T(8,128)(2,1)S(1)} %get-tuple-element.49.after_ref.last_ref, bf16[64,512]{1,0:T(8,128)(2,1)S(1)} %get-tuple-element.50.d_gate_ref.refs_4_, ...), custom_call_target="tpu_custom_call" | custom-call | flops 1000000 | bytes 1000000 | tf_op jit(solution)/shard_map/terms/pallas_call | solution.py:382
  40.8 0.2 collective-permute-start.6
  41.0 1.2 %terms.4 = bf16[64,1792]{1,0:T(8,128)(2,1)S(1)} custom-call(s32[1]{0:T(128)} %bitcast.2.me_ref, bf16[64,128]{1,0:T(8,128)(2,1)S(1)} %get-tuple-element.49.after_ref.last_ref, bf16[64,128]{1,0:T(8,128)(2,1)S(1)} %get-tuple-element.49.after_ref.last_ref, bf16[64,512]{1,0:T(8,128)(2,1)S(1)} %get-tuple-element.50.d_gate_ref.refs_4_, ...), custom_call_target="tpu_custom_call" | custom-call | flops 1000000 | bytes 1000000 | tf_op jit(solution)/shard_map/terms/pallas_call | solution.py:382
  42.2 0.1 collective-permute-done.6
  42.3 0.1 add_convert_fusion.1.after_ref
  42.4 1.6 %collective-permute-start.7 = (bf16[64,1792]{1,0:T(8,128)(2,1)S(1)}, bf16[64,1792]{1,0:T(8,128)(2,1)S(1)}, u32[]{:S(2)}, u32[]{:S(2)}) collective-permute-start(bf16[64,1792]{1,0:T(8,128)(2,1)S(1)} %add_convert_fusion.1.after_ref), channel_id=1, source_target_pairs={{0,2},{1,3},{2,0},{3,1},{4,6},{5,7},{6,4},{7,5},{8,10},{9,11},{10,... | collective-permute-start | bytes 688136 | tf_op jit(solution)/shard_map/ppermute | solution.py:24
  43.9 4.0 %outer_columns.1.last_ref.after_ref = bf16[512,7168]{1,0:T(8,128)(2,1)} custom-call(bf16[64,1792]{1,0:T(8,128)(2,1)S(1)} %add_convert_fusion.1.after_ref, bf16[64,512]{1,0:T(8,128)(2,1)S(1)} %get-tuple-element.52.left_ref, bf16[64,1792]{1,0:T(8,128)(2,1)S(1)} %get-tuple-element.57.refs_1_.refs_0_, ...), custom_call_target="tpu_custom_call" | custom-call | flops 1000000 | bytes 1000000 | tf_op jit(solution)/shard_map/outer_columns/pallas_call | solution.py:487
  48.0 2.2 %collective-permute-done.7.after_ref.arrived_ref = bf16[64,1792]{1,0:T(8,128)(2,1)S(1)} collective-permute-done((bf16[64,1792]{1,0:T(8,128)(2,1)S(1)}, bf16[64,1792]{1,0:T(8,128)(2,1)S(1)}, u32[]{:S(2)}, u32[]{:S(2)}) %collective-permute-start.7) | collective-permute-done | bytes 229408 | tf_op jit(solution)/shard_map/ppermute | solution.py:24
  50.2 1.2 %terms.7 = bf16[64,1792]{1,0:T(8,128)(2,1)S(1)} custom-call(s32[1]{0:T(128)} %bitcast.2.me_ref, bf16[64,1792]{1,0:T(8,128)(2,1)S(1)} %collective-permute-done.7.after_ref.arrived_ref, bf16[512,7168]{1,0:T(8,128)(2,1)} %outer_columns.1.last_ref.after_ref, bf16[64,512]{1,0:T(8,128)(2,1)S(1)} %get-tuple-element.50.d_gate_ref.refs_4_, ...), custom_call_target="tpu_custom_call" | custom-call | flops 1000000 | bytes 1000000 | tf_op jit(solution)/shard_map/terms/pallas_call | solution.py:382
  51.4 0.1 collective-permute-start.8
  51.5 1.6 %collective-permute-start.10 = (bf16[64,128]{1,0:T(8,128)(2,1)S(1)}, bf16[64,128]{1,0:T(8,128)(2,1)S(1)}, u32[]{:S(2)}, u32[]{:S(2)}) collective-permute-start(bf16[64,128]{1,0:T(8,128)(2,1)S(1)} %add_convert_fusion.2.cols_ref), channel_id=1, source_target_pairs={{0,2},{1,3},{2,0},{3,1},{4,6},{5,7},{6,4},{7,5},{8,10},{9,11},{10,... | collective-permute-start | bytes 49160 | tf_op jit(solution)/shard_map/ppermute | solution.py:24
  53.1 1.2 %terms.6 = bf16[64,1792]{1,0:T(8,128)(2,1)S(1)} custom-call(s32[1]{0:T(128)} %bitcast.2.me_ref, bf16[64,1792]{1,0:T(8,128)(2,1)S(1)} %collective-permute-done.7.after_ref.arrived_ref, bf16[512,7168]{1,0:T(8,128)(2,1)} %outer_columns.1.last_ref.after_ref, bf16[64,512]{1,0:T(8,128)(2,1)S(1)} %get-tuple-element.50.d_gate_ref.refs_4_, ...), custom_call_target="tpu_custom_call" | custom-call | flops 1000000 | bytes 1000000 | tf_op jit(solution)/shard_map/terms/pallas_call | solution.py:382
  54.3 0.1 add_convert_fusion.held_ref
  54.4 1.0 %collective-permute-done.10.more_ref = bf16[64,128]{1,0:T(8,128)(2,1)S(1)} collective-permute-done((bf16[64,128]{1,0:T(8,128)(2,1)S(1)}, bf16[64,128]{1,0:T(8,128)(2,1)S(1)}, u32[]{:S(2)}, u32[]{:S(2)}) %collective-permute-start.10) | collective-permute-done | bytes 16416 | tf_op jit(solution)/shard_map/ppermute | solution.py:24
  55.3 0.8 %settle.1.after_ref = bf16[8,8,1920]{2,1,0:T(8,128)(2,1)} custom-call(bf16[64,1792]{1,0:T(8,128)(2,1)S(1)} %add_convert_fusion.held_ref, bf16[64,1792]{1,0:T(8,128)(2,1)S(1)} %collective-permute-done.7.after_ref.arrived_ref, bf16[64,128]{1,0:T(8,128)(2,1)S(1)} %add_convert_fusion.2.cols_ref, bf16[64,128]{1,0:T(8,128)(2,1)S(1)} %collective-permute-done.10.more_ref, ...), custom_call_target="tpu_custom_call" | custom-call | bytes 1000000 | tf_op jit(solution)/shard_map/settle/pallas_call | solution.py:514
  56.1 3.6 %all-to-all-start.1 = ((bf16[8,8,1920]{2,1,0:T(8,128)(2,1)}), bf16[8,8,1920]{2,1,0:T(8,128)(2,1)S(1)}, u32[]{:S(2)}, u32[]{:S(2)}) async-start(bf16[8,8,1920]{2,1,0:T(8,128)(2,1)} %settle.1.after_ref), calls=%async_computation.1 | async-start | bytes 491520 | tf_op jit(solution)/shard_map/all_to_all | solution.py:611
  59.7 8.1 %outer_rows.1 = (bf16[7168,512]{1,0:T(8,128)(2,1)}, bf16[7168,512]{1,0:T(8,128)(2,1)}) custom-call(bf16[8,8,1920]{2,1,0:T(8,128)(2,1)} %settle.1.after_ref, bf16[64,1792]{1,0:T(8,128)(2,1)S(1)} %get-tuple-element.58.refs_0_, bf16[64,1792]{1,0:T(8,128)(2,1)S(1)} %collective-permute-done.1.refs_2_.refs_1_, ...), custom_call_target="tpu_custom_call" | custom-call | flops 939524096 | bytes 14680064 | tf_op jit(solution)/shard_map/outer_rows/pallas_call | solution.py:449
  67.9 0.1 all-to-all-done.1
  67.9 1.8 %combine.1 = (bf16[128,1792]{1,0:T(8,128)(2,1)}, f32[2,128]{1,0:T(2,128)}) custom-call(bf16[64,128]{1,0:T(8,128)(2,1)} %get-tuple-element.31.pick_ref, f32[2,128]{1,0:T(2,128)} %get-tuple-element.32.gates_ref, bf16[64,1920]{1,0:T(8,128)(2,1)S(1)} %bitcast.15), custom_call_target="tpu_custom_call" | custom-call | flops 100000000 | bytes 1000000 | tf_op jit(solution)/shard_map/combine/pallas_call | solution.py:539
  (10 shorter events, 0.1 us)
Async XLA Ops:
  23.5 2.6 %collective-permute-start.2 = (bf16[64,1792]{1,0:T(8,128)(2,1)S(1)}, bf16[64,1792]{1,0:T(8,128)(2,1)S(1)}, u32[]{:S(2)}, u32[]{:S(2)}) collective-permute-start(bf16[64,1792]{1,0:T(8,128)(2,1)S(1)} %get-tuple-element.57.refs_1_.refs_0_), channel_id=1, source_target_pairs={{0,1},{1,0},{2,3},{3,2},{4,5},{5,4},{6,7},{7,6},{8,9},{9,8},{10,11... | collective-permute-start | bytes 688136 | tf_op jit(solution)/shard_map/ppermute | solution.py:24
  23.6 2.5 %collective-permute-start.1 = (bf16[64,1792]{1,0:T(8,128)(2,1)S(1)}, bf16[64,1792]{1,0:T(8,128)(2,1)S(1)}, u32[]{:S(2)}, u32[]{:S(2)}) collective-permute-start(bf16[64,1792]{1,0:T(8,128)(2,1)S(1)} %get-tuple-element.58.refs_0_), channel_id=1, source_target_pairs={{0,1},{1,0},{2,3},{3,2},{4,5},{5,4},{6,7},{7,6},{8,9},{9,8},{10,11... | collective-permute-start | bytes 688136 | tf_op jit(solution)/shard_map/ppermute | solution.py:24
  24.1 9.7 %collective-permute-start = (bf16[64,1792]{1,0:T(8,128)(2,1)S(1)}, bf16[64,1792]{1,0:T(8,128)(2,1)S(1)}, u32[]{:S(2)}, u32[]{:S(2)}) collective-permute-start(bf16[64,1792]{1,0:T(8,128)(2,1)S(1)} %get-tuple-element.58.refs_0_), channel_id=1, source_target_pairs={{0,2},{1,3},{2,0},{3,1},{4,6},{5,7},{6,4},{7,5},{8,10},{9,11},{10,... | collective-permute-start | bytes 688136 | tf_op jit(solution)/shard_map/ppermute | solution.py:24
  25.6 11.0 %collective-permute-start.4 = (bf16[64,1792]{1,0:T(8,128)(2,1)S(1)}, bf16[64,1792]{1,0:T(8,128)(2,1)S(1)}, u32[]{:S(2)}, u32[]{:S(2)}) collective-permute-start(bf16[64,1792]{1,0:T(8,128)(2,1)S(1)} %get-tuple-element.57.refs_1_.refs_0_), channel_id=1, source_target_pairs={{0,2},{1,3},{2,0},{3,1},{4,6},{5,7},{6,4},{7,5},{8,10},{9,11},{10,... | collective-permute-start | bytes 688136 | tf_op jit(solution)/shard_map/ppermute | solution.py:24
  33.8 3.5 %collective-permute-start.3 = (bf16[64,1792]{1,0:T(8,128)(2,1)S(1)}, bf16[64,1792]{1,0:T(8,128)(2,1)S(1)}, u32[]{:S(2)}, u32[]{:S(2)}) collective-permute-start(bf16[64,1792]{1,0:T(8,128)(2,1)S(1)} %collective-permute-done.refs_0_.refs_2_), channel_id=1, source_target_pairs={{0,1},{1,0},{2,3},{3,2},{4,5},{5,4},{6,7},{7,6},{8,9},{9,8},{10,11... | collective-permute-start | bytes 688136 | tf_op jit(solution)/shard_map/ppermute | solution.py:24
  36.6 1.5 %collective-permute-start.5 = (bf16[64,1792]{1,0:T(8,128)(2,1)S(1)}, bf16[64,1792]{1,0:T(8,128)(2,1)S(1)}, u32[]{:S(2)}, u32[]{:S(2)}) collective-permute-start(bf16[64,1792]{1,0:T(8,128)(2,1)S(1)} %collective-permute-done.4.refs_0_.refs_2_), channel_id=1, source_target_pairs={{0,1},{1,0},{2,3},{3,2},{4,5},{5,4},{6,7},{7,6},{8,9},{9,8},{10,11... | collective-permute-start | bytes 688136 | tf_op jit(solution)/shard_map/ppermute | solution.py:24
  40.8 1.6 %collective-permute-start.6 = (bf16[64,1792]{1,0:T(8,128)(2,1)S(1)}, bf16[64,1792]{1,0:T(8,128)(2,1)S(1)}, u32[]{:S(2)}, u32[]{:S(2)}) collective-permute-start(bf16[64,1792]{1,0:T(8,128)(2,1)S(1)} %terms.5), channel_id=1, source_target_pairs={{0,1},{1,0},{2,3},{3,2},{4,5},{5,4},{6,7},{7,6},{8,9},{9,8},{10,11... | collective-permute-start | bytes 688136 | tf_op jit(solution)/shard_map/ppermute | solution.py:24
  42.4 7.8 %collective-permute-start.7 = (bf16[64,1792]{1,0:T(8,128)(2,1)S(1)}, bf16[64,1792]{1,0:T(8,128)(2,1)S(1)}, u32[]{:S(2)}, u32[]{:S(2)}) collective-permute-start(bf16[64,1792]{1,0:T(8,128)(2,1)S(1)} %add_convert_fusion.1.after_ref), channel_id=1, source_target_pairs={{0,2},{1,3},{2,0},{3,1},{4,6},{5,7},{6,4},{7,5},{8,10},{9,11},{10,... | collective-permute-start | bytes 688136 | tf_op jit(solution)/shard_map/ppermute | solution.py:24
  43.9 7.6 %collective-permute-start.9 = (bf16[64,128]{1,0:T(8,128)(2,1)S(1)}, bf16[64,128]{1,0:T(8,128)(2,1)S(1)}, u32[]{:S(2)}, u32[]{:S(2)}) collective-permute-start(bf16[64,128]{1,0:T(8,128)(2,1)S(1)} %get-tuple-element.49.after_ref.last_ref), channel_id=1, source_target_pairs={{0,1},{1,0},{2,3},{3,2},{4,5},{5,4},{6,7},{7,6},{8,9},{9,8},{10,11... | collective-permute-start | bytes 49160 | tf_op jit(solution)/shard_map/ppermute | solution.py:24
  51.4 2.9 %collective-permute-start.8 = (bf16[64,1792]{1,0:T(8,128)(2,1)S(1)}, bf16[64,1792]{1,0:T(8,128)(2,1)S(1)}, u32[]{:S(2)}, u32[]{:S(2)}) collective-permute-start(bf16[64,1792]{1,0:T(8,128)(2,1)S(1)} %terms.7), channel_id=1, source_target_pairs={{0,1},{1,0},{2,3},{3,2},{4,5},{5,4},{6,7},{7,6},{8,9},{9,8},{10,11... | collective-permute-start | bytes 688136 | tf_op jit(solution)/shard_map/ppermute | solution.py:24
  51.5 3.8 %collective-permute-start.10 = (bf16[64,128]{1,0:T(8,128)(2,1)S(1)}, bf16[64,128]{1,0:T(8,128)(2,1)S(1)}, u32[]{:S(2)}, u32[]{:S(2)}) collective-permute-start(bf16[64,128]{1,0:T(8,128)(2,1)S(1)} %add_convert_fusion.2.cols_ref), channel_id=1, source_target_pairs={{0,2},{1,3},{2,0},{3,1},{4,6},{5,7},{6,4},{7,5},{8,10},{9,11},{10,... | collective-permute-start | bytes 49160 | tf_op jit(solution)/shard_map/ppermute | solution.py:24
  56.1 11.8 %all-to-all-start.1 = ((bf16[8,8,1920]{2,1,0:T(8,128)(2,1)}), bf16[8,8,1920]{2,1,0:T(8,128)(2,1)S(1)}, u32[]{:S(2)}, u32[]{:S(2)}) async-start(bf16[8,8,1920]{2,1,0:T(8,128)(2,1)} %settle.1.after_ref), calls=%async_computation.1 | async-start | bytes 491520 | tf_op jit(solution)/shard_map/all_to_all | solution.py:611

commit v2 on v1

--- a/solution.py
+++ b/solution.py
@@ -1,4 +1,5 @@
 import functools
+import math
 
 import jax
 import jax.numpy as jnp
@@ -73,18 +74,6 @@
                 total = value if total is None else add(total, value)
         mask *= 2
     return total
-
-
-def sum_all(value, axis):
-    size = lax.axis_size(axis)
-    arrived = jnp.zeros_like(value)
-    mask = 1
-    while mask < size:
-        if mask > 1:
-            value = add(value, arrived)
-        arrived = swap(value, axis, mask)
-        mask *= 2
-    return value, arrived
 
 
 def one_hot(ids, gates, expert, experts):
@@ -107,32 +96,84 @@
     return lax.broadcasted_iota(jnp.int32, (experts * CAP, tokens), 0) // CAP
 
 
-def pack_kernel(experts, ids_ref, gates_ref, x_ref, d_ref, slot_out, pick_out, gates_out):
-    ids = ids_ref[...]
-    gates = gates_ref[...].astype(F32)
-    pick, pick_gate = one_hot(ids, gates, row_blocks(experts, ids.shape[1]), experts)
-    pick_out[...] = pick.astype(BF16)
+def column_block(feat):
+    return feat // 2 if feat % (2 * LANES) == 0 else feat
+
+
+def pack_kernel(
+    experts, block, ids_hbm, gates_hbm, x_hbm, d_hbm, slot_hbm, pick_out, gates_out, ids, gates_low, x_ref, d_ref, slots, sems
+):
+    feat = x_ref.shape[1]
+    steps = feat // block
+
+    def columns(step):
+        return slice(step * block, (step + 1) * block)
+
+    small = [
+        pltpu.make_async_copy(ids_hbm, ids, sems.at[3, 0]),
+        pltpu.make_async_copy(gates_hbm, gates_low, sems.at[4, 0]),
+    ]
+    loads = [
+        [
+            pltpu.make_async_copy(src.at[:, columns(step)], dst.at[:, columns(step)], sems.at[i, step])
+            for i, (src, dst) in enumerate(((x_hbm, x_ref), (d_hbm, d_ref)))
+        ]
+        for step in range(steps)
+    ]
+    stores = [
+        pltpu.make_async_copy(
+            slots.at[:, :, columns(step)], slot_hbm.at[:, :, columns(step)], sems.at[2, step]
+        )
+        for step in range(steps)
+    ]
+    for copy in small + [copy for pair in loads for copy in pair]:
+        copy.start()
+    for copy in small:
+        copy.wait()
+    gates = gates_low[...].astype(F32)
+    pick, pick_gate = one_hot(ids[...], gates, row_blocks(experts, ids.shape[1]), experts)
+    pick, pick_gate = pick.astype(BF16), pick_gate.astype(BF16)
+    for step in range(steps):
+        for copy in loads[step]:
+            copy.wait()
+        slot_x = jnp.dot(pick, x_ref[:, columns(step)], preferred_element_type=F32)
+        slot_d = jnp.dot(pick_gate, d_ref[:, columns(step)], preferred_element_type=F32)
+        for i in range(experts):
+            slots[i, :, columns(step)] = jnp.concatenate(
+                [slot_x[i * CAP:(i + 1) * CAP], slot_d[i * CAP:(i + 1) * CAP]], axis=0
+            ).astype(BF16)
+        stores[step].start()
+    pick_out[...] = pick
     gates_out[...] = gates
-    slot_x = jnp.dot(pick.astype(BF16), x_ref[...], preferred_element_type=F32)
-    slot_d = jnp.dot(pick_gate.astype(BF16), d_ref[...], preferred_element_type=F32)
-    for i in range(experts):
-        slot_out[i] = jnp.concatenate(
-            [slot_x[i * CAP:(i + 1) * CAP], slot_d[i * CAP:(i + 1) * CAP]], axis=0
-        ).astype(BF16)
+    for copy in stores:
+        copy.wait()
 
 
 def pack(ids, gates, tokens, cotangent, experts):
     count, feat = tokens.shape
-    return pl.pallas_call(
-        functools.partial(pack_kernel, experts),
+    block = column_block(feat)
+    steps = feat // block
+    rows = experts * CAP
+    hbm = pl.BlockSpec(memory_space=pltpu.HBM)
+    return pl.pallas_call(
+        functools.partial(pack_kernel, experts, block),
         out_shape=[
             jax.ShapeDtypeStruct((experts, 2 * CAP, feat), BF16),
-            jax.ShapeDtypeStruct((experts * CAP, count), BF16),
+            jax.ShapeDtypeStruct((rows, count), BF16),
             jax.ShapeDtypeStruct((2, count), F32),
         ],
-        in_specs=[VMEM] * 4,
-        out_specs=[VMEM] * 3,
+        in_specs=[hbm] * 4,
+        out_specs=[hbm, VMEM, VMEM],
+        scratch_shapes=[
+            pltpu.VMEM((2, count), jnp.int32),
+            pltpu.VMEM((2, count), BF16),
+            pltpu.VMEM((count, feat), BF16),
+            pltpu.VMEM((count, feat), BF16),
+            pltpu.VMEM((experts, 2 * CAP, feat), BF16),
+            pltpu.SemaphoreType.DMA((5, steps)),
+        ],
         cost_estimate=pl.CostEstimate(flops=10**8, bytes_accessed=2 * 10**6, transcendentals=0),
+        compiler_params=pltpu.CompilerParams(vmem_limit_bytes=2**23),
         name="pack",
     )(*[pltpu.with_memory_space_constraint(a, pltpu.HBM) for a in (ids, gates, tokens, cotangent)])
 
@@ -256,83 +297,79 @@
     return index
 
 
-def load_early_kernel(near, far, x0, d0, x1, d1, gate_in, up_in, down_in, gate, up, down, *refs):
+def load_early_kernel(x0, d0, gate_in, up_in, down_in, gate, up, down, *refs):
     sums, sems = refs[:3], refs[3]
     feat = x0.shape[1]
     me = lax.axis_index("expert")
+    shards = gate.shape[0] // feat
+
+    def place(rel):
+        return pl.ds(pl.multiple_of(flip(me, rel) * feat, feat), feat)
 
     def copies(rel):
-        at = pl.ds(pl.multiple_of(flip(me, rel) * feat, feat), feat)
+        at = place(rel)
         return [
-            pltpu.make_async_copy(src.at[place], dst.at[place], sems.at[i, rel])
-            for i, (src, dst, place) in enumerate(
+            pltpu.make_async_copy(src.at[where], dst.at[where], sems.at[i, rel])
+            for i, (src, dst, where) in enumerate(
                 ((gate_in, gate, at), (up_in, up, at), (down_in, down, (slice(None), at)))
             )
         ]
 
-    first = [copies(rel) for rel in near]
-    rest = [copies(rel) for rel in far]
+    first, *rest = [copies(rel) for rel in range(shards)]
+    for copy in first:
+        copy.start()
+    for group in rest:
+        for copy in group:
+            copy.start()
+    at = place(0)
     for i in range(3):
-        for group in first:
-            group[i].start()
-    for i in range(3):
-        for group in first:
-            group[i].wait()
-        if i == 0:
-            for group in rest:
-                for copy in group:
-                    copy.start()
-        total = None
-        for rel, x_ref, d_ref in zip(near, (x0, x1), (d0, d1)):
-            at = pl.ds(pl.multiple_of(flip(me, rel) * feat, feat), feat)
-            if i < 2:
-                part = jnp.dot(x_ref[...], (gate, up)[i][at, :], preferred_element_type=F32)
-            else:
-                part = lax.dot_general(
-                    d_ref[...], down[:, at], (((1,), (1,)), ((), ())), preferred_element_type=F32
-                )
-            total = part if total is None else total + part
-        sums[i][...] = total
+        first[i].wait()
+        if i < 2:
+            sums[i][...] = jnp.dot(x0[...], (gate, up)[i][at, :], preferred_element_type=F32)
+        else:
+            sums[i][...] = lax.dot_general(
+                d0[...], down[:, at], (((1,), (1,)), ((), ())), preferred_element_type=F32
+            )
     for group in rest:
         for copy in group:
             copy.wait()
 
 
 def load_early(x, d, weights, after):
+    rows = x.shape[0]
+    units = weights[0].shape[1]
     shards = lax.axis_size("expert")
-    rows = x[0].shape[0]
-    units = weights[0].shape[1]
-    near, far = list(range(2)), list(range(2, shards))
-    kernel = functools.partial(load_early_kernel, near, far)
     out = pl.pallas_call(
-        lambda after_ref, *refs: kernel(*refs),
+        lambda after_ref, *refs: load_early_kernel(*refs),
         out_shape=[pltpu.VMEM(a.shape, a.dtype) for a in weights]
         + [jax.ShapeDtypeStruct((rows, units), F32)] * 3,
         in_specs=[pl.BlockSpec(memory_space=pl.ANY)]
-        + [VMEM] * 4
+        + [VMEM] * 2
         + [pl.BlockSpec(memory_space=pltpu.HBM)] * 3,
         out_specs=[VMEM] * 6,
         scratch_shapes=[pltpu.SemaphoreType.DMA((3, shards))],
         cost_estimate=pl.CostEstimate(
-            flops=6 * rows * units * x[0].shape[1],
+            flops=6 * rows * units * x.shape[1],
             bytes_accessed=sum(a.size * 2 for a in weights),
             transcendentals=0,
         ),
         compiler_params=pltpu.CompilerParams(vmem_limit_bytes=2**23),
         name="load_early",
     )(
-        after,
-        *[keep(a) for a in (x[0], d[0], x[1], d[1])],
+        keep(after),
+        keep(x),
+        keep(d),
         *[pltpu.with_memory_space_constraint(a, pltpu.HBM) for a in weights],
     )
     return out[:3], out[3:]
 
 
-def late_kernel(rels, me_ref, *refs):
+def late_kernel(rels, feat, me_ref, *refs):
     count = len(rels)
     x_refs, d_refs, refs = refs[:count], refs[count:2 * count], refs[2 * count:]
-    gate_ref, up_ref, down_ref, sum_refs = refs[0], refs[1], refs[2], refs[3:-4]
-    hidden_out, d_gate_out, d_up_out, cols_out = refs[-4:]
+    refs, outs = refs[:-4 - count], refs[-4 - count:]
+    (gate_ref, up_ref, down_ref), sum_refs = refs[:3], refs[3:]
+    hidden_out, d_gate_out, d_up_out, cols_out = outs[:4]
     totals = [ref[...] for ref in sum_refs[:3]]
     for i, ref in enumerate(sum_refs[3:]):
         totals[i % 3] += ref[...]
@@ -343,22 +380,29 @@
     sig = 1.0 / (1.0 + jnp.exp(-pre_gate))
     act = pre_gate * sig
     hidden = (act * pre_up).astype(BF16)
+    d_gate = (dhid * pre_up * sig * (1.0 + pre_gate * (1.0 - sig))).astype(BF16)
+    d_up = (dhid * act).astype(BF16)
+    total = jnp.sum(dhid * hidden.astype(F32), axis=1, keepdims=True)
+    cols = jnp.broadcast_to(total, cols_out.shape).astype(BF16)
+    for rel, out in zip(rels, outs[4:]):
+        out[:, :feat] = term_piece(me_ref, rel, 0, feat, feat, d_gate, d_up, gate_ref, up_ref)
+        out[:, feat:] = cols
     hidden_out[...] = hidden
-    d_gate_out[...] = (dhid * pre_up * sig * (1.0 + pre_gate * (1.0 - sig))).astype(BF16)
-    d_up_out[...] = (dhid * act).astype(BF16)
-    total = jnp.sum(dhid * hidden.astype(F32), axis=1, keepdims=True)
-    cols_out[...] = jnp.broadcast_to(total, cols_out.shape).astype(BF16)
-
-
-def late(rels, me, x, d, weights, sums):
+    d_gate_out[...] = d_gate
+    d_up_out[...] = d_up
+    cols_out[...] = cols
+
+
+def late(rels, me, x, d, weights, sums, feat):
     rows, units = sums[0].shape
-    work = 6 * rows * units * max(1, sum(a.shape[1] for a in x))
-    return pl.pallas_call(
-        functools.partial(late_kernel, rels),
+    work = 10 * rows * units * feat * max(1, len(rels))
+    return pl.pallas_call(
+        functools.partial(late_kernel, rels, feat),
         out_shape=[jax.ShapeDtypeStruct((rows, units), BF16)] * 3
-        + [jax.ShapeDtypeStruct((rows, LANES), BF16)],
+        + [jax.ShapeDtypeStruct((rows, LANES), BF16)]
+        + [jax.ShapeDtypeStruct((rows, feat + LANES), BF16)] * len(rels),
         in_specs=[SMEM] + [VMEM] * (2 * len(rels) + 3 + len(sums)),
-        out_specs=[VMEM] * 4,
+        out_specs=[VMEM] * (4 + len(rels)),
         cost_estimate=pl.CostEstimate(
             flops=work, bytes_accessed=work // rows, transcendentals=rows * units
         ),
@@ -367,33 +411,45 @@
     )(me, *[keep(a) for a in (*x, *d, *weights, *sums)])
 
 
-def term_kernel(rels, me_ref, after_ref, last_ref, d_gate_ref, d_up_ref, gate_ref, up_ref, *outs):
-    feat = outs[0].shape[1]
+def term_piece(me_ref, rel, low, high, feat, d_gate, d_up, gate_ref, up_ref):
     dims = (((1,), (1,)), ((), ()))
-    for rel, out in zip(rels, outs):
-        at = shard_at(me_ref, rel, feat)
-        term = lax.dot_general(d_gate_ref[...], gate_ref[at, :], dims, preferred_element_type=F32)
-        term += lax.dot_general(d_up_ref[...], up_ref[at, :], dims, preferred_element_type=F32)
-        out[...] = term.astype(BF16)
-
-
-def terms(rels, me, after, d_gate, d_up, gate_m, up_m, feat):
-    rows, units = d_gate.shape
-    return pl.pallas_call(
-        functools.partial(term_kernel, rels),
-        out_shape=[jax.ShapeDtypeStruct((rows, feat), BF16)] * len(rels),
-        in_specs=[SMEM] + [pl.BlockSpec(memory_space=pl.ANY)] * 2 + [VMEM] * 4,
-        out_specs=[VMEM] * len(rels),
-        cost_estimate=pl.CostEstimate(flops=10**6, bytes_accessed=10**6, transcendentals=0),
+    start = (me_ref[0] ^ rel) * feat + low
+    at = pl.ds(pl.multiple_of(start, math.gcd(feat, low)), high - low)
+    term = lax.dot_general(d_gate, gate_ref[at, :], dims, preferred_element_type=F32)
+    term += lax.dot_general(d_up, up_ref[at, :], dims, preferred_element_type=F32)
+    return term.astype(BF16)
+
+
+def term_kernel(pieces, feat, me_ref, after_ref, last_ref, d_gate_ref, d_up_ref, cols_ref, gate_ref, up_ref, *outs):
+    for (rel, low, high), out in zip(pieces, outs):
+        out[:, :high - low] = term_piece(
+            me_ref, rel, low, high, feat, d_gate_ref[...], d_up_ref[...], gate_ref, up_ref
+        )
+        if high == feat:
+            out[:, high - low:] = cols_ref[...]
+
+
+def terms(pieces, me, after, d_gate, d_up, cols, gate_m, up_m, feat):
+    rows = d_gate.shape[0]
+    return pl.pallas_call(
+        functools.partial(term_kernel, pieces, feat),
+        out_shape=[
+            jax.ShapeDtypeStruct((rows, high - low + (LANES if high == feat else 0)), BF16)
+            for rel, low, high in pieces
+        ],
+        in_specs=[SMEM] + [pl.BlockSpec(memory_space=pl.ANY)] * 2 + [VMEM] * 5,
+        out_specs=[VMEM] * len(pieces),
+        cost_estimate=pl.CostEstimate(flops=1, bytes_accessed=1, transcendentals=0),
         compiler_params=pltpu.CompilerParams(vmem_limit_bytes=2**24),
         name="terms",
-    )(me, *after, *[keep(a) for a in (d_gate, d_up, gate_m, up_m)])
+    )(me, *after, *[keep(a) for a in (d_gate, d_up, cols, gate_m, up_m)])
 
 
 SLOTS = 4
 
 
-def stream(steps, fill, copies):
+def stream(steps, fill, copies, beside=()):
+    beside = list(beside)
     for step in range(steps + SLOTS):
         if step >= SLOTS:
             for copy in copies(step - SLOTS, step % SLOTS):
@@ -402,6 +458,8 @@
             fill(step, step % SLOTS)
             for copy in copies(step, step % SLOTS):
                 copy.start()
+            if steps - step <= len(beside):
+                beside[step - steps]()
 
 
 def places(feat, shards, block):
@@ -465,10 +523,13 @@
     )(pltpu.with_memory_space_constraint(after, pltpu.HBM), *[keep(a) for a in (*lefts, *rights)])
 
 
-def outer_columns_kernel(block, shards, after_ref, left_ref, *refs):
-    rights, (out_ref, turned, stage, sems) = refs[:shards], refs[shards:]
+def middle_kernel(
+    block, pieces, feat, me_ref, after_ref, left_ref, d_gate_ref, d_up_ref, cols_ref, gate_ref, up_ref, *refs
+):
+    outs, (turned, stage, sems) = refs[-4 - len(pieces):-3], refs[-3:]
+    rights, out_ref, outs = refs[:-4 - len(pieces)], outs[0], outs[1:]
     turned[...] = left_ref[...].astype(F32).T.astype(BF16)
-    steps, source, place = places(rights[0].shape[1], shards, block)
+    steps, source, place = places(rights[0].shape[1], len(rights), block)
 
     def fill(step, slot):
         rel, at = source(step)
@@ -477,76 +538,102 @@
     def copies(step, slot):
         return [pltpu.make_async_copy(stage.at[slot], out_ref.at[:, place(step)], sems.at[slot])]
 
-    stream(steps, fill, copies)
-
-
-def outer_columns(left, rights, after, block):
-    rows, feat = rights[0].shape
-    wide = feat * len(rights)
+    def term(piece, out):
+        rel, low, high = piece
+        out[:, :high - low] = term_piece(
+            me_ref, rel, low, high, feat, d_gate_ref[...], d_up_ref[...], gate_ref, up_ref
+        )
+        if high == feat:
+            out[:, high - low:] = cols_ref[...]
+
+    stream(steps, fill, copies, [functools.partial(term, *pair) for pair in zip(pieces, outs)])
+
+
+def middle(left, rights, after, block, pieces, me, d_gate, d_up, cols, gate_m, up_m, feat):
+    rows = left.shape[0]
+    wide = rights[0].shape[1] * len(rights)
     tall = left.shape[1]
     return pl.pallas_call(
-        functools.partial(outer_columns_kernel, block, len(rights)),
-        out_shape=jax.ShapeDtypeStruct((tall, wide), BF16),
-        in_specs=[pl.BlockSpec(memory_space=pl.ANY)] + [VMEM] * (1 + len(rights)),
-        out_specs=pl.BlockSpec(memory_space=pltpu.HBM),
+        functools.partial(middle_kernel, block, pieces, feat),
+        out_shape=[jax.ShapeDtypeStruct((tall, wide), BF16)]
+        + [
+            jax.ShapeDtypeStruct((rows, high - low + (LANES if high == feat else 0)), BF16)
+            for rel, low, high in pieces
+        ],
+        in_specs=[SMEM, pl.BlockSpec(memory_space=pl.ANY)] + [VMEM] * (6 + len(rights)),
+        out_specs=[pl.BlockSpec(memory_space=pltpu.HBM)] + [VMEM] * len(pieces),
         scratch_shapes=[
             pltpu.VMEM((tall, rows), BF16),
             pltpu.VMEM((SLOTS, tall, block), BF16),
             pltpu.SemaphoreType.DMA((SLOTS,)),
         ],
-        cost_estimate=pl.CostEstimate(flops=10**6, bytes_accessed=10**6, transcendentals=0),
+        cost_estimate=pl.CostEstimate(
+            flops=4 * rows * wide * tall, bytes_accessed=2 * wide * tall, transcendentals=0
+        ),
         compiler_params=pltpu.CompilerParams(vmem_limit_bytes=2**24),
-        name="outer_columns",
-    )(keep(after), keep(left), *[keep(a) for a in rights])
-
-
-def settle_kernel(held_ref, arrived_ref, cols_ref, more_ref, after_ref, out_ref):
-    feat = held_ref.shape[1]
-    total = held_ref[...].astype(F32) + arrived_ref[...].astype(F32)
-    cols = cols_ref[...].astype(F32) + more_ref[...].astype(F32)
-    for i in range(out_ref.shape[0]):
-        out_ref[i, :, :feat] = total[i * CAP:(i + 1) * CAP].astype(BF16)
-        out_ref[i, :, feat:] = cols[i * CAP:(i + 1) * CAP].astype(BF16)
-
-
-def settle(own, cols, after):
-    rows, feat = own[0].shape
-    return pl.pallas_call(
-        settle_kernel,
-        out_shape=jax.ShapeDtypeStruct((rows // CAP, CAP, feat + LANES), BF16),
-        in_specs=[VMEM] * 4 + [pl.BlockSpec(memory_space=pl.ANY)],
+        name="middle",
+    )(me, keep(after), *[keep(a) for a in (left, d_gate, d_up, cols, gate_m, up_m, *rights)])
+
+
+def settle_kernel(count, *refs):
+    pieces, parts, out_ref = refs[:count], refs[count:-2], refs[-1]
+    low = 0
+    for piece in pieces:
+        at = slice(low, low + piece.shape[1])
+        total = piece[...].astype(F32)
+        for ref in parts:
+            total += ref[:, at].astype(F32)
+        for i in range(out_ref.shape[0]):
+            out_ref[i, :, at] = total[i * CAP:(i + 1) * CAP].astype(BF16)
+        low += piece.shape[1]
+
+
+def settle(pieces, parts, after):
+    rows = pieces[0].shape[0]
+    wide = sum(a.shape[1] for a in pieces)
+    return pl.pallas_call(
+        functools.partial(settle_kernel, len(pieces)),
+        out_shape=jax.ShapeDtypeStruct((rows // CAP, CAP, wide), BF16),
+        in_specs=[VMEM] * (len(pieces) + len(parts)) + [pl.BlockSpec(memory_space=pl.ANY)],
         out_specs=VMEM,
         cost_estimate=pl.CostEstimate(flops=0, bytes_accessed=10**6, transcendentals=0),
         name="settle",
-    )(*[keep(a) for a in (*own, *cols)], pltpu.with_memory_space_constraint(after, pltpu.HBM))
-
-
-def combine_kernel(pick_ref, gates_ref, rows_ref, grad_ref, gate_ref):
-    feat = grad_ref.shape[1]
-    half = pick_ref.shape[0] // 2
+    )(*[keep(a) for a in (*pieces, *parts)], pltpu.with_memory_space_constraint(after, pltpu.HBM))
+
+
+def combine_kernel(feat, block, pick_ref, gates_ref, rows_ref, grad_ref, gate_ref):
     pick = pick_ref[...]
-    rows = rows_ref[...]
+    at = pl.ds(pl.multiple_of(pl.program_id(0) * block, block), block) if block < feat else slice(0, feat)
     grad_ref[...] = lax.dot_general(
-        pick, rows[:, :feat], (((0,), (0,)), ((), ())), preferred_element_type=F32
+        pick, rows_ref[:, at], (((0,), (0,)), ((), ())), preferred_element_type=F32
     ).astype(BF16)
-    terms = pick.astype(F32) * rows[:, feat:].astype(F32)
-    gate_ref[0:1, :] = jnp.sum(terms[:half], axis=0, keepdims=True) / gates_ref[0:1, :]
-    gate_ref[1:2, :] = jnp.sum(terms[half:], axis=0, keepdims=True) / gates_ref[1:2, :]
+
+    @pl.when(pl.program_id(0) == 0)
+    def _():
+        half = pick.shape[0] // 2
+        terms = pick.astype(F32) * rows_ref[:, feat:].astype(F32)
+        gate_ref[0:1, :] = jnp.sum(terms[:half], axis=0, keepdims=True) / gates_ref[0:1, :]
+        gate_ref[1:2, :] = jnp.sum(terms[half:], axis=0, keepdims=True) / gates_ref[1:2, :]
 
 
 def combine(pick, gates, rows, feat):
     count = pick.shape[1]
-    return pl.pallas_call(
-        combine_kernel,
+    block = column_block(feat)
+    return pl.pallas_call(
+        functools.partial(combine_kernel, feat, block),
+        grid=(feat // block,),
         out_shape=[
             jax.ShapeDtypeStruct((count, feat), BF16),
             jax.ShapeDtypeStruct((2, count), F32),
         ],
         in_specs=[VMEM] * 3,
-        out_specs=[VMEM] * 2,
+        out_specs=[
+            pl.BlockSpec((count, block), lambda i: (0, i)),
+            pl.BlockSpec((2, count), lambda i: (0, 0)),
+        ],
         cost_estimate=pl.CostEstimate(flops=10**8, bytes_accessed=10**6, transcendentals=0),
         name="combine",
-    )(pick, gates, pltpu.with_memory_space_constraint(rows, pltpu.VMEM))
+    )(*[keep(a) for a in (pick, gates, rows)])
 
 
 def per_device(tokens, cotangent, gates, expert_ids, w_gate, w_up, w_down):
@@ -572,42 +659,47 @@
         odd = []
     else:
         x[1], d[1] = swap(x[0], "expert", 1), swap(d[0], "expert", 1)
-        weights, sums = load_early(x, d, weights, slots)
+        weights, sums = load_early(x[0], d[0], weights, slots)
         even = list(range(2, shards, 2))
         odd = list(range(3, shards, 2))
         rest, sums = lax.optimization_barrier(([x[i] for i in even], sums))
         for i, x_i in zip(even, rest):
             x[i], x[i + 1] = x_i, swap(x_i, "expert", 1)
-        more = partial(partial_x_kernel, 2, even, me_ref, sums[0], rest, weights)
+        rels = [1] + even
+        more = partial(partial_x_kernel, 2, rels, me_ref, sums[0], [x[1]] + rest, weights)
         rest, more = lax.optimization_barrier(([d[i] for i in even], more))
         for i, d_i in zip(even, rest):
             d[i], d[i + 1] = d_i, swap(d_i, "expert", 1)
-        more = [*more, *partial(partial_d_kernel, 1, even, me_ref, more[0], rest, weights)]
+        more = [*more, *partial(partial_d_kernel, 1, rels, me_ref, more[0], [d[1]] + rest, weights)]
         x, d = [x[i] for i in range(shards)], [d[i] for i in range(shards)]
         sums = [*sums, *more]
-    hidden, d_gate, d_up, cols = late(odd, me_ref, [x[i] for i in odd], [d[i] for i in odd], weights, sums)
-
-    def term(rels, after):
-        got = terms(rels, me_ref, after, d_gate, d_up, *weights[:2], feat) if rels else []
-        return dict(zip(rels, got))
+    hidden, d_gate, d_up, cols, *sent = late(
+        odd, me_ref, [x[i] for i in odd], [d[i] for i in odd], weights, sums, feat
+    )
+
+    def term(pieces, after):
+        return terms(pieces, me_ref, after, d_gate, d_up, cols, *weights[:2], feat) if pieces else []
 
     start = (keep(cols), keep(cols))
-    sent = term(list(range(3, shards, 2)), start)
-    arrived = {rel ^ 1: swap(part, "expert", 1) for rel, part in sent.items()}
-    kept = term(list(range(2, shards, 2)), start)
-    held = {rel: add(part, arrived[rel]) for rel, part in kept.items()}
+    if not odd:
+        sent = term([(rel, 0, feat) for rel in range(3, shards, 2)], start)
+    arrived = [swap(part, "expert", 1) for part in sent]
+    even = list(range(2, shards, 2))
+    kept = term([(rel, 0, feat) for rel in even], start)
+    held = {rel: add(part, more) for rel, part, more in zip(even, kept, arrived)}
     last = held[max(held)] if held else cols
     wide = feat * shards
-    grad_down = outer_columns(hidden, d, last, wide // 8)
     other = sum_far(held, "expert")
-    if other is None:
-        other = jnp.zeros((rows, feat), BF16)
-    start = (keep(other), pltpu.with_memory_space_constraint(grad_down, pltpu.HBM))
-    sent = term([1] if shards > 1 else [], start)
-    own = term([0], start)[0]
-    for part in sent.values():
-        own = add(own, swap(part, "expert", 1))
-    total = settle((own, other), sum_all(cols, "expert"), grad_down)
+    half = feat // (2 * LANES) * LANES
+    pieces = ([(1, 0, feat)] if shards > 1 else []) + [(0, 0, half)]
+    grad_down, *sent, first = middle(
+        hidden, d, last, wide // 8, pieces, me_ref, d_gate, d_up, cols, *weights[:2], feat
+    )
+    down_done = pltpu.with_memory_space_constraint(grad_down, pltpu.HBM)
+    parts = [swap(part, "expert", 1) for part in sent]
+    parts += [] if other is None else [other]
+    second, = term([(0, half, feat)], (keep(parts[-1] if parts else cols), down_done))
+    total = settle([first, second], parts, grad_down)
     got = lax.all_to_all(total, "dp", split_axis=0, concat_axis=0, tiled=True)
     got = got.reshape(rows, feat + LANES)
     grad_gate, grad_up = outer_rows(x, (d_gate, d_up), total, wide // 16)

time: 70.1 us -> 63.5 us (0.906)
  waiting for transfers between devices: 6.13 us -> 1.68 us
  Pallas kernels: 32.5 us -> 31.5 us
  starting transfers between devices: 9.64 us -> 8.89 us
    ppermute x11 -> x9, waiting for transfers between devices: 6.08 us -> 1.36 us  [swap(): return lax.ppermute(value, axis, [(i, i ^ mask) for i in range(size)])]
    pallas_call x10 -> x8, Pallas kernels: 22.9 us -> 20.8 us  [the longest x1 7.44 us: load_early(): pl.pallas_call(lambda after_ref, *refs: load_early_kernel(*refs), out_sha...]
    pallas_call x2, Pallas kernels: 1.43 us -> 2.6 us  [partial(): pl.pallas_call(functools.partial(kernel, rels), out_shape=[jax.ShapeDtype...]
    ppermute x11 -> x9, starting transfers between devices: 6.05 us -> 4.93 us  [swap(): return lax.ppermute(value, axis, [(i, i ^ mask) for i in range(size)])]
  transfers between devices with their start and end apart: 12 -> 10, of which waited for: 6 -> 2; matrix products, arithmetic and copies ran while one was open for 0% -> 0% of each run, Pallas kernels for 36% -> 40%
where the time goes in v2:
time: 63.5 us; the launch traced here: 63.2 us
  Pallas kernels  31.5 us (50%)
  blocking collectives  20.3 us (32%)
  starting transfers between devices  8.89 us (14%)
  waiting for transfers between devices  1.68 us (3%)
  between operations  0.74 us (1%)
    all_to_all x1, blocking collectives, per_device(): slots = lax.all_to_all(slots, 'dp', split_axis=0, concat_axis=0, tiled=True)  20.3 us
    pallas_call x1, Pallas kernels, outer_rows(): pl.pallas_call(functools.partial(outer_rows_kernel, block, len(lefts)), o...  8.15 us
    pallas_call x1, Pallas kernels, load_early(): pl.pallas_call(lambda after_ref, *refs: load_early_kernel(*refs), out_sha...  7.44 us
    pallas_call x1, Pallas kernels, middle(): pl.pallas_call(functools.partial(middle_kernel, block, pieces, feat), out...  5.24 us
    ppermute x9, starting transfers between devices, swap(): return lax.ppermute(value, axis, [(i, i ^ mask) for i in range(size)])  4.93 us
    all_to_all x1, starting transfers between devices, per_device(): got = lax.all_to_all(total, 'dp', split_axis=0, concat_axis=0, tiled=True)  3.96 us
    pallas_call x2, Pallas kernels, partial(): pl.pallas_call(functools.partial(kernel, rels), out_shape=[jax.ShapeDtype...  2.6 us
    pallas_call x1, Pallas kernels, late(): pl.pallas_call(functools.partial(late_kernel, rels, feat), out_shape=[jax...  2.55 us
  transfers between devices with their start and end apart: 10, of which 2 were waited for; matrix products, arithmetic and copies ran while one was open for 0% of the time, Pallas kernels for 40%

profile of v2, /device:TPU:0, one launch (start us, length us, event | category | flops | bytes accessed | tf_op | source)
XLA Modules:
  0.0 63.2 jit_solution(2629757302766883240)
XLA Ops:
  0.6 1.7 %pack.1 = (bf16[8,16,1792]{2,1,0:T(8,128)(2,1)S(1)}, bf16[64,128]{1,0:T(8,128)(2,1)S(1)}, f32[2,128]{1,0:T(2,128)S(1)}) custom-call(s32[2,128]{1,0:T(2,128)} %bitcast.20, bf16[2,128]{1,0:T(2,128)(2,1)} %bitcast.21, bf16[128,1792]{1,0:T(8,128)(2,1)} %x_hbm.1, bf16[128,1792]{1,0:T(8,128)(2,1)} %d_hbm.1), custom_call_target="tpu_custom_call" | custom-call | flops 100000000 | bytes 2000000 | tf_op jit(solution)/shard_map/pack/pallas_call | solution.py:158
  2.3 20.3 %all_to_all.10.after_ref = bf16[8,16,1792]{2,1,0:T(8,128)(2,1)S(1)} all-to-all(bf16[8,16,1792]{2,1,0:T(8,128)(2,1)S(1)} %get-tuple-element.37), channel_id=1, replica_groups=mesh['dp'=8,'expert'=4] {'dp'}, dimensions={0} | all-to-all | bytes 917504 | tf_op jit(solution)/shard_map/all_to_all | solution.py:649
  22.6 1.6 %collective-permute-start = (bf16[64,1792]{1,0:T(8,128)(2,1)S(1)}, bf16[64,1792]{1,0:T(8,128)(2,1)S(1)}, u32[]{:S(2)}, u32[]{:S(2)}) collective-permute-start(bf16[64,1792]{1,0:T(8,128)(2,1)S(1)} %get-tuple-element.66.refs_0_), channel_id=1, source_target_pairs={{0,2},{1,3},{2,0},{3,1},{4,6},{5,7},{6,4},{7,5},{8,10},{9,11},{10,... | collective-permute-start | bytes 688136 | tf_op jit(solution)/shard_map/ppermute | solution.py:25
  24.2 0.0 collective-permute-start.3
  24.2 0.5 collective-permute-start.2
  24.7 0.2 collective-permute-start.5
  25.0 7.4 %load_early.1 = (bf16[7168,512]{1,0:T(8,128)(2,1)S(1)}, bf16[7168,512]{1,0:T(8,128)(2,1)S(1)}, bf16[512,7168]{1,0:T(8,128)(2,1)S(1)}, f32[64,512]{1,0:T(8,128)S(...) custom-call(bf16[8,16,1792]{2,1,0:T(8,128)(2,1)S(1)} %all_to_all.10.after_ref, ...), custom_call_target="tpu_custom_call" | custom-call | flops 352321536 | bytes 22020096 | tf_op jit(solution)/shard_map/load_early/pallas_call | solution.py:342
  32.4 0.3 collective-permute-start.1
  32.8 0.0 collective-permute-done.3.refs_0_.refs_1_
  32.8 1.4 %partial.2 = (f32[64,512]{1,0:T(8,128)S(1)}, f32[64,512]{1,0:T(8,128)S(1)}) custom-call(s32[1]{0:T(128)} %bitcast.2.me_ref, f32[64,512]{1,0:T(8,128)S(1)} %get-tuple-element.42.after_ref.refs_5_, bf16[7168,512]{1,0:T(8,128)(2,1)S(1)} %get-tuple-element.43.gate_ref.refs_2_, bf16[7168,512]{1,0:T(8,128)(2,1)S(1)} %get-tuple-element.44.up_ref.refs_3_, ...), custom_call_target="tpu_custom_call" | custom-call | flops 469762048 | bytes 7340032 | tf_op jit(solution)/shard_map/partial/pallas_call | solution.py:280
  34.2 0.0 collective-permute-done.2.refs_1_.refs_2_
  34.2 0.3 collective-permute-start.4
  34.5 0.0 collective-permute-done.5.refs_0_.refs_1_
  34.5 1.2 %partial.3.refs_10_ = f32[64,512]{1,0:T(8,128)S(1)} custom-call(s32[1]{0:T(128)} %bitcast.2.me_ref, f32[64,512]{1,0:T(8,128)S(1)} %get-tuple-element.51.after_ref.refs_8_, bf16[7168,512]{1,0:T(8,128)(2,1)S(1)} %get-tuple-element.43.gate_ref.refs_2_, bf16[7168,512]{1,0:T(8,128)(2,1)S(1)} %get-tuple-element.44.up_ref.refs_3_, ...), custom_call_target="tpu_custom_call" | custom-call | flops 234881024 | bytes 3670016 | tf_op jit(solution)/shard_map/partial/pallas_call | solution.py:280
  35.7 0.0 collective-permute-done.1.refs_0_.refs_3_
  35.7 0.0 collective-permute-done.4.refs_1_.refs_3_
  35.7 2.5 %late.1 = (bf16[64,512]{1,0:T(8,128)(2,1)S(1)}, bf16[64,512]{1,0:T(8,128)(2,1)S(1)}, bf16[64,512]{1,0:T(8,128)(2,1)S(1)}, bf16[64,128]{1,0:T(8,128)(2,1)S(1)}, bf16[64,1920]{1,0:T(8,128)(2,1)S(1)}) custom-call(s32[1]{0:T(128)} %bitcast.2.me_ref, bf16[64,1792]{1,0:T(8,128)(2,1)S(1)} %collective-permute-done.1.refs_0_.refs_3_, ...), custom_call_target="tpu_custom_call" | custom-call | flops 587202560 | bytes 9175040 | tf_op jit(solution)/shard_map/late/pallas_call | solution.py:399
  38.3 0.3 collective-permute-start.6
  38.6 1.2 %terms.2 = bf16[64,1920]{1,0:T(8,128)(2,1)S(1)} custom-call(s32[1]{0:T(128)} %bitcast.2.me_ref, bf16[64,128]{1,0:T(8,128)(2,1)S(1)} %get-tuple-element.53.after_ref.last_ref.cols_ref, bf16[64,128]{1,0:T(8,128)(2,1)S(1)} %get-tuple-element.53.after_ref.last_ref.cols_ref, bf16[64,512]{1,0:T(8,128)(2,1)S(1)} %get-tuple-element.54.d_gate_ref.refs_4_, ...), custom_call_target="tpu_custom_call" | custom-call | flops 1 | bytes 1 | tf_op jit(solution)/shard_map/terms/pallas_call | solution.py:434
  39.8 0.0 collective-permute-done.6
  39.9 0.1 add_convert_fusion.after_ref
  39.9 1.6 %collective-permute-start.7 = (bf16[64,1920]{1,0:T(8,128)(2,1)S(1)}, bf16[64,1920]{1,0:T(8,128)(2,1)S(1)}, u32[]{:S(2)}, u32[]{:S(2)}) collective-permute-start(bf16[64,1920]{1,0:T(8,128)(2,1)S(1)} %add_convert_fusion.after_ref), channel_id=1, source_target_pairs={{0,2},{1,3},{2,0},{3,1},{4,6},{5,7},{6,4},{7,5},{8,10},{9,11},{10,... | collective-permute-start | bytes 737288 | tf_op jit(solution)/shard_map/ppermute | solution.py:25
  41.5 5.2 %middle.1 = (bf16[512,7168]{1,0:T(8,128)(2,1)}, bf16[64,1920]{1,0:T(8,128)(2,1)S(1)}, bf16[64,896]{1,0:T(8,128)(2,1)S(1)}) custom-call(s32[1]{0:T(128)} %bitcast.2.me_ref, bf16[64,1920]{1,0:T(8,128)(2,1)S(1)} %add_convert_fusion.after_ref, bf16[64,512]{1,0:T(8,128)(2,1)S(1)} %get-tuple-element.57.left_ref, ...), custom_call_target="tpu_custom_call" | custom-call | flops 939524096 | bytes 7340032 | tf_op jit(solution)/shard_map/middle/pallas_call | solution.py:556
  46.7 0.1 collective-permute-start.8
  46.8 1.3 %collective-permute-done.7.after_ref.refs_3_ = bf16[64,1920]{1,0:T(8,128)(2,1)S(1)} collective-permute-done((bf16[64,1920]{1,0:T(8,128)(2,1)S(1)}, bf16[64,1920]{1,0:T(8,128)(2,1)S(1)}, u32[]{:S(2)}, u32[]{:S(2)}) %collective-permute-start.7) | collective-permute-done | bytes 245792 | tf_op jit(solution)/shard_map/ppermute | solution.py:25
  48.1 0.7 %terms.3.refs_1_ = bf16[64,1024]{1,0:T(8,128)(2,1)S(1)} custom-call(s32[1]{0:T(128)} %bitcast.2.me_ref, bf16[64,1920]{1,0:T(8,128)(2,1)S(1)} %collective-permute-done.7.after_ref.refs_3_, bf16[512,7168]{1,0:T(8,128)(2,1)} %get-tuple-element.59.last_ref.refs_4_, bf16[64,512]{1,0:T(8,128)(2,1)S(1)} %get-tuple-element.54.d_gate_ref.refs_4_, ...), custom_call_target="tpu_custom_call" | custom-call | flops 1 | bytes 1 | tf_op jit(solution)/shard_map/terms/pallas_call | solution.py:434
  48.8 0.0 collective-permute-done.8.refs_2_
  48.8 0.8 %settle.1.after_ref = bf16[8,8,1920]{2,1,0:T(8,128)(2,1)} custom-call(bf16[64,896]{1,0:T(8,128)(2,1)S(1)} %get-tuple-element.58.refs_0_, bf16[64,1024]{1,0:T(8,128)(2,1)S(1)} %terms.3.refs_1_, bf16[64,1920]{1,0:T(8,128)(2,1)S(1)} %collective-permute-done.8.refs_2_, bf16[64,1920]{1,0:T(8,128)(2,1)S(1)} %collective-permute-done.7.after_ref.refs_3_, ...), custom_call_target="tpu_custom_call" | custom-call | bytes 1000000 | tf_op jit(solution)/shard_map/settle/pallas_call | solution.py:594
  49.6 4.0 %all-to-all-start.1 = ((bf16[8,8,1920]{2,1,0:T(8,128)(2,1)}), bf16[8,8,1920]{2,1,0:T(8,128)(2,1)S(1)}, u32[]{:S(2)}, u32[]{:S(2)}) async-start(bf16[8,8,1920]{2,1,0:T(8,128)(2,1)} %settle.1.after_ref), calls=%async_computation.1 | async-start | bytes 491520 | tf_op jit(solution)/shard_map/all_to_all | solution.py:703
  53.6 8.1 %outer_rows.1 = (bf16[7168,512]{1,0:T(8,128)(2,1)}, bf16[7168,512]{1,0:T(8,128)(2,1)}) custom-call(bf16[8,8,1920]{2,1,0:T(8,128)(2,1)} %settle.1.after_ref, bf16[64,1792]{1,0:T(8,128)(2,1)S(1)} %get-tuple-element.66.refs_0_, bf16[64,1792]{1,0:T(8,128)(2,1)S(1)} %collective-permute-done.3.refs_0_.refs_1_, ...), custom_call_target="tpu_custom_call" | custom-call | flops 939524096 | bytes 14680064 | tf_op jit(solution)/shard_map/outer_rows/pallas_call | solution.py:507
  61.7 0.3 all-to-all-done.1
  62.0 1.2 %combine.1 = (bf16[128,1792]{1,0:T(8,128)(2,1)}, f32[2,128]{1,0:T(2,128)}) custom-call(bf16[64,128]{1,0:T(8,128)(2,1)S(1)} %get-tuple-element.35.pick_ref, f32[2,128]{1,0:T(2,128)S(1)} %get-tuple-element.36.gates_ref, bf16[64,1920]{1,0:T(8,128)(2,1)S(1)} %bitcast.15), custom_call_target="tpu_custom_call" | custom-call | flops 100000000 | bytes 1000000 | tf_op jit(solution)/shard_map/combine/pallas_call | solution.py:622
  (2 shorter events, 0.0 us)
Async XLA Ops:
  22.6 9.8 %collective-permute-start = (bf16[64,1792]{1,0:T(8,128)(2,1)S(1)}, bf16[64,1792]{1,0:T(8,128)(2,1)S(1)}, u32[]{:S(2)}, u32[]{:S(2)}) collective-permute-start(bf16[64,1792]{1,0:T(8,128)(2,1)S(1)} %get-tuple-element.66.refs_0_), channel_id=1, source_target_pairs={{0,2},{1,3},{2,0},{3,1},{4,6},{5,7},{6,4},{7,5},{8,10},{9,11},{10,... | collective-permute-start | bytes 688136 | tf_op jit(solution)/shard_map/ppermute | solution.py:25
  24.2 8.6 %collective-permute-start.3 = (bf16[64,1792]{1,0:T(8,128)(2,1)S(1)}, bf16[64,1792]{1,0:T(8,128)(2,1)S(1)}, u32[]{:S(2)}, u32[]{:S(2)}) collective-permute-start(bf16[64,1792]{1,0:T(8,128)(2,1)S(1)} %get-tuple-element.66.refs_0_), channel_id=1, source_target_pairs={{0,1},{1,0},{2,3},{3,2},{4,5},{5,4},{6,7},{7,6},{8,9},{9,8},{10,11... | collective-permute-start | bytes 688136 | tf_op jit(solution)/shard_map/ppermute | solution.py:25
  24.2 10.0 %collective-permute-start.2 = (bf16[64,1792]{1,0:T(8,128)(2,1)S(1)}, bf16[64,1792]{1,0:T(8,128)(2,1)S(1)}, u32[]{:S(2)}, u32[]{:S(2)}) collective-permute-start(bf16[64,1792]{1,0:T(8,128)(2,1)S(1)} %get-tuple-element.65.refs_1_.refs_0_), channel_id=1, source_target_pairs={{0,2},{1,3},{2,0},{3,1},{4,6},{5,7},{6,4},{7,5},{8,10},{9,11},{10,... | collective-permute-start | bytes 688136 | tf_op jit(solution)/shard_map/ppermute | solution.py:25
  24.7 9.7 %collective-permute-start.5 = (bf16[64,1792]{1,0:T(8,128)(2,1)S(1)}, bf16[64,1792]{1,0:T(8,128)(2,1)S(1)}, u32[]{:S(2)}, u32[]{:S(2)}) collective-permute-start(bf16[64,1792]{1,0:T(8,128)(2,1)S(1)} %get-tuple-element.65.refs_1_.refs_0_), channel_id=1, source_target_pairs={{0,1},{1,0},{2,3},{3,2},{4,5},{5,4},{6,7},{7,6},{8,9},{9,8},{10,11... | collective-permute-start | bytes 688136 | tf_op jit(solution)/shard_map/ppermute | solution.py:25
  32.4 3.3 %collective-permute-start.1 = (bf16[64,1792]{1,0:T(8,128)(2,1)S(1)}, bf16[64,1792]{1,0:T(8,128)(2,1)S(1)}, u32[]{:S(2)}, u32[]{:S(2)}) collective-permute-start(bf16[64,1792]{1,0:T(8,128)(2,1)S(1)} %collective-permute-done.refs_1_.refs_2_), channel_id=1, source_target_pairs={{0,1},{1,0},{2,3},{3,2},{4,5},{5,4},{6,7},{7,6},{8,9},{9,8},{10,11... | collective-permute-start | bytes 688136 | tf_op jit(solution)/shard_map/ppermute | solution.py:25
  34.2 1.6 %collective-permute-start.4 = (bf16[64,1792]{1,0:T(8,128)(2,1)S(1)}, bf16[64,1792]{1,0:T(8,128)(2,1)S(1)}, u32[]{:S(2)}, u32[]{:S(2)}) collective-permute-start(bf16[64,1792]{1,0:T(8,128)(2,1)S(1)} %collective-permute-done.2.refs_1_.refs_2_), channel_id=1, source_target_pairs={{0,1},{1,0},{2,3},{3,2},{4,5},{5,4},{6,7},{7,6},{8,9},{9,8},{10,11... | collective-permute-start | bytes 688136 | tf_op jit(solution)/shard_map/ppermute | solution.py:25
  38.3 1.6 %collective-permute-start.6 = (bf16[64,1920]{1,0:T(8,128)(2,1)S(1)}, bf16[64,1920]{1,0:T(8,128)(2,1)S(1)}, u32[]{:S(2)}, u32[]{:S(2)}) collective-permute-start(bf16[64,1920]{1,0:T(8,128)(2,1)S(1)} %get-tuple-element.56), channel_id=1, source_target_pairs={{0,1},{1,0},{2,3},{3,2},{4,5},{5,4},{6,7},{7,6},{8,9},{9,8},{10,11... | collective-permute-start | bytes 737288 | tf_op jit(solution)/shard_map/ppermute | solution.py:25
  39.9 8.2 %collective-permute-start.7 = (bf16[64,1920]{1,0:T(8,128)(2,1)S(1)}, bf16[64,1920]{1,0:T(8,128)(2,1)S(1)}, u32[]{:S(2)}, u32[]{:S(2)}) collective-permute-start(bf16[64,1920]{1,0:T(8,128)(2,1)S(1)} %add_convert_fusion.after_ref), channel_id=1, source_target_pairs={{0,2},{1,3},{2,0},{3,1},{4,6},{5,7},{6,4},{7,5},{8,10},{9,11},{10,... | collective-permute-start | bytes 737288 | tf_op jit(solution)/shard_map/ppermute | solution.py:25
  46.7 2.1 %collective-permute-start.8 = (bf16[64,1920]{1,0:T(8,128)(2,1)S(1)}, bf16[64,1920]{1,0:T(8,128)(2,1)S(1)}, u32[]{:S(2)}, u32[]{:S(2)}) collective-permute-start(bf16[64,1920]{1,0:T(8,128)(2,1)S(1)} %get-tuple-element.60), channel_id=1, source_target_pairs={{0,1},{1,0},{2,3},{3,2},{4,5},{5,4},{6,7},{7,6},{8,9},{9,8},{10,11... | collective-permute-start | bytes 737288 | tf_op jit(solution)/shard_map/ppermute | solution.py:25
  49.6 12.4 %all-to-all-start.1 = ((bf16[8,8,1920]{2,1,0:T(8,128)(2,1)}), bf16[8,8,1920]{2,1,0:T(8,128)(2,1)S(1)}, u32[]{:S(2)}, u32[]{:S(2)}) async-start(bf16[8,8,1920]{2,1,0:T(8,128)(2,1)} %settle.1.after_ref), calls=%async_computation.1 | async-start | bytes 491520 | tf_op jit(solution)/shard_map/all_to_all | solution.py:703

commit v3 on v2

--- a/solution.py
+++ b/solution.py
@@ -462,6 +462,15 @@
                 beside[step - steps]()
 
 
+def product(left, right, out):
+    for j in range(0, right.shape[1], 256):
+        part = right[:, j:j + 256]
+        for i in range(0, left.shape[0], 128):
+            out[i:i + 128, j:j + 256] = jnp.dot(
+                left[i:i + 128], part, preferred_element_type=F32
+            ).astype(BF16)
+
+
 def places(feat, shards, block):
     me = lax.axis_index("expert") if shards > 1 else 0
 
@@ -488,7 +497,7 @@
         rel, at = source(step)
         left = lefts[rel][:, at].astype(F32).T.astype(BF16)
         for i, right in enumerate(rights):
-            stage[slot, i] = jnp.dot(left, right[...], preferred_element_type=F32).astype(BF16)
+            product(left, right, stage.at[slot, i])
 
     def copies(step, slot):
         return [
@@ -533,7 +542,7 @@
 
     def fill(step, slot):
         rel, at = source(step)
-        stage[slot] = jnp.dot(turned[...], rights[rel][:, at], preferred_element_type=F32).astype(BF16)
+        product(turned, rights[rel].at[:, at], stage.at[slot])
 
     def copies(step, slot):
         return [pltpu.make_async_copy(stage.at[slot], out_ref.at[:, place(step)], sems.at[slot])]
@@ -690,7 +699,7 @@
     last = held[max(held)] if held else cols
     wide = feat * shards
     other = sum_far(held, "expert")
-    half = feat // (2 * LANES) * LANES
+    half = max(LANES, (feat - 2 * LANES) // LANES * LANES)
     pieces = ([(1, 0, feat)] if shards > 1 else []) + [(0, 0, half)]
     grad_down, *sent, first = middle(
         hidden, d, last, wide // 8, pieces, me_ref, d_gate, d_up, cols, *weights[:2], feat

time: 63.5 us -> 63.8 us (level)
  transfers between devices with their start and end apart: 10 -> 10, of which waited for: 2 -> 3; matrix products, arithmetic and copies ran while one was open for 0% -> 0% of each run, Pallas kernels for 40% -> 40%
where the time goes in v3:
time: 63.8 us; the launch traced here: 63.5 us
  Pallas kernels  31.4 us (49%)
  blocking collectives  20.3 us (32%)
  starting transfers between devices  8.89 us (14%)
  waiting for transfers between devices  2.05 us (3%)
  between operations  0.74 us (1%)
    all_to_all x1, blocking collectives, per_device(): slots = lax.all_to_all(slots, 'dp', split_axis=0, concat_axis=0, tiled=True)  20.3 us
    pallas_call x1, Pallas kernels, outer_rows(): pl.pallas_call(functools.partial(outer_rows_kernel, block, len(lefts)), o...  8.17 us
    pallas_call x1, Pallas kernels, load_early(): pl.pallas_call(lambda after_ref, *refs: load_early_kernel(*refs), out_sha...  7.44 us
    pallas_call x1, Pallas kernels, middle(): pl.pallas_call(functools.partial(middle_kernel, block, pieces, feat), out...  5.52 us
    ppermute x9, starting transfers between devices, swap(): return lax.ppermute(value, axis, [(i, i ^ mask) for i in range(size)])  4.93 us
    all_to_all x1, starting transfers between devices, per_device(): got = lax.all_to_all(total, 'dp', split_axis=0, concat_axis=0, tiled=True)  3.96 us
    pallas_call x2, Pallas kernels, partial(): pl.pallas_call(functools.partial(kernel, rels), out_shape=[jax.ShapeDtype...  2.6 us
    pallas_call x1, Pallas kernels, late(): pl.pallas_call(functools.partial(late_kernel, rels, feat), out_shape=[jax...  2.55 us
  transfers between devices with their start and end apart: 10, of which 3 were waited for; matrix products, arithmetic and copies ran while one was open for 0% of the time, Pallas kernels for 40%

profile of v3, /device:TPU:0, one launch (start us, length us, event | category | flops | bytes accessed | tf_op | source)
XLA Modules:
  0.0 63.5 jit_solution(3136691874316763694)
XLA Ops:
  0.6 1.7 %pack.1 = (bf16[8,16,1792]{2,1,0:T(8,128)(2,1)S(1)}, bf16[64,128]{1,0:T(8,128)(2,1)S(1)}, f32[2,128]{1,0:T(2,128)S(1)}) custom-call(s32[2,128]{1,0:T(2,128)} %bitcast.20, bf16[2,128]{1,0:T(2,128)(2,1)} %bitcast.21, bf16[128,1792]{1,0:T(8,128)(2,1)} %x_hbm.1, bf16[128,1792]{1,0:T(8,128)(2,1)} %d_hbm.1), custom_call_target="tpu_custom_call" | custom-call | flops 100000000 | bytes 2000000 | tf_op jit(solution)/shard_map/pack/pallas_call | solution.py:158
  2.3 20.3 %all_to_all.10.after_ref = bf16[8,16,1792]{2,1,0:T(8,128)(2,1)S(1)} all-to-all(bf16[8,16,1792]{2,1,0:T(8,128)(2,1)S(1)} %get-tuple-element.37), channel_id=1, replica_groups=mesh['dp'=8,'expert'=4] {'dp'}, dimensions={0} | all-to-all | bytes 917504 | tf_op jit(solution)/shard_map/all_to_all | solution.py:658
  22.6 1.6 %collective-permute-start = (bf16[64,1792]{1,0:T(8,128)(2,1)S(1)}, bf16[64,1792]{1,0:T(8,128)(2,1)S(1)}, u32[]{:S(2)}, u32[]{:S(2)}) collective-permute-start(bf16[64,1792]{1,0:T(8,128)(2,1)S(1)} %get-tuple-element.66.refs_0_), channel_id=1, source_target_pairs={{0,2},{1,3},{2,0},{3,1},{4,6},{5,7},{6,4},{7,5},{8,10},{9,11},{10,... | collective-permute-start | bytes 688136 | tf_op jit(solution)/shard_map/ppermute | solution.py:25
  24.2 0.0 collective-permute-start.3
  24.2 0.5 collective-permute-start.2
  24.7 0.2 collective-permute-start.5
  25.0 7.4 %load_early.1 = (bf16[7168,512]{1,0:T(8,128)(2,1)S(1)}, bf16[7168,512]{1,0:T(8,128)(2,1)S(1)}, bf16[512,7168]{1,0:T(8,128)(2,1)S(1)}, f32[64,512]{1,0:T(8,128)S(...) custom-call(bf16[8,16,1792]{2,1,0:T(8,128)(2,1)S(1)} %all_to_all.10.after_ref, ...), custom_call_target="tpu_custom_call" | custom-call | flops 352321536 | bytes 22020096 | tf_op jit(solution)/shard_map/load_early/pallas_call | solution.py:342
  32.4 0.0 collective-permute-done.refs_1_.refs_2_
  32.4 0.3 collective-permute-start.1
  32.8 0.0 collective-permute-done.3.refs_0_.refs_1_
  32.8 1.4 %partial.2 = (f32[64,512]{1,0:T(8,128)S(1)}, f32[64,512]{1,0:T(8,128)S(1)}) custom-call(s32[1]{0:T(128)} %bitcast.2.me_ref, f32[64,512]{1,0:T(8,128)S(1)} %get-tuple-element.42.after_ref.refs_5_, bf16[7168,512]{1,0:T(8,128)(2,1)S(1)} %get-tuple-element.43.gate_ref.refs_2_, bf16[7168,512]{1,0:T(8,128)(2,1)S(1)} %get-tuple-element.44.up_ref.refs_3_, ...), custom_call_target="tpu_custom_call" | custom-call | flops 469762048 | bytes 7340032 | tf_op jit(solution)/shard_map/partial/pallas_call | solution.py:280
  34.2 0.0 collective-permute-done.2.refs_1_.refs_2_
  34.2 0.3 collective-permute-start.4
  34.5 0.0 collective-permute-done.5.refs_0_.refs_1_
  34.5 1.2 %partial.3.refs_10_ = f32[64,512]{1,0:T(8,128)S(1)} custom-call(s32[1]{0:T(128)} %bitcast.2.me_ref, f32[64,512]{1,0:T(8,128)S(1)} %get-tuple-element.51.after_ref.refs_8_, bf16[7168,512]{1,0:T(8,128)(2,1)S(1)} %get-tuple-element.43.gate_ref.refs_2_, bf16[7168,512]{1,0:T(8,128)(2,1)S(1)} %get-tuple-element.44.up_ref.refs_3_, ...), custom_call_target="tpu_custom_call" | custom-call | flops 234881024 | bytes 3670016 | tf_op jit(solution)/shard_map/partial/pallas_call | solution.py:280
  35.7 0.0 collective-permute-done.1.refs_0_.refs_3_
  35.7 0.0 collective-permute-done.4.refs_1_.refs_3_
  35.7 2.5 %late.1 = (bf16[64,512]{1,0:T(8,128)(2,1)S(1)}, bf16[64,512]{1,0:T(8,128)(2,1)S(1)}, bf16[64,512]{1,0:T(8,128)(2,1)S(1)}, bf16[64,128]{1,0:T(8,128)(2,1)S(1)}, bf16[64,1920]{1,0:T(8,128)(2,1)S(1)}) custom-call(s32[1]{0:T(128)} %bitcast.2.me_ref, bf16[64,1792]{1,0:T(8,128)(2,1)S(1)} %collective-permute-done.1.refs_0_.refs_3_, ...), custom_call_target="tpu_custom_call" | custom-call | flops 587202560 | bytes 9175040 | tf_op jit(solution)/shard_map/late/pallas_call | solution.py:399
  38.3 0.3 collective-permute-start.6
  38.6 1.2 %terms.2 = bf16[64,1920]{1,0:T(8,128)(2,1)S(1)} custom-call(s32[1]{0:T(128)} %bitcast.2.me_ref, bf16[64,128]{1,0:T(8,128)(2,1)S(1)} %get-tuple-element.53.after_ref.last_ref.cols_ref, bf16[64,128]{1,0:T(8,128)(2,1)S(1)} %get-tuple-element.53.after_ref.last_ref.cols_ref, bf16[64,512]{1,0:T(8,128)(2,1)S(1)} %get-tuple-element.54.d_gate_ref.refs_4_, ...), custom_call_target="tpu_custom_call" | custom-call | flops 1 | bytes 1 | tf_op jit(solution)/shard_map/terms/pallas_call | solution.py:434
  39.9 0.1 add_convert_fusion.after_ref
  39.9 1.6 %collective-permute-start.7 = (bf16[64,1920]{1,0:T(8,128)(2,1)S(1)}, bf16[64,1920]{1,0:T(8,128)(2,1)S(1)}, u32[]{:S(2)}, u32[]{:S(2)}) collective-permute-start(bf16[64,1920]{1,0:T(8,128)(2,1)S(1)} %add_convert_fusion.after_ref), channel_id=1, source_target_pairs={{0,2},{1,3},{2,0},{3,1},{4,6},{5,7},{6,4},{7,5},{8,10},{9,11},{10,... | collective-permute-start | bytes 737288 | tf_op jit(solution)/shard_map/ppermute | solution.py:25
  41.5 5.5 %middle.1 = (bf16[512,7168]{1,0:T(8,128)(2,1)}, bf16[64,1920]{1,0:T(8,128)(2,1)S(1)}, bf16[64,1536]{1,0:T(8,128)(2,1)S(1)}) custom-call(s32[1]{0:T(128)} %bitcast.2.me_ref, bf16[64,1920]{1,0:T(8,128)(2,1)S(1)} %add_convert_fusion.after_ref, bf16[64,512]{1,0:T(8,128)(2,1)S(1)} %get-tuple-element.57.left_ref, ...), custom_call_target="tpu_custom_call" | custom-call | flops 939524096 | bytes 7340032 | tf_op jit(solution)/shard_map/middle/pallas_call | solution.py:565
  47.0 0.1 collective-permute-start.8
  47.1 1.0 %collective-permute-done.7.after_ref.refs_3_ = bf16[64,1920]{1,0:T(8,128)(2,1)S(1)} collective-permute-done((bf16[64,1920]{1,0:T(8,128)(2,1)S(1)}, bf16[64,1920]{1,0:T(8,128)(2,1)S(1)}, u32[]{:S(2)}, u32[]{:S(2)}) %collective-permute-start.7) | collective-permute-done | bytes 245792 | tf_op jit(solution)/shard_map/ppermute | solution.py:25
  48.1 0.3 terms.3.refs_1_
  48.4 0.2 collective-permute-done.8.refs_2_
  48.6 0.8 %settle.1.after_ref = bf16[8,8,1920]{2,1,0:T(8,128)(2,1)} custom-call(bf16[64,1536]{1,0:T(8,128)(2,1)S(1)} %get-tuple-element.58.refs_0_, bf16[64,384]{1,0:T(8,128)(2,1)S(1)} %terms.3.refs_1_, bf16[64,1920]{1,0:T(8,128)(2,1)S(1)} %collective-permute-done.8.refs_2_, bf16[64,1920]{1,0:T(8,128)(2,1)S(1)} %collective-permute-done.7.after_ref.refs_3_, ...), custom_call_target="tpu_custom_call" | custom-call | bytes 1000000 | tf_op jit(solution)/shard_map/settle/pallas_call | solution.py:603
  49.4 4.0 %all-to-all-start.1 = ((bf16[8,8,1920]{2,1,0:T(8,128)(2,1)}), bf16[8,8,1920]{2,1,0:T(8,128)(2,1)S(1)}, u32[]{:S(2)}, u32[]{:S(2)}) async-start(bf16[8,8,1920]{2,1,0:T(8,128)(2,1)} %settle.1.after_ref), calls=%async_computation.1 | async-start | bytes 491520 | tf_op jit(solution)/shard_map/all_to_all | solution.py:712
  53.3 8.2 %outer_rows.1 = (bf16[7168,512]{1,0:T(8,128)(2,1)}, bf16[7168,512]{1,0:T(8,128)(2,1)}) custom-call(bf16[8,8,1920]{2,1,0:T(8,128)(2,1)} %settle.1.after_ref, bf16[64,1792]{1,0:T(8,128)(2,1)S(1)} %get-tuple-element.66.refs_0_, bf16[64,1792]{1,0:T(8,128)(2,1)S(1)} %collective-permute-done.3.refs_0_.refs_1_, ...), custom_call_target="tpu_custom_call" | custom-call | flops 939524096 | bytes 14680064 | tf_op jit(solution)/shard_map/outer_rows/pallas_call | solution.py:516
  61.5 0.8 %all-to-all-done.1 = bf16[8,8,1920]{2,1,0:T(8,128)(2,1)S(1)} async-done(((bf16[8,8,1920]{2,1,0:T(8,128)(2,1)}), bf16[8,8,1920]{2,1,0:T(8,128)(2,1)S(1)}, u32[]{:S(2)}, u32[]{:S(2)}) %all-to-all-start.1) | async-done | bytes 245792 | tf_op jit(solution)/shard_map/all_to_all | solution.py:712
  62.3 1.2 %combine.1 = (bf16[128,1792]{1,0:T(8,128)(2,1)}, f32[2,128]{1,0:T(2,128)}) custom-call(bf16[64,128]{1,0:T(8,128)(2,1)S(1)} %get-tuple-element.35.pick_ref, f32[2,128]{1,0:T(2,128)S(1)} %get-tuple-element.36.gates_ref, bf16[64,1920]{1,0:T(8,128)(2,1)S(1)} %bitcast.15), custom_call_target="tpu_custom_call" | custom-call | flops 100000000 | bytes 1000000 | tf_op jit(solution)/shard_map/combine/pallas_call | solution.py:631
  (2 shorter events, 0.0 us)
Async XLA Ops:
  22.6 9.8 %collective-permute-start = (bf16[64,1792]{1,0:T(8,128)(2,1)S(1)}, bf16[64,1792]{1,0:T(8,128)(2,1)S(1)}, u32[]{:S(2)}, u32[]{:S(2)}) collective-permute-start(bf16[64,1792]{1,0:T(8,128)(2,1)S(1)} %get-tuple-element.66.refs_0_), channel_id=1, source_target_pairs={{0,2},{1,3},{2,0},{3,1},{4,6},{5,7},{6,4},{7,5},{8,10},{9,11},{10,... | collective-permute-start | bytes 688136 | tf_op jit(solution)/shard_map/ppermute | solution.py:25
  24.2 8.6 %collective-permute-start.3 = (bf16[64,1792]{1,0:T(8,128)(2,1)S(1)}, bf16[64,1792]{1,0:T(8,128)(2,1)S(1)}, u32[]{:S(2)}, u32[]{:S(2)}) collective-permute-start(bf16[64,1792]{1,0:T(8,128)(2,1)S(1)} %get-tuple-element.66.refs_0_), channel_id=1, source_target_pairs={{0,1},{1,0},{2,3},{3,2},{4,5},{5,4},{6,7},{7,6},{8,9},{9,8},{10,11... | collective-permute-start | bytes 688136 | tf_op jit(solution)/shard_map/ppermute | solution.py:25
  24.2 10.0 %collective-permute-start.2 = (bf16[64,1792]{1,0:T(8,128)(2,1)S(1)}, bf16[64,1792]{1,0:T(8,128)(2,1)S(1)}, u32[]{:S(2)}, u32[]{:S(2)}) collective-permute-start(bf16[64,1792]{1,0:T(8,128)(2,1)S(1)} %get-tuple-element.65.refs_1_.refs_0_), channel_id=1, source_target_pairs={{0,2},{1,3},{2,0},{3,1},{4,6},{5,7},{6,4},{7,5},{8,10},{9,11},{10,... | collective-permute-start | bytes 688136 | tf_op jit(solution)/shard_map/ppermute | solution.py:25
  24.7 9.7 %collective-permute-start.5 = (bf16[64,1792]{1,0:T(8,128)(2,1)S(1)}, bf16[64,1792]{1,0:T(8,128)(2,1)S(1)}, u32[]{:S(2)}, u32[]{:S(2)}) collective-permute-start(bf16[64,1792]{1,0:T(8,128)(2,1)S(1)} %get-tuple-element.65.refs_1_.refs_0_), channel_id=1, source_target_pairs={{0,1},{1,0},{2,3},{3,2},{4,5},{5,4},{6,7},{7,6},{8,9},{9,8},{10,11... | collective-permute-start | bytes 688136 | tf_op jit(solution)/shard_map/ppermute | solution.py:25
  32.4 3.3 %collective-permute-start.1 = (bf16[64,1792]{1,0:T(8,128)(2,1)S(1)}, bf16[64,1792]{1,0:T(8,128)(2,1)S(1)}, u32[]{:S(2)}, u32[]{:S(2)}) collective-permute-start(bf16[64,1792]{1,0:T(8,128)(2,1)S(1)} %collective-permute-done.refs_1_.refs_2_), channel_id=1, source_target_pairs={{0,1},{1,0},{2,3},{3,2},{4,5},{5,4},{6,7},{7,6},{8,9},{9,8},{10,11... | collective-permute-start | bytes 688136 | tf_op jit(solution)/shard_map/ppermute | solution.py:25
  34.2 1.6 %collective-permute-start.4 = (bf16[64,1792]{1,0:T(8,128)(2,1)S(1)}, bf16[64,1792]{1,0:T(8,128)(2,1)S(1)}, u32[]{:S(2)}, u32[]{:S(2)}) collective-permute-start(bf16[64,1792]{1,0:T(8,128)(2,1)S(1)} %collective-permute-done.2.refs_1_.refs_2_), channel_id=1, source_target_pairs={{0,1},{1,0},{2,3},{3,2},{4,5},{5,4},{6,7},{7,6},{8,9},{9,8},{10,11... | collective-permute-start | bytes 688136 | tf_op jit(solution)/shard_map/ppermute | solution.py:25
  38.3 1.6 %collective-permute-start.6 = (bf16[64,1920]{1,0:T(8,128)(2,1)S(1)}, bf16[64,1920]{1,0:T(8,128)(2,1)S(1)}, u32[]{:S(2)}, u32[]{:S(2)}) collective-permute-start(bf16[64,1920]{1,0:T(8,128)(2,1)S(1)} %get-tuple-element.56), channel_id=1, source_target_pairs={{0,1},{1,0},{2,3},{3,2},{4,5},{5,4},{6,7},{7,6},{8,9},{9,8},{10,11... | collective-permute-start | bytes 737288 | tf_op jit(solution)/shard_map/ppermute | solution.py:25
  39.9 8.2 %collective-permute-start.7 = (bf16[64,1920]{1,0:T(8,128)(2,1)S(1)}, bf16[64,1920]{1,0:T(8,128)(2,1)S(1)}, u32[]{:S(2)}, u32[]{:S(2)}) collective-permute-start(bf16[64,1920]{1,0:T(8,128)(2,1)S(1)} %add_convert_fusion.after_ref), channel_id=1, source_target_pairs={{0,2},{1,3},{2,0},{3,1},{4,6},{5,7},{6,4},{7,5},{8,10},{9,11},{10,... | collective-permute-start | bytes 737288 | tf_op jit(solution)/shard_map/ppermute | solution.py:25
  47.0 1.6 %collective-permute-start.8 = (bf16[64,1920]{1,0:T(8,128)(2,1)S(1)}, bf16[64,1920]{1,0:T(8,128)(2,1)S(1)}, u32[]{:S(2)}, u32[]{:S(2)}) collective-permute-start(bf16[64,1920]{1,0:T(8,128)(2,1)S(1)} %get-tuple-element.60), channel_id=1, source_target_pairs={{0,1},{1,0},{2,3},{3,2},{4,5},{5,4},{6,7},{7,6},{8,9},{9,8},{10,11... | collective-permute-start | bytes 737288 | tf_op jit(solution)/shard_map/ppermute | solution.py:25
  49.4 12.9 %all-to-all-start.1 = ((bf16[8,8,1920]{2,1,0:T(8,128)(2,1)}), bf16[8,8,1920]{2,1,0:T(8,128)(2,1)S(1)}, u32[]{:S(2)}, u32[]{:S(2)}) async-start(bf16[8,8,1920]{2,1,0:T(8,128)(2,1)} %settle.1.after_ref), calls=%async_computation.1 | async-start | bytes 491520 | tf_op jit(solution)/shard_map/all_to_all | solution.py:712

commit v4 on v2

--- a/solution.py
+++ b/solution.py
@@ -92,8 +92,25 @@
     return jnp.where(pick, 1.0, 0.0), jnp.where(pick, gate, 0.0)
 
 
-def row_blocks(experts, tokens):
-    return lax.broadcasted_iota(jnp.int32, (experts * CAP, tokens), 0) // CAP
+def owner_order(experts):
+    places = experts // 2
+    near = sorted(range(places), key=lambda place: abs(2 * place - places + 1))
+    return [2 * place + last for place in near for last in range(2)]
+
+
+def row_owners(experts, tokens):
+    block = lax.broadcasted_iota(jnp.int32, (experts * CAP, tokens), 0) // CAP
+    owner = jnp.zeros_like(block)
+    for i, expert in enumerate(owner_order(experts)):
+        owner = jnp.where(block == i, expert, owner)
+    return owner
+
+
+def exchange(blocks, axis):
+    groups = [owner_order(lax.axis_size(axis))]
+    return lax.all_to_all(
+        blocks, axis, split_axis=0, concat_axis=0, axis_index_groups=groups, tiled=True
+    )
 
 
 def column_block(feat):
@@ -131,7 +148,7 @@
     for copy in small:
         copy.wait()
     gates = gates_low[...].astype(F32)
-    pick, pick_gate = one_hot(ids[...], gates, row_blocks(experts, ids.shape[1]), experts)
+    pick, pick_gate = one_hot(ids[...], gates, row_owners(experts, ids.shape[1]), experts)
     pick, pick_gate = pick.astype(BF16), pick_gate.astype(BF16)
     for step in range(steps):
         for copy in loads[step]:
@@ -610,10 +627,12 @@
 
     @pl.when(pl.program_id(0) == 0)
     def _():
-        half = pick.shape[0] // 2
+        rows, count = pick.shape
+        experts = rows // CAP
         terms = pick.astype(F32) * rows_ref[:, feat:].astype(F32)
-        gate_ref[0:1, :] = jnp.sum(terms[:half], axis=0, keepdims=True) / gates_ref[0:1, :]
-        gate_ref[1:2, :] = jnp.sum(terms[half:], axis=0, keepdims=True) / gates_ref[1:2, :]
+        low = row_owners(experts, count) < experts // 2
+        for i, part in enumerate((jnp.where(low, terms, 0.0), jnp.where(low, 0.0, terms))):
+            gate_ref[i:i + 1, :] = jnp.sum(part, axis=0, keepdims=True) / gates_ref[i:i + 1, :]
 
 
 def combine(pick, gates, rows, feat):
@@ -646,7 +665,7 @@
     gates_t = gates.T
     me_ref = me.reshape(1)
     slots, pick, gates_f = pack(ids_t, gates_t, tokens, cotangent, experts)
-    slots = lax.all_to_all(slots, "dp", split_axis=0, concat_axis=0, tiled=True)
+    slots = exchange(slots, "dp")
     x = gather_far(slots[:, :CAP].reshape(rows, feat), "expert")
     d = gather_far(slots[:, CAP:].reshape(rows, feat), "expert")
     weights = [w_gate[0], w_up[0], w_down[0]]
@@ -690,7 +709,7 @@
     last = held[max(held)] if held else cols
     wide = feat * shards
     other = sum_far(held, "expert")
-    half = feat // (2 * LANES) * LANES
+    half = max(LANES, (feat - 2 * LANES) // LANES * LANES)
     pieces = ([(1, 0, feat)] if shards > 1 else []) + [(0, 0, half)]
     grad_down, *sent, first = middle(
         hidden, d, last, wide // 8, pieces, me_ref, d_gate, d_up, cols, *weights[:2], feat
@@ -700,7 +719,7 @@
     parts += [] if other is None else [other]
     second, = term([(0, half, feat)], (keep(parts[-1] if parts else cols), down_done))
     total = settle([first, second], parts, grad_down)
-    got = lax.all_to_all(total, "dp", split_axis=0, concat_axis=0, tiled=True)
+    got = exchange(total, "dp")
     got = got.reshape(rows, feat + LANES)
     grad_gate, grad_up = outer_rows(x, (d_gate, d_up), total, wide // 16)
     grad_tokens, gate_grads = combine(pick, gates_f, got, feat)

time: 63.5 us -> 62.6 us (0.986)
  no operation moved by 1% of the time
where the time goes in v4:
time: 62.6 us; the launch traced here: 62.3 us
  Pallas kernels  31.1 us (50%)
  blocking collectives  20.2 us (32%)
  starting transfers between devices  8.56 us (14%)
  waiting for transfers between devices  1.6 us (3%)
  between operations  0.74 us (1%)
    all_to_all x1, blocking collectives, exchange(): lax.all_to_all(blocks, axis, split_axis=0, concat_axis=0, axis_index_grou...  20.2 us
    pallas_call x1, Pallas kernels, outer_rows(): pl.pallas_call(functools.partial(outer_rows_kernel, block, len(lefts)), o...  8.16 us
    pallas_call x1, Pallas kernels, load_early(): pl.pallas_call(lambda after_ref, *refs: load_early_kernel(*refs), out_sha...  7.44 us
    pallas_call x1, Pallas kernels, middle(): pl.pallas_call(functools.partial(middle_kernel, block, pieces, feat), out...  5.23 us
    ppermute x9, starting transfers between devices, swap(): return lax.ppermute(value, axis, [(i, i ^ mask) for i in range(size)])  4.93 us
    all_to_all x1, starting transfers between devices, exchange(): lax.all_to_all(blocks, axis, split_axis=0, concat_axis=0, axis_index_grou...  3.63 us
    pallas_call x2, Pallas kernels, partial(): pl.pallas_call(functools.partial(kernel, rels), out_shape=[jax.ShapeDtype...  2.6 us
    pallas_call x1, Pallas kernels, late(): pl.pallas_call(functools.partial(late_kernel, rels, feat), out_shape=[jax...  2.55 us
  transfers between devices with their start and end apart: 10, of which 2 were waited for; matrix products, arithmetic and copies ran while one was open for 0% of the time, Pallas kernels for 40%

profile of v4, /device:TPU:0, one launch (start us, length us, event | category | flops | bytes accessed | tf_op | source)
XLA Modules:
  0.0 62.3 jit_solution(10437014917359430176)
XLA Ops:
  0.6 1.7 %pack.1 = (bf16[8,16,1792]{2,1,0:T(8,128)(2,1)S(1)}, bf16[64,128]{1,0:T(8,128)(2,1)S(1)}, f32[2,128]{1,0:T(2,128)S(1)}) custom-call(s32[2,128]{1,0:T(2,128)} %bitcast.20, bf16[2,128]{1,0:T(2,128)(2,1)} %bitcast.21, bf16[128,1792]{1,0:T(8,128)(2,1)} %x_hbm.1, bf16[128,1792]{1,0:T(8,128)(2,1)} %d_hbm.1), custom_call_target="tpu_custom_call" | custom-call | flops 100000000 | bytes 2000000 | tf_op jit(solution)/shard_map/pack/pallas_call | solution.py:175
  2.3 20.2 %all_to_all.10.after_ref = bf16[8,16,1792]{2,1,0:T(8,128)(2,1)S(1)} all-to-all(bf16[8,16,1792]{2,1,0:T(8,128)(2,1)S(1)} %get-tuple-element.37), channel_id=1, replica_groups={{8,12,16,20,0,4,24,28},{9,13,17,21,1,5,25,29},{10,14,18,22,2,6,26,30},{..., dimensions={0} | all-to-all | bytes 917504 | tf_op jit(solution)/shard_map/all_to_all | solution.py:111
  22.5 1.6 %collective-permute-start = (bf16[64,1792]{1,0:T(8,128)(2,1)S(1)}, bf16[64,1792]{1,0:T(8,128)(2,1)S(1)}, u32[]{:S(2)}, u32[]{:S(2)}) collective-permute-start(bf16[64,1792]{1,0:T(8,128)(2,1)S(1)} %get-tuple-element.66.refs_0_), channel_id=1, source_target_pairs={{0,2},{1,3},{2,0},{3,1},{4,6},{5,7},{6,4},{7,5},{8,10},{9,11},{10,... | collective-permute-start | bytes 688136 | tf_op jit(solution)/shard_map/ppermute | solution.py:25
  24.0 0.0 collective-permute-start.3
  24.1 0.5 collective-permute-start.2
  24.6 0.2 collective-permute-start.5
  24.8 7.4 %load_early.1 = (bf16[7168,512]{1,0:T(8,128)(2,1)S(1)}, bf16[7168,512]{1,0:T(8,128)(2,1)S(1)}, bf16[512,7168]{1,0:T(8,128)(2,1)S(1)}, f32[64,512]{1,0:T(8,128)S(...) custom-call(bf16[8,16,1792]{2,1,0:T(8,128)(2,1)S(1)} %all_to_all.10.after_ref, ...), custom_call_target="tpu_custom_call" | custom-call | flops 352321536 | bytes 22020096 | tf_op jit(solution)/shard_map/load_early/pallas_call | solution.py:359
  32.3 0.0 collective-permute-done.refs_1_.refs_2_
  32.3 0.3 collective-permute-start.1
  32.6 0.0 collective-permute-done.3.refs_0_.refs_1_
  32.6 1.4 %partial.2 = (f32[64,512]{1,0:T(8,128)S(1)}, f32[64,512]{1,0:T(8,128)S(1)}) custom-call(s32[1]{0:T(128)} %bitcast.2.me_ref, f32[64,512]{1,0:T(8,128)S(1)} %get-tuple-element.42.after_ref.refs_5_, bf16[7168,512]{1,0:T(8,128)(2,1)S(1)} %get-tuple-element.43.gate_ref.refs_2_, bf16[7168,512]{1,0:T(8,128)(2,1)S(1)} %get-tuple-element.44.up_ref.refs_3_, ...), custom_call_target="tpu_custom_call" | custom-call | flops 469762048 | bytes 7340032 | tf_op jit(solution)/shard_map/partial/pallas_call | solution.py:297
  34.0 0.0 collective-permute-done.2.refs_1_.refs_2_
  34.0 0.3 collective-permute-start.4
  34.3 0.0 collective-permute-done.5.refs_0_.refs_1_
  34.3 1.2 %partial.3.refs_10_ = f32[64,512]{1,0:T(8,128)S(1)} custom-call(s32[1]{0:T(128)} %bitcast.2.me_ref, f32[64,512]{1,0:T(8,128)S(1)} %get-tuple-element.51.after_ref.refs_8_, bf16[7168,512]{1,0:T(8,128)(2,1)S(1)} %get-tuple-element.43.gate_ref.refs_2_, bf16[7168,512]{1,0:T(8,128)(2,1)S(1)} %get-tuple-element.44.up_ref.refs_3_, ...), custom_call_target="tpu_custom_call" | custom-call | flops 234881024 | bytes 3670016 | tf_op jit(solution)/shard_map/partial/pallas_call | solution.py:297
  35.5 0.0 collective-permute-done.1.refs_0_.refs_3_
  35.6 0.0 collective-permute-done.4.refs_1_.refs_3_
  35.6 2.6 %late.1 = (bf16[64,512]{1,0:T(8,128)(2,1)S(1)}, bf16[64,512]{1,0:T(8,128)(2,1)S(1)}, bf16[64,512]{1,0:T(8,128)(2,1)S(1)}, bf16[64,128]{1,0:T(8,128)(2,1)S(1)}, bf16[64,1920]{1,0:T(8,128)(2,1)S(1)}) custom-call(s32[1]{0:T(128)} %bitcast.2.me_ref, bf16[64,1792]{1,0:T(8,128)(2,1)S(1)} %collective-permute-done.1.refs_0_.refs_3_, ...), custom_call_target="tpu_custom_call" | custom-call | flops 587202560 | bytes 9175040 | tf_op jit(solution)/shard_map/late/pallas_call | solution.py:416
  38.1 0.3 collective-permute-start.6
  38.5 1.2 %terms.2 = bf16[64,1920]{1,0:T(8,128)(2,1)S(1)} custom-call(s32[1]{0:T(128)} %bitcast.2.me_ref, bf16[64,128]{1,0:T(8,128)(2,1)S(1)} %get-tuple-element.53.after_ref.last_ref.cols_ref, bf16[64,128]{1,0:T(8,128)(2,1)S(1)} %get-tuple-element.53.after_ref.last_ref.cols_ref, bf16[64,512]{1,0:T(8,128)(2,1)S(1)} %get-tuple-element.54.d_gate_ref.refs_4_, ...), custom_call_target="tpu_custom_call" | custom-call | flops 1 | bytes 1 | tf_op jit(solution)/shard_map/terms/pallas_call | solution.py:451
  39.7 0.0 collective-permute-done.6
  39.7 0.1 add_convert_fusion.after_ref
  39.8 1.6 %collective-permute-start.7 = (bf16[64,1920]{1,0:T(8,128)(2,1)S(1)}, bf16[64,1920]{1,0:T(8,128)(2,1)S(1)}, u32[]{:S(2)}, u32[]{:S(2)}) collective-permute-start(bf16[64,1920]{1,0:T(8,128)(2,1)S(1)} %add_convert_fusion.after_ref), channel_id=1, source_target_pairs={{0,2},{1,3},{2,0},{3,1},{4,6},{5,7},{6,4},{7,5},{8,10},{9,11},{10,... | collective-permute-start | bytes 737288 | tf_op jit(solution)/shard_map/ppermute | solution.py:25
  41.3 5.2 %middle.1 = (bf16[512,7168]{1,0:T(8,128)(2,1)}, bf16[64,1920]{1,0:T(8,128)(2,1)S(1)}, bf16[64,1536]{1,0:T(8,128)(2,1)S(1)}) custom-call(s32[1]{0:T(128)} %bitcast.2.me_ref, bf16[64,1920]{1,0:T(8,128)(2,1)S(1)} %add_convert_fusion.after_ref, bf16[64,512]{1,0:T(8,128)(2,1)S(1)} %get-tuple-element.57.left_ref, ...), custom_call_target="tpu_custom_call" | custom-call | flops 939524096 | bytes 7340032 | tf_op jit(solution)/shard_map/middle/pallas_call | solution.py:573
  46.6 0.1 collective-permute-start.8
  46.6 1.3 %collective-permute-done.7.after_ref.refs_3_ = bf16[64,1920]{1,0:T(8,128)(2,1)S(1)} collective-permute-done((bf16[64,1920]{1,0:T(8,128)(2,1)S(1)}, bf16[64,1920]{1,0:T(8,128)(2,1)S(1)}, u32[]{:S(2)}, u32[]{:S(2)}) %collective-permute-start.7) | collective-permute-done | bytes 245792 | tf_op jit(solution)/shard_map/ppermute | solution.py:25
  48.0 0.3 terms.3.refs_1_
  48.3 0.8 %settle.1.after_ref = bf16[8,8,1920]{2,1,0:T(8,128)(2,1)} custom-call(bf16[64,1536]{1,0:T(8,128)(2,1)S(1)} %get-tuple-element.58.refs_0_, bf16[64,384]{1,0:T(8,128)(2,1)S(1)} %terms.3.refs_1_, bf16[64,1920]{1,0:T(8,128)(2,1)S(1)} %collective-permute-done.8.refs_2_, bf16[64,1920]{1,0:T(8,128)(2,1)S(1)} %collective-permute-done.7.after_ref.refs_3_, ...), custom_call_target="tpu_custom_call" | custom-call | bytes 1000000 | tf_op jit(solution)/shard_map/settle/pallas_call | solution.py:611
  49.1 3.6 %all-to-all-start.1 = ((bf16[8,8,1920]{2,1,0:T(8,128)(2,1)}), bf16[8,8,1920]{2,1,0:T(8,128)(2,1)S(1)}, u32[]{:S(2)}, u32[]{:S(2)}) async-start(bf16[8,8,1920]{2,1,0:T(8,128)(2,1)} %settle.1.after_ref), calls=%async_computation.1 | async-start | bytes 491520 | tf_op jit(solution)/shard_map/all_to_all | solution.py:111
  52.7 8.2 %outer_rows.1 = (bf16[7168,512]{1,0:T(8,128)(2,1)}, bf16[7168,512]{1,0:T(8,128)(2,1)}) custom-call(bf16[8,8,1920]{2,1,0:T(8,128)(2,1)} %settle.1.after_ref, bf16[64,1792]{1,0:T(8,128)(2,1)S(1)} %get-tuple-element.66.refs_0_, bf16[64,1792]{1,0:T(8,128)(2,1)S(1)} %collective-permute-done.3.refs_0_.refs_1_, ...), custom_call_target="tpu_custom_call" | custom-call | flops 939524096 | bytes 14680064 | tf_op jit(solution)/shard_map/outer_rows/pallas_call | solution.py:524
  60.9 0.2 all-to-all-done.1
  61.1 1.2 %combine.1 = (bf16[128,1792]{1,0:T(8,128)(2,1)}, f32[2,128]{1,0:T(2,128)}) custom-call(bf16[64,128]{1,0:T(8,128)(2,1)S(1)} %get-tuple-element.35.pick_ref, f32[2,128]{1,0:T(2,128)S(1)} %get-tuple-element.36.gates_ref, bf16[64,1920]{1,0:T(8,128)(2,1)S(1)} %bitcast.15), custom_call_target="tpu_custom_call" | custom-call | flops 100000000 | bytes 1000000 | tf_op jit(solution)/shard_map/combine/pallas_call | solution.py:641
  (2 shorter events, 0.0 us)
Async XLA Ops:
  22.5 9.8 %collective-permute-start = (bf16[64,1792]{1,0:T(8,128)(2,1)S(1)}, bf16[64,1792]{1,0:T(8,128)(2,1)S(1)}, u32[]{:S(2)}, u32[]{:S(2)}) collective-permute-start(bf16[64,1792]{1,0:T(8,128)(2,1)S(1)} %get-tuple-element.66.refs_0_), channel_id=1, source_target_pairs={{0,2},{1,3},{2,0},{3,1},{4,6},{5,7},{6,4},{7,5},{8,10},{9,11},{10,... | collective-permute-start | bytes 688136 | tf_op jit(solution)/shard_map/ppermute | solution.py:25
  24.0 8.6 %collective-permute-start.3 = (bf16[64,1792]{1,0:T(8,128)(2,1)S(1)}, bf16[64,1792]{1,0:T(8,128)(2,1)S(1)}, u32[]{:S(2)}, u32[]{:S(2)}) collective-permute-start(bf16[64,1792]{1,0:T(8,128)(2,1)S(1)} %get-tuple-element.66.refs_0_), channel_id=1, source_target_pairs={{0,1},{1,0},{2,3},{3,2},{4,5},{5,4},{6,7},{7,6},{8,9},{9,8},{10,11... | collective-permute-start | bytes 688136 | tf_op jit(solution)/shard_map/ppermute | solution.py:25
  24.1 10.0 %collective-permute-start.2 = (bf16[64,1792]{1,0:T(8,128)(2,1)S(1)}, bf16[64,1792]{1,0:T(8,128)(2,1)S(1)}, u32[]{:S(2)}, u32[]{:S(2)}) collective-permute-start(bf16[64,1792]{1,0:T(8,128)(2,1)S(1)} %get-tuple-element.65.refs_1_.refs_0_), channel_id=1, source_target_pairs={{0,2},{1,3},{2,0},{3,1},{4,6},{5,7},{6,4},{7,5},{8,10},{9,11},{10,... | collective-permute-start | bytes 688136 | tf_op jit(solution)/shard_map/ppermute | solution.py:25
  24.6 9.7 %collective-permute-start.5 = (bf16[64,1792]{1,0:T(8,128)(2,1)S(1)}, bf16[64,1792]{1,0:T(8,128)(2,1)S(1)}, u32[]{:S(2)}, u32[]{:S(2)}) collective-permute-start(bf16[64,1792]{1,0:T(8,128)(2,1)S(1)} %get-tuple-element.65.refs_1_.refs_0_), channel_id=1, source_target_pairs={{0,1},{1,0},{2,3},{3,2},{4,5},{5,4},{6,7},{7,6},{8,9},{9,8},{10,11... | collective-permute-start | bytes 688136 | tf_op jit(solution)/shard_map/ppermute | solution.py:25
  32.3 3.3 %collective-permute-start.1 = (bf16[64,1792]{1,0:T(8,128)(2,1)S(1)}, bf16[64,1792]{1,0:T(8,128)(2,1)S(1)}, u32[]{:S(2)}, u32[]{:S(2)}) collective-permute-start(bf16[64,1792]{1,0:T(8,128)(2,1)S(1)} %collective-permute-done.refs_1_.refs_2_), channel_id=1, source_target_pairs={{0,1},{1,0},{2,3},{3,2},{4,5},{5,4},{6,7},{7,6},{8,9},{9,8},{10,11... | collective-permute-start | bytes 688136 | tf_op jit(solution)/shard_map/ppermute | solution.py:25
  34.0 1.6 %collective-permute-start.4 = (bf16[64,1792]{1,0:T(8,128)(2,1)S(1)}, bf16[64,1792]{1,0:T(8,128)(2,1)S(1)}, u32[]{:S(2)}, u32[]{:S(2)}) collective-permute-start(bf16[64,1792]{1,0:T(8,128)(2,1)S(1)} %collective-permute-done.2.refs_1_.refs_2_), channel_id=1, source_target_pairs={{0,1},{1,0},{2,3},{3,2},{4,5},{5,4},{6,7},{7,6},{8,9},{9,8},{10,11... | collective-permute-start | bytes 688136 | tf_op jit(solution)/shard_map/ppermute | solution.py:25
  38.1 1.6 %collective-permute-start.6 = (bf16[64,1920]{1,0:T(8,128)(2,1)S(1)}, bf16[64,1920]{1,0:T(8,128)(2,1)S(1)}, u32[]{:S(2)}, u32[]{:S(2)}) collective-permute-start(bf16[64,1920]{1,0:T(8,128)(2,1)S(1)} %get-tuple-element.56), channel_id=1, source_target_pairs={{0,1},{1,0},{2,3},{3,2},{4,5},{5,4},{6,7},{7,6},{8,9},{9,8},{10,11... | collective-permute-start | bytes 737288 | tf_op jit(solution)/shard_map/ppermute | solution.py:25
  39.8 8.2 %collective-permute-start.7 = (bf16[64,1920]{1,0:T(8,128)(2,1)S(1)}, bf16[64,1920]{1,0:T(8,128)(2,1)S(1)}, u32[]{:S(2)}, u32[]{:S(2)}) collective-permute-start(bf16[64,1920]{1,0:T(8,128)(2,1)S(1)} %add_convert_fusion.after_ref), channel_id=1, source_target_pairs={{0,2},{1,3},{2,0},{3,1},{4,6},{5,7},{6,4},{7,5},{8,10},{9,11},{10,... | collective-permute-start | bytes 737288 | tf_op jit(solution)/shard_map/ppermute | solution.py:25
  46.6 1.7 %collective-permute-start.8 = (bf16[64,1920]{1,0:T(8,128)(2,1)S(1)}, bf16[64,1920]{1,0:T(8,128)(2,1)S(1)}, u32[]{:S(2)}, u32[]{:S(2)}) collective-permute-start(bf16[64,1920]{1,0:T(8,128)(2,1)S(1)} %get-tuple-element.60), channel_id=1, source_target_pairs={{0,1},{1,0},{2,3},{3,2},{4,5},{5,4},{6,7},{7,6},{8,9},{9,8},{10,11... | collective-permute-start | bytes 737288 | tf_op jit(solution)/shard_map/ppermute | solution.py:25
  49.1 12.0 %all-to-all-start.1 = ((bf16[8,8,1920]{2,1,0:T(8,128)(2,1)}), bf16[8,8,1920]{2,1,0:T(8,128)(2,1)S(1)}, u32[]{:S(2)}, u32[]{:S(2)}) async-start(bf16[8,8,1920]{2,1,0:T(8,128)(2,1)} %settle.1.after_ref), calls=%async_computation.1 | async-start | bytes 491520 | tf_op jit(solution)/shard_map/all_to_all | solution.py:111

commit v5 on v4

--- a/solution.py
+++ b/solution.py
@@ -94,8 +94,8 @@
 
 def owner_order(experts):
     places = experts // 2
-    near = sorted(range(places), key=lambda place: abs(2 * place - places + 1))
-    return [2 * place + last for place in near for last in range(2)]
+    near = sorted(range(places), key=lambda place: (abs(2 * place - places + 1), -place))
+    return [2 * place + last for place in near for last in (1, 0)]
 
 
 def row_owners(experts, tokens):

time: 62.6 us -> 62.4 us (level)
  starting transfers between devices: 8.56 us -> 11.2 us
  blocking collectives: 20.2 us -> 17.6 us
    all_to_all x1, starting transfers between devices: 3.63 us -> 6.25 us  [exchange(): lax.all_to_all(blocks, axis, split_axis=0, concat_axis=0, axis_index_grou...]
    all_to_all x1, blocking collectives: 20.2 us -> 17.6 us  [exchange(): lax.all_to_all(blocks, axis, split_axis=0, concat_axis=0, axis_index_grou...]
  transfers between devices with their start and end apart: 10 -> 10, of which waited for: 2 -> 1; matrix products, arithmetic and copies ran while one was open for 0% -> 0% of each run, Pallas kernels for 40% -> 40%
where the time goes in v5:
time: 62.4 us; the launch traced here: 62.1 us
  Pallas kernels  31.1 us (50%)
  blocking collectives  17.6 us (28%)
  starting transfers between devices  11.2 us (18%)
  waiting for transfers between devices  1.37 us (2%)
  between operations  0.75 us (1%)
    all_to_all x1, blocking collectives, exchange(): lax.all_to_all(blocks, axis, split_axis=0, concat_axis=0, axis_index_grou...  17.6 us
    pallas_call x1, Pallas kernels, outer_rows(): pl.pallas_call(functools.partial(outer_rows_kernel, block, len(lefts)), o...  8.15 us
    pallas_call x1, Pallas kernels, load_early(): pl.pallas_call(lambda after_ref, *refs: load_early_kernel(*refs), out_sha...  7.44 us
    all_to_all x1, starting transfers between devices, exchange(): lax.all_to_all(blocks, axis, split_axis=0, concat_axis=0, axis_index_grou...  6.25 us
    pallas_call x1, Pallas kernels, middle(): pl.pallas_call(functools.partial(middle_kernel, block, pieces, feat), out...  5.22 us
    ppermute x9, starting transfers between devices, swap(): return lax.ppermute(value, axis, [(i, i ^ mask) for i in range(size)])  4.94 us
    pallas_call x2, Pallas kernels, partial(): pl.pallas_call(functools.partial(kernel, rels), out_shape=[jax.ShapeDtype...  2.59 us
    pallas_call x1, Pallas kernels, late(): pl.pallas_call(functools.partial(late_kernel, rels, feat), out_shape=[jax...  2.55 us
  transfers between devices with their start and end apart: 10, of which 1 were waited for; matrix products, arithmetic and copies ran while one was open for 0% of the time, Pallas kernels for 40%

profile of v5, /device:TPU:0, one launch (start us, length us, event | category | flops | bytes accessed | tf_op | source)
XLA Modules:
  0.0 62.1 jit_solution(15169735600216040847)
XLA Ops:
  0.6 1.7 %pack.1 = (bf16[8,16,1792]{2,1,0:T(8,128)(2,1)S(1)}, bf16[64,128]{1,0:T(8,128)(2,1)S(1)}, f32[2,128]{1,0:T(2,128)S(1)}) custom-call(s32[2,128]{1,0:T(2,128)} %bitcast.20, bf16[2,128]{1,0:T(2,128)(2,1)} %bitcast.21, bf16[128,1792]{1,0:T(8,128)(2,1)} %x_hbm.1, bf16[128,1792]{1,0:T(8,128)(2,1)} %d_hbm.1), custom_call_target="tpu_custom_call" | custom-call | flops 100000000 | bytes 2000000 | tf_op jit(solution)/shard_map/pack/pallas_call | solution.py:175
  2.3 17.6 %all_to_all.10.after_ref = bf16[8,16,1792]{2,1,0:T(8,128)(2,1)S(1)} all-to-all(bf16[8,16,1792]{2,1,0:T(8,128)(2,1)S(1)} %get-tuple-element.37), channel_id=1, replica_groups={{20,16,12,8,28,24,4,0},{21,17,13,9,29,25,5,1},{22,18,14,10,30,26,6,2},{..., dimensions={0} | all-to-all | bytes 917504 | tf_op jit(solution)/shard_map/all_to_all | solution.py:111
  19.9 1.6 %collective-permute-start = (bf16[64,1792]{1,0:T(8,128)(2,1)S(1)}, bf16[64,1792]{1,0:T(8,128)(2,1)S(1)}, u32[]{:S(2)}, u32[]{:S(2)}) collective-permute-start(bf16[64,1792]{1,0:T(8,128)(2,1)S(1)} %get-tuple-element.66.refs_0_), channel_id=1, source_target_pairs={{0,2},{1,3},{2,0},{3,1},{4,6},{5,7},{6,4},{7,5},{8,10},{9,11},{10,... | collective-permute-start | bytes 688136 | tf_op jit(solution)/shard_map/ppermute | solution.py:25
  21.5 0.0 collective-permute-start.3
  21.5 0.5 collective-permute-start.2
  22.0 0.2 collective-permute-start.5
  22.2 7.4 %load_early.1 = (bf16[7168,512]{1,0:T(8,128)(2,1)S(1)}, bf16[7168,512]{1,0:T(8,128)(2,1)S(1)}, bf16[512,7168]{1,0:T(8,128)(2,1)S(1)}, f32[64,512]{1,0:T(8,128)S(...) custom-call(bf16[8,16,1792]{2,1,0:T(8,128)(2,1)S(1)} %all_to_all.10.after_ref, ...), custom_call_target="tpu_custom_call" | custom-call | flops 352321536 | bytes 22020096 | tf_op jit(solution)/shard_map/load_early/pallas_call | solution.py:359
  29.7 0.0 collective-permute-done.refs_1_.refs_2_
  29.7 0.3 collective-permute-start.1
  30.1 0.0 collective-permute-done.3.refs_0_.refs_1_
  30.1 1.4 %partial.2 = (f32[64,512]{1,0:T(8,128)S(1)}, f32[64,512]{1,0:T(8,128)S(1)}) custom-call(s32[1]{0:T(128)} %bitcast.2.me_ref, f32[64,512]{1,0:T(8,128)S(1)} %get-tuple-element.42.after_ref.refs_5_, bf16[7168,512]{1,0:T(8,128)(2,1)S(1)} %get-tuple-element.43.gate_ref.refs_2_, bf16[7168,512]{1,0:T(8,128)(2,1)S(1)} %get-tuple-element.44.up_ref.refs_3_, ...), custom_call_target="tpu_custom_call" | custom-call | flops 469762048 | bytes 7340032 | tf_op jit(solution)/shard_map/partial/pallas_call | solution.py:297
  31.4 0.0 collective-permute-done.2.refs_1_.refs_2_
  31.4 0.3 collective-permute-start.4
  31.7 0.0 collective-permute-done.5.refs_0_.refs_1_
  31.7 1.2 %partial.3.refs_10_ = f32[64,512]{1,0:T(8,128)S(1)} custom-call(s32[1]{0:T(128)} %bitcast.2.me_ref, f32[64,512]{1,0:T(8,128)S(1)} %get-tuple-element.51.after_ref.refs_8_, bf16[7168,512]{1,0:T(8,128)(2,1)S(1)} %get-tuple-element.43.gate_ref.refs_2_, bf16[7168,512]{1,0:T(8,128)(2,1)S(1)} %get-tuple-element.44.up_ref.refs_3_, ...), custom_call_target="tpu_custom_call" | custom-call | flops 234881024 | bytes 3670016 | tf_op jit(solution)/shard_map/partial/pallas_call | solution.py:297
  33.0 0.0 collective-permute-done.1.refs_0_.refs_3_
  33.0 0.0 collective-permute-done.4.refs_1_.refs_3_
  33.0 2.5 %late.1 = (bf16[64,512]{1,0:T(8,128)(2,1)S(1)}, bf16[64,512]{1,0:T(8,128)(2,1)S(1)}, bf16[64,512]{1,0:T(8,128)(2,1)S(1)}, bf16[64,128]{1,0:T(8,128)(2,1)S(1)}, bf16[64,1920]{1,0:T(8,128)(2,1)S(1)}) custom-call(s32[1]{0:T(128)} %bitcast.2.me_ref, bf16[64,1792]{1,0:T(8,128)(2,1)S(1)} %collective-permute-done.1.refs_0_.refs_3_, ...), custom_call_target="tpu_custom_call" | custom-call | flops 587202560 | bytes 9175040 | tf_op jit(solution)/shard_map/late/pallas_call | solution.py:416
  35.6 0.3 collective-permute-start.6
  35.9 1.2 %terms.2 = bf16[64,1920]{1,0:T(8,128)(2,1)S(1)} custom-call(s32[1]{0:T(128)} %bitcast.2.me_ref, bf16[64,128]{1,0:T(8,128)(2,1)S(1)} %get-tuple-element.53.after_ref.last_ref.cols_ref, bf16[64,128]{1,0:T(8,128)(2,1)S(1)} %get-tuple-element.53.after_ref.last_ref.cols_ref, bf16[64,512]{1,0:T(8,128)(2,1)S(1)} %get-tuple-element.54.d_gate_ref.refs_4_, ...), custom_call_target="tpu_custom_call" | custom-call | flops 1 | bytes 1 | tf_op jit(solution)/shard_map/terms/pallas_call | solution.py:451
  37.1 0.0 collective-permute-done.6
  37.1 0.1 add_convert_fusion.after_ref
  37.2 1.6 %collective-permute-start.7 = (bf16[64,1920]{1,0:T(8,128)(2,1)S(1)}, bf16[64,1920]{1,0:T(8,128)(2,1)S(1)}, u32[]{:S(2)}, u32[]{:S(2)}) collective-permute-start(bf16[64,1920]{1,0:T(8,128)(2,1)S(1)} %add_convert_fusion.after_ref), channel_id=1, source_target_pairs={{0,2},{1,3},{2,0},{3,1},{4,6},{5,7},{6,4},{7,5},{8,10},{9,11},{10,... | collective-permute-start | bytes 737288 | tf_op jit(solution)/shard_map/ppermute | solution.py:25
  38.8 5.2 %middle.1 = (bf16[512,7168]{1,0:T(8,128)(2,1)}, bf16[64,1920]{1,0:T(8,128)(2,1)S(1)}, bf16[64,1536]{1,0:T(8,128)(2,1)S(1)}) custom-call(s32[1]{0:T(128)} %bitcast.2.me_ref, bf16[64,1920]{1,0:T(8,128)(2,1)S(1)} %add_convert_fusion.after_ref, bf16[64,512]{1,0:T(8,128)(2,1)S(1)} %get-tuple-element.57.left_ref, ...), custom_call_target="tpu_custom_call" | custom-call | flops 939524096 | bytes 7340032 | tf_op jit(solution)/shard_map/middle/pallas_call | solution.py:573
  44.0 0.1 collective-permute-start.8
  44.1 1.3 %collective-permute-done.7.after_ref.refs_3_ = bf16[64,1920]{1,0:T(8,128)(2,1)S(1)} collective-permute-done((bf16[64,1920]{1,0:T(8,128)(2,1)S(1)}, bf16[64,1920]{1,0:T(8,128)(2,1)S(1)}, u32[]{:S(2)}, u32[]{:S(2)}) %collective-permute-start.7) | collective-permute-done | bytes 245792 | tf_op jit(solution)/shard_map/ppermute | solution.py:25
  45.4 0.3 terms.3.refs_1_
  45.7 0.8 %settle.1.after_ref = bf16[8,8,1920]{2,1,0:T(8,128)(2,1)} custom-call(bf16[64,1536]{1,0:T(8,128)(2,1)S(1)} %get-tuple-element.58.refs_0_, bf16[64,384]{1,0:T(8,128)(2,1)S(1)} %terms.3.refs_1_, bf16[64,1920]{1,0:T(8,128)(2,1)S(1)} %collective-permute-done.8.refs_2_, bf16[64,1920]{1,0:T(8,128)(2,1)S(1)} %collective-permute-done.7.after_ref.refs_3_, ...), custom_call_target="tpu_custom_call" | custom-call | bytes 1000000 | tf_op jit(solution)/shard_map/settle/pallas_call | solution.py:611
  46.5 6.2 %all-to-all-start.1 = ((bf16[8,8,1920]{2,1,0:T(8,128)(2,1)}), bf16[8,8,1920]{2,1,0:T(8,128)(2,1)S(1)}, u32[]{:S(2)}, u32[]{:S(2)}) async-start(bf16[8,8,1920]{2,1,0:T(8,128)(2,1)} %settle.1.after_ref), calls=%async_computation.1 | async-start | bytes 491520 | tf_op jit(solution)/shard_map/all_to_all | solution.py:111
  52.7 8.1 %outer_rows.1 = (bf16[7168,512]{1,0:T(8,128)(2,1)}, bf16[7168,512]{1,0:T(8,128)(2,1)}) custom-call(bf16[8,8,1920]{2,1,0:T(8,128)(2,1)} %settle.1.after_ref, bf16[64,1792]{1,0:T(8,128)(2,1)S(1)} %get-tuple-element.66.refs_0_, bf16[64,1792]{1,0:T(8,128)(2,1)S(1)} %collective-permute-done.3.refs_0_.refs_1_, ...), custom_call_target="tpu_custom_call" | custom-call | flops 939524096 | bytes 14680064 | tf_op jit(solution)/shard_map/outer_rows/pallas_call | solution.py:524
  60.9 0.0 all-to-all-done.1
  60.9 1.2 %combine.1 = (bf16[128,1792]{1,0:T(8,128)(2,1)}, f32[2,128]{1,0:T(2,128)}) custom-call(bf16[64,128]{1,0:T(8,128)(2,1)S(1)} %get-tuple-element.35.pick_ref, f32[2,128]{1,0:T(2,128)S(1)} %get-tuple-element.36.gates_ref, bf16[64,1920]{1,0:T(8,128)(2,1)S(1)} %bitcast.15), custom_call_target="tpu_custom_call" | custom-call | flops 100000000 | bytes 1000000 | tf_op jit(solution)/shard_map/combine/pallas_call | solution.py:641
  (2 shorter events, 0.0 us)
Async XLA Ops:
  19.9 9.8 %collective-permute-start = (bf16[64,1792]{1,0:T(8,128)(2,1)S(1)}, bf16[64,1792]{1,0:T(8,128)(2,1)S(1)}, u32[]{:S(2)}, u32[]{:S(2)}) collective-permute-start(bf16[64,1792]{1,0:T(8,128)(2,1)S(1)} %get-tuple-element.66.refs_0_), channel_id=1, source_target_pairs={{0,2},{1,3},{2,0},{3,1},{4,6},{5,7},{6,4},{7,5},{8,10},{9,11},{10,... | collective-permute-start | bytes 688136 | tf_op jit(solution)/shard_map/ppermute | solution.py:25
  21.5 8.6 %collective-permute-start.3 = (bf16[64,1792]{1,0:T(8,128)(2,1)S(1)}, bf16[64,1792]{1,0:T(8,128)(2,1)S(1)}, u32[]{:S(2)}, u32[]{:S(2)}) collective-permute-start(bf16[64,1792]{1,0:T(8,128)(2,1)S(1)} %get-tuple-element.66.refs_0_), channel_id=1, source_target_pairs={{0,1},{1,0},{2,3},{3,2},{4,5},{5,4},{6,7},{7,6},{8,9},{9,8},{10,11... | collective-permute-start | bytes 688136 | tf_op jit(solution)/shard_map/ppermute | solution.py:25
  21.5 10.0 %collective-permute-start.2 = (bf16[64,1792]{1,0:T(8,128)(2,1)S(1)}, bf16[64,1792]{1,0:T(8,128)(2,1)S(1)}, u32[]{:S(2)}, u32[]{:S(2)}) collective-permute-start(bf16[64,1792]{1,0:T(8,128)(2,1)S(1)} %get-tuple-element.65.refs_1_.refs_0_), channel_id=1, source_target_pairs={{0,2},{1,3},{2,0},{3,1},{4,6},{5,7},{6,4},{7,5},{8,10},{9,11},{10,... | collective-permute-start | bytes 688136 | tf_op jit(solution)/shard_map/ppermute | solution.py:25
  22.0 9.7 %collective-permute-start.5 = (bf16[64,1792]{1,0:T(8,128)(2,1)S(1)}, bf16[64,1792]{1,0:T(8,128)(2,1)S(1)}, u32[]{:S(2)}, u32[]{:S(2)}) collective-permute-start(bf16[64,1792]{1,0:T(8,128)(2,1)S(1)} %get-tuple-element.65.refs_1_.refs_0_), channel_id=1, source_target_pairs={{0,1},{1,0},{2,3},{3,2},{4,5},{5,4},{6,7},{7,6},{8,9},{9,8},{10,11... | collective-permute-start | bytes 688136 | tf_op jit(solution)/shard_map/ppermute | solution.py:25
  29.7 3.3 %collective-permute-start.1 = (bf16[64,1792]{1,0:T(8,128)(2,1)S(1)}, bf16[64,1792]{1,0:T(8,128)(2,1)S(1)}, u32[]{:S(2)}, u32[]{:S(2)}) collective-permute-start(bf16[64,1792]{1,0:T(8,128)(2,1)S(1)} %collective-permute-done.refs_1_.refs_2_), channel_id=1, source_target_pairs={{0,1},{1,0},{2,3},{3,2},{4,5},{5,4},{6,7},{7,6},{8,9},{9,8},{10,11... | collective-permute-start | bytes 688136 | tf_op jit(solution)/shard_map/ppermute | solution.py:25
  31.4 1.6 %collective-permute-start.4 = (bf16[64,1792]{1,0:T(8,128)(2,1)S(1)}, bf16[64,1792]{1,0:T(8,128)(2,1)S(1)}, u32[]{:S(2)}, u32[]{:S(2)}) collective-permute-start(bf16[64,1792]{1,0:T(8,128)(2,1)S(1)} %collective-permute-done.2.refs_1_.refs_2_), channel_id=1, source_target_pairs={{0,1},{1,0},{2,3},{3,2},{4,5},{5,4},{6,7},{7,6},{8,9},{9,8},{10,11... | collective-permute-start | bytes 688136 | tf_op jit(solution)/shard_map/ppermute | solution.py:25
  35.6 1.6 %collective-permute-start.6 = (bf16[64,1920]{1,0:T(8,128)(2,1)S(1)}, bf16[64,1920]{1,0:T(8,128)(2,1)S(1)}, u32[]{:S(2)}, u32[]{:S(2)}) collective-permute-start(bf16[64,1920]{1,0:T(8,128)(2,1)S(1)} %get-tuple-element.56), channel_id=1, source_target_pairs={{0,1},{1,0},{2,3},{3,2},{4,5},{5,4},{6,7},{7,6},{8,9},{9,8},{10,11... | collective-permute-start | bytes 737288 | tf_op jit(solution)/shard_map/ppermute | solution.py:25
  37.2 8.2 %collective-permute-start.7 = (bf16[64,1920]{1,0:T(8,128)(2,1)S(1)}, bf16[64,1920]{1,0:T(8,128)(2,1)S(1)}, u32[]{:S(2)}, u32[]{:S(2)}) collective-permute-start(bf16[64,1920]{1,0:T(8,128)(2,1)S(1)} %add_convert_fusion.after_ref), channel_id=1, source_target_pairs={{0,2},{1,3},{2,0},{3,1},{4,6},{5,7},{6,4},{7,5},{8,10},{9,11},{10,... | collective-permute-start | bytes 737288 | tf_op jit(solution)/shard_map/ppermute | solution.py:25
  44.0 1.7 %collective-permute-start.8 = (bf16[64,1920]{1,0:T(8,128)(2,1)S(1)}, bf16[64,1920]{1,0:T(8,128)(2,1)S(1)}, u32[]{:S(2)}, u32[]{:S(2)}) collective-permute-start(bf16[64,1920]{1,0:T(8,128)(2,1)S(1)} %get-tuple-element.60), channel_id=1, source_target_pairs={{0,1},{1,0},{2,3},{3,2},{4,5},{5,4},{6,7},{7,6},{8,9},{9,8},{10,11... | collective-permute-start | bytes 737288 | tf_op jit(solution)/shard_map/ppermute | solution.py:25
  46.5 14.4 %all-to-all-start.1 = ((bf16[8,8,1920]{2,1,0:T(8,128)(2,1)}), bf16[8,8,1920]{2,1,0:T(8,128)(2,1)S(1)}, u32[]{:S(2)}, u32[]{:S(2)}) async-start(bf16[8,8,1920]{2,1,0:T(8,128)(2,1)} %settle.1.after_ref), calls=%async_computation.1 | async-start | bytes 491520 | tf_op jit(solution)/shard_map/all_to_all | solution.py:111

commit v6 on v4

--- a/solution.py
+++ b/solution.py
@@ -95,7 +95,9 @@
 def owner_order(experts):
     places = experts // 2
     near = sorted(range(places), key=lambda place: abs(2 * place - places + 1))
-    return [2 * place + last for place in near for last in range(2)]
+    return [
+        2 * place + last for i in range(0, places, 2) for last in range(2) for place in near[i:i + 2]
+    ]
 
 
 def row_owners(experts, tokens):

time: 62.6 us -> 62.6 us (level)
  no operation moved by 1% of the time
where the time goes in v6:
time: 62.6 us; the launch traced here: 62.3 us
  Pallas kernels  31.1 us (50%)
  blocking collectives  20.2 us (32%)
  starting transfers between devices  8.55 us (14%)
  waiting for transfers between devices  1.64 us (3%)
  between operations  0.74 us (1%)
    all_to_all x1, blocking collectives, exchange(): lax.all_to_all(blocks, axis, split_axis=0, concat_axis=0, axis_index_grou...  20.2 us
    pallas_call x1, Pallas kernels, outer_rows(): pl.pallas_call(functools.partial(outer_rows_kernel, block, len(lefts)), o...  8.16 us
    pallas_call x1, Pallas kernels, load_early(): pl.pallas_call(lambda after_ref, *refs: load_early_kernel(*refs), out_sha...  7.44 us
    pallas_call x1, Pallas kernels, middle(): pl.pallas_call(functools.partial(middle_kernel, block, pieces, feat), out...  5.22 us
    ppermute x9, starting transfers between devices, swap(): return lax.ppermute(value, axis, [(i, i ^ mask) for i in range(size)])  4.91 us
    all_to_all x1, starting transfers between devices, exchange(): lax.all_to_all(blocks, axis, split_axis=0, concat_axis=0, axis_index_grou...  3.64 us
    pallas_call x2, Pallas kernels, partial(): pl.pallas_call(functools.partial(kernel, rels), out_shape=[jax.ShapeDtype...  2.59 us
    pallas_call x1, Pallas kernels, late(): pl.pallas_call(functools.partial(late_kernel, rels, feat), out_shape=[jax...  2.55 us
  transfers between devices with their start and end apart: 10, of which 2 were waited for; matrix products, arithmetic and copies ran while one was open for 0% of the time, Pallas kernels for 40%

profile of v6, /device:TPU:0, one launch (start us, length us, event | category | flops | bytes accessed | tf_op | source)
XLA Modules:
  0.0 62.3 jit_solution(3254174732316587793)
XLA Ops:
  0.6 1.7 %pack.1 = (bf16[8,16,1792]{2,1,0:T(8,128)(2,1)S(1)}, bf16[64,128]{1,0:T(8,128)(2,1)S(1)}, f32[2,128]{1,0:T(2,128)S(1)}) custom-call(s32[2,128]{1,0:T(2,128)} %bitcast.20, bf16[2,128]{1,0:T(2,128)(2,1)} %bitcast.21, bf16[128,1792]{1,0:T(8,128)(2,1)} %x_hbm.1, bf16[128,1792]{1,0:T(8,128)(2,1)} %d_hbm.1), custom_call_target="tpu_custom_call" | custom-call | flops 100000000 | bytes 2000000 | tf_op jit(solution)/shard_map/pack/pallas_call | solution.py:177
  2.3 20.2 %all_to_all.10.after_ref = bf16[8,16,1792]{2,1,0:T(8,128)(2,1)S(1)} all-to-all(bf16[8,16,1792]{2,1,0:T(8,128)(2,1)S(1)} %get-tuple-element.37), channel_id=1, replica_groups={{8,16,12,20,0,24,4,28},{9,17,13,21,1,25,5,29},{10,18,14,22,2,26,6,30},{..., dimensions={0} | all-to-all | bytes 917504 | tf_op jit(solution)/shard_map/all_to_all | solution.py:113
  22.5 1.6 %collective-permute-start = (bf16[64,1792]{1,0:T(8,128)(2,1)S(1)}, bf16[64,1792]{1,0:T(8,128)(2,1)S(1)}, u32[]{:S(2)}, u32[]{:S(2)}) collective-permute-start(bf16[64,1792]{1,0:T(8,128)(2,1)S(1)} %get-tuple-element.66.refs_0_), channel_id=1, source_target_pairs={{0,2},{1,3},{2,0},{3,1},{4,6},{5,7},{6,4},{7,5},{8,10},{9,11},{10,... | collective-permute-start | bytes 688136 | tf_op jit(solution)/shard_map/ppermute | solution.py:25
  24.0 0.0 collective-permute-start.3
  24.0 0.5 collective-permute-start.2
  24.6 0.2 collective-permute-start.5
  24.8 7.4 %load_early.1 = (bf16[7168,512]{1,0:T(8,128)(2,1)S(1)}, bf16[7168,512]{1,0:T(8,128)(2,1)S(1)}, bf16[512,7168]{1,0:T(8,128)(2,1)S(1)}, f32[64,512]{1,0:T(8,128)S(...) custom-call(bf16[8,16,1792]{2,1,0:T(8,128)(2,1)S(1)} %all_to_all.10.after_ref, ...), custom_call_target="tpu_custom_call" | custom-call | flops 352321536 | bytes 22020096 | tf_op jit(solution)/shard_map/load_early/pallas_call | solution.py:361
  32.3 0.0 collective-permute-done.refs_1_.refs_2_
  32.3 0.3 collective-permute-start.1
  32.6 0.0 collective-permute-done.3.refs_0_.refs_1_
  32.6 1.4 %partial.2 = (f32[64,512]{1,0:T(8,128)S(1)}, f32[64,512]{1,0:T(8,128)S(1)}) custom-call(s32[1]{0:T(128)} %bitcast.2.me_ref, f32[64,512]{1,0:T(8,128)S(1)} %get-tuple-element.42.after_ref.refs_5_, bf16[7168,512]{1,0:T(8,128)(2,1)S(1)} %get-tuple-element.43.gate_ref.refs_2_, bf16[7168,512]{1,0:T(8,128)(2,1)S(1)} %get-tuple-element.44.up_ref.refs_3_, ...), custom_call_target="tpu_custom_call" | custom-call | flops 469762048 | bytes 7340032 | tf_op jit(solution)/shard_map/partial/pallas_call | solution.py:299
  34.0 0.0 collective-permute-done.2.refs_1_.refs_2_
  34.0 0.3 collective-permute-start.4
  34.3 0.0 collective-permute-done.5.refs_0_.refs_1_
  34.3 1.2 %partial.3.refs_10_ = f32[64,512]{1,0:T(8,128)S(1)} custom-call(s32[1]{0:T(128)} %bitcast.2.me_ref, f32[64,512]{1,0:T(8,128)S(1)} %get-tuple-element.51.after_ref.refs_8_, bf16[7168,512]{1,0:T(8,128)(2,1)S(1)} %get-tuple-element.43.gate_ref.refs_2_, bf16[7168,512]{1,0:T(8,128)(2,1)S(1)} %get-tuple-element.44.up_ref.refs_3_, ...), custom_call_target="tpu_custom_call" | custom-call | flops 234881024 | bytes 3670016 | tf_op jit(solution)/shard_map/partial/pallas_call | solution.py:299
  35.5 0.0 collective-permute-done.1.refs_0_.refs_3_
  35.5 0.0 collective-permute-done.4.refs_1_.refs_3_
  35.6 2.5 %late.1 = (bf16[64,512]{1,0:T(8,128)(2,1)S(1)}, bf16[64,512]{1,0:T(8,128)(2,1)S(1)}, bf16[64,512]{1,0:T(8,128)(2,1)S(1)}, bf16[64,128]{1,0:T(8,128)(2,1)S(1)}, bf16[64,1920]{1,0:T(8,128)(2,1)S(1)}) custom-call(s32[1]{0:T(128)} %bitcast.2.me_ref, bf16[64,1792]{1,0:T(8,128)(2,1)S(1)} %collective-permute-done.1.refs_0_.refs_3_, ...), custom_call_target="tpu_custom_call" | custom-call | flops 587202560 | bytes 9175040 | tf_op jit(solution)/shard_map/late/pallas_call | solution.py:418
  38.1 0.3 collective-permute-start.6
  38.5 1.2 %terms.2 = bf16[64,1920]{1,0:T(8,128)(2,1)S(1)} custom-call(s32[1]{0:T(128)} %bitcast.2.me_ref, bf16[64,128]{1,0:T(8,128)(2,1)S(1)} %get-tuple-element.53.after_ref.last_ref.cols_ref, bf16[64,128]{1,0:T(8,128)(2,1)S(1)} %get-tuple-element.53.after_ref.last_ref.cols_ref, bf16[64,512]{1,0:T(8,128)(2,1)S(1)} %get-tuple-element.54.d_gate_ref.refs_4_, ...), custom_call_target="tpu_custom_call" | custom-call | flops 1 | bytes 1 | tf_op jit(solution)/shard_map/terms/pallas_call | solution.py:453
  39.7 0.1 add_convert_fusion.after_ref
  39.8 1.6 %collective-permute-start.7 = (bf16[64,1920]{1,0:T(8,128)(2,1)S(1)}, bf16[64,1920]{1,0:T(8,128)(2,1)S(1)}, u32[]{:S(2)}, u32[]{:S(2)}) collective-permute-start(bf16[64,1920]{1,0:T(8,128)(2,1)S(1)} %add_convert_fusion.after_ref), channel_id=1, source_target_pairs={{0,2},{1,3},{2,0},{3,1},{4,6},{5,7},{6,4},{7,5},{8,10},{9,11},{10,... | collective-permute-start | bytes 737288 | tf_op jit(solution)/shard_map/ppermute | solution.py:25
  41.3 5.2 %middle.1 = (bf16[512,7168]{1,0:T(8,128)(2,1)}, bf16[64,1920]{1,0:T(8,128)(2,1)S(1)}, bf16[64,1536]{1,0:T(8,128)(2,1)S(1)}) custom-call(s32[1]{0:T(128)} %bitcast.2.me_ref, bf16[64,1920]{1,0:T(8,128)(2,1)S(1)} %add_convert_fusion.after_ref, bf16[64,512]{1,0:T(8,128)(2,1)S(1)} %get-tuple-element.57.left_ref, ...), custom_call_target="tpu_custom_call" | custom-call | flops 939524096 | bytes 7340032 | tf_op jit(solution)/shard_map/middle/pallas_call | solution.py:575
  46.6 0.1 collective-permute-start.8
  46.6 1.3 %collective-permute-done.7.after_ref.refs_3_ = bf16[64,1920]{1,0:T(8,128)(2,1)S(1)} collective-permute-done((bf16[64,1920]{1,0:T(8,128)(2,1)S(1)}, bf16[64,1920]{1,0:T(8,128)(2,1)S(1)}, u32[]{:S(2)}, u32[]{:S(2)}) %collective-permute-start.7) | collective-permute-done | bytes 245792 | tf_op jit(solution)/shard_map/ppermute | solution.py:25
  48.0 0.3 terms.3.refs_1_
  48.3 0.0 collective-permute-done.8.refs_2_
  48.3 0.8 %settle.1.after_ref = bf16[8,8,1920]{2,1,0:T(8,128)(2,1)} custom-call(bf16[64,1536]{1,0:T(8,128)(2,1)S(1)} %get-tuple-element.58.refs_0_, bf16[64,384]{1,0:T(8,128)(2,1)S(1)} %terms.3.refs_1_, bf16[64,1920]{1,0:T(8,128)(2,1)S(1)} %collective-permute-done.8.refs_2_, bf16[64,1920]{1,0:T(8,128)(2,1)S(1)} %collective-permute-done.7.after_ref.refs_3_, ...), custom_call_target="tpu_custom_call" | custom-call | bytes 1000000 | tf_op jit(solution)/shard_map/settle/pallas_call | solution.py:613
  49.0 3.6 %all-to-all-start.1 = ((bf16[8,8,1920]{2,1,0:T(8,128)(2,1)}), bf16[8,8,1920]{2,1,0:T(8,128)(2,1)S(1)}, u32[]{:S(2)}, u32[]{:S(2)}) async-start(bf16[8,8,1920]{2,1,0:T(8,128)(2,1)} %settle.1.after_ref), calls=%async_computation.1 | async-start | bytes 491520 | tf_op jit(solution)/shard_map/all_to_all | solution.py:113
  52.7 8.2 %outer_rows.1 = (bf16[7168,512]{1,0:T(8,128)(2,1)}, bf16[7168,512]{1,0:T(8,128)(2,1)}) custom-call(bf16[8,8,1920]{2,1,0:T(8,128)(2,1)} %settle.1.after_ref, bf16[64,1792]{1,0:T(8,128)(2,1)S(1)} %get-tuple-element.66.refs_0_, bf16[64,1792]{1,0:T(8,128)(2,1)S(1)} %collective-permute-done.3.refs_0_.refs_1_, ...), custom_call_target="tpu_custom_call" | custom-call | flops 939524096 | bytes 14680064 | tf_op jit(solution)/shard_map/outer_rows/pallas_call | solution.py:526
  60.9 0.2 all-to-all-done.1
  61.1 1.2 %combine.1 = (bf16[128,1792]{1,0:T(8,128)(2,1)}, f32[2,128]{1,0:T(2,128)}) custom-call(bf16[64,128]{1,0:T(8,128)(2,1)S(1)} %get-tuple-element.35.pick_ref, f32[2,128]{1,0:T(2,128)S(1)} %get-tuple-element.36.gates_ref, bf16[64,1920]{1,0:T(8,128)(2,1)S(1)} %bitcast.15), custom_call_target="tpu_custom_call" | custom-call | flops 100000000 | bytes 1000000 | tf_op jit(solution)/shard_map/combine/pallas_call | solution.py:643
  (2 shorter events, 0.0 us)
Async XLA Ops:
  22.5 9.8 %collective-permute-start = (bf16[64,1792]{1,0:T(8,128)(2,1)S(1)}, bf16[64,1792]{1,0:T(8,128)(2,1)S(1)}, u32[]{:S(2)}, u32[]{:S(2)}) collective-permute-start(bf16[64,1792]{1,0:T(8,128)(2,1)S(1)} %get-tuple-element.66.refs_0_), channel_id=1, source_target_pairs={{0,2},{1,3},{2,0},{3,1},{4,6},{5,7},{6,4},{7,5},{8,10},{9,11},{10,... | collective-permute-start | bytes 688136 | tf_op jit(solution)/shard_map/ppermute | solution.py:25
  24.0 8.6 %collective-permute-start.3 = (bf16[64,1792]{1,0:T(8,128)(2,1)S(1)}, bf16[64,1792]{1,0:T(8,128)(2,1)S(1)}, u32[]{:S(2)}, u32[]{:S(2)}) collective-permute-start(bf16[64,1792]{1,0:T(8,128)(2,1)S(1)} %get-tuple-element.66.refs_0_), channel_id=1, source_target_pairs={{0,1},{1,0},{2,3},{3,2},{4,5},{5,4},{6,7},{7,6},{8,9},{9,8},{10,11... | collective-permute-start | bytes 688136 | tf_op jit(solution)/shard_map/ppermute | solution.py:25
  24.0 10.0 %collective-permute-start.2 = (bf16[64,1792]{1,0:T(8,128)(2,1)S(1)}, bf16[64,1792]{1,0:T(8,128)(2,1)S(1)}, u32[]{:S(2)}, u32[]{:S(2)}) collective-permute-start(bf16[64,1792]{1,0:T(8,128)(2,1)S(1)} %get-tuple-element.65.refs_1_.refs_0_), channel_id=1, source_target_pairs={{0,2},{1,3},{2,0},{3,1},{4,6},{5,7},{6,4},{7,5},{8,10},{9,11},{10,... | collective-permute-start | bytes 688136 | tf_op jit(solution)/shard_map/ppermute | solution.py:25
  24.6 9.7 %collective-permute-start.5 = (bf16[64,1792]{1,0:T(8,128)(2,1)S(1)}, bf16[64,1792]{1,0:T(8,128)(2,1)S(1)}, u32[]{:S(2)}, u32[]{:S(2)}) collective-permute-start(bf16[64,1792]{1,0:T(8,128)(2,1)S(1)} %get-tuple-element.65.refs_1_.refs_0_), channel_id=1, source_target_pairs={{0,1},{1,0},{2,3},{3,2},{4,5},{5,4},{6,7},{7,6},{8,9},{9,8},{10,11... | collective-permute-start | bytes 688136 | tf_op jit(solution)/shard_map/ppermute | solution.py:25
  32.3 3.3 %collective-permute-start.1 = (bf16[64,1792]{1,0:T(8,128)(2,1)S(1)}, bf16[64,1792]{1,0:T(8,128)(2,1)S(1)}, u32[]{:S(2)}, u32[]{:S(2)}) collective-permute-start(bf16[64,1792]{1,0:T(8,128)(2,1)S(1)} %collective-permute-done.refs_1_.refs_2_), channel_id=1, source_target_pairs={{0,1},{1,0},{2,3},{3,2},{4,5},{5,4},{6,7},{7,6},{8,9},{9,8},{10,11... | collective-permute-start | bytes 688136 | tf_op jit(solution)/shard_map/ppermute | solution.py:25
  34.0 1.5 %collective-permute-start.4 = (bf16[64,1792]{1,0:T(8,128)(2,1)S(1)}, bf16[64,1792]{1,0:T(8,128)(2,1)S(1)}, u32[]{:S(2)}, u32[]{:S(2)}) collective-permute-start(bf16[64,1792]{1,0:T(8,128)(2,1)S(1)} %collective-permute-done.2.refs_1_.refs_2_), channel_id=1, source_target_pairs={{0,1},{1,0},{2,3},{3,2},{4,5},{5,4},{6,7},{7,6},{8,9},{9,8},{10,11... | collective-permute-start | bytes 688136 | tf_op jit(solution)/shard_map/ppermute | solution.py:25
  38.1 1.6 %collective-permute-start.6 = (bf16[64,1920]{1,0:T(8,128)(2,1)S(1)}, bf16[64,1920]{1,0:T(8,128)(2,1)S(1)}, u32[]{:S(2)}, u32[]{:S(2)}) collective-permute-start(bf16[64,1920]{1,0:T(8,128)(2,1)S(1)} %get-tuple-element.56), channel_id=1, source_target_pairs={{0,1},{1,0},{2,3},{3,2},{4,5},{5,4},{6,7},{7,6},{8,9},{9,8},{10,11... | collective-permute-start | bytes 737288 | tf_op jit(solution)/shard_map/ppermute | solution.py:25
  39.8 8.2 %collective-permute-start.7 = (bf16[64,1920]{1,0:T(8,128)(2,1)S(1)}, bf16[64,1920]{1,0:T(8,128)(2,1)S(1)}, u32[]{:S(2)}, u32[]{:S(2)}) collective-permute-start(bf16[64,1920]{1,0:T(8,128)(2,1)S(1)} %add_convert_fusion.after_ref), channel_id=1, source_target_pairs={{0,2},{1,3},{2,0},{3,1},{4,6},{5,7},{6,4},{7,5},{8,10},{9,11},{10,... | collective-permute-start | bytes 737288 | tf_op jit(solution)/shard_map/ppermute | solution.py:25
  46.6 1.7 %collective-permute-start.8 = (bf16[64,1920]{1,0:T(8,128)(2,1)S(1)}, bf16[64,1920]{1,0:T(8,128)(2,1)S(1)}, u32[]{:S(2)}, u32[]{:S(2)}) collective-permute-start(bf16[64,1920]{1,0:T(8,128)(2,1)S(1)} %get-tuple-element.60), channel_id=1, source_target_pairs={{0,1},{1,0},{2,3},{3,2},{4,5},{5,4},{6,7},{7,6},{8,9},{9,8},{10,11... | collective-permute-start | bytes 737288 | tf_op jit(solution)/shard_map/ppermute | solution.py:25
  49.0 12.0 %all-to-all-start.1 = ((bf16[8,8,1920]{2,1,0:T(8,128)(2,1)}), bf16[8,8,1920]{2,1,0:T(8,128)(2,1)S(1)}, u32[]{:S(2)}, u32[]{:S(2)}) async-start(bf16[8,8,1920]{2,1,0:T(8,128)(2,1)} %settle.1.after_ref), calls=%async_computation.1 | async-start | bytes 491520 | tf_op jit(solution)/shard_map/all_to_all | solution.py:113

commit v7 on v5

--- a/solution.py
+++ b/solution.py
@@ -618,39 +618,42 @@
     )(*[keep(a) for a in (*pieces, *parts)], pltpu.with_memory_space_constraint(after, pltpu.HBM))
 
 
-def combine_kernel(feat, block, pick_ref, gates_ref, rows_ref, grad_ref, gate_ref):
+def combine_kernel(feat, block, pick_ref, gates_ref, rows_ref, grad_hbm, gate_ref, stage, sems):
     pick = pick_ref[...]
-    at = pl.ds(pl.multiple_of(pl.program_id(0) * block, block), block) if block < feat else slice(0, feat)
-    grad_ref[...] = lax.dot_general(
-        pick, rows_ref[:, at], (((0,), (0,)), ((), ())), preferred_element_type=F32
-    ).astype(BF16)
-
-    @pl.when(pl.program_id(0) == 0)
-    def _():
-        rows, count = pick.shape
-        experts = rows // CAP
-        terms = pick.astype(F32) * rows_ref[:, feat:].astype(F32)
-        low = row_owners(experts, count) < experts // 2
-        for i, part in enumerate((jnp.where(low, terms, 0.0), jnp.where(low, 0.0, terms))):
-            gate_ref[i:i + 1, :] = jnp.sum(part, axis=0, keepdims=True) / gates_ref[i:i + 1, :]
+    turned = pick.astype(F32).T.astype(BF16)
+    copies = []
+    for i, low in enumerate(range(0, feat, block)):
+        at = slice(low, low + block)
+        stage[:, at] = jnp.dot(turned, rows_ref[:, at], preferred_element_type=F32).astype(BF16)
+        copies.append(pltpu.make_async_copy(stage.at[:, at], grad_hbm.at[:, at], sems.at[i]))
+        copies[-1].start()
+    rows, count = pick.shape
+    experts = rows // CAP
+    terms = pick.astype(F32) * rows_ref[:, feat:].astype(F32)
+    low = row_owners(experts, count) < experts // 2
+    for i, part in enumerate((jnp.where(low, terms, 0.0), jnp.where(low, 0.0, terms))):
+        gate_ref[i:i + 1, :] = jnp.sum(part, axis=0, keepdims=True) / gates_ref[i:i + 1, :]
+    for copy in copies:
+        copy.wait()
 
 
 def combine(pick, gates, rows, feat):
     count = pick.shape[1]
-    block = column_block(feat)
+    block = 2 * LANES if feat % (2 * LANES) == 0 else feat
     return pl.pallas_call(
         functools.partial(combine_kernel, feat, block),
-        grid=(feat // block,),
         out_shape=[
             jax.ShapeDtypeStruct((count, feat), BF16),
             jax.ShapeDtypeStruct((2, count), F32),
         ],
         in_specs=[VMEM] * 3,
-        out_specs=[
-            pl.BlockSpec((count, block), lambda i: (0, i)),
-            pl.BlockSpec((2, count), lambda i: (0, 0)),
+        out_specs=[pl.BlockSpec(memory_space=pltpu.HBM), VMEM],
+        scratch_shapes=[
+            pltpu.VMEM((count, feat), BF16),
+            pltpu.SemaphoreType.DMA((feat // block,)),
         ],
         cost_estimate=pl.CostEstimate(flops=10**8, bytes_accessed=10**6, transcendentals=0),
+        compiler_params=pltpu.CompilerParams(vmem_limit_bytes=2**23),
         name="combine",
     )(*[keep(a) for a in (pick, gates, rows)])
 
@@ -709,7 +712,7 @@
     last = held[max(held)] if held else cols
     wide = feat * shards
     other = sum_far(held, "expert")
-    half = max(LANES, (feat - 2 * LANES) // LANES * LANES)
+    half = max(LANES, (feat - LANES) // LANES * LANES)
     pieces = ([(1, 0, feat)] if shards > 1 else []) + [(0, 0, half)]
     grad_down, *sent, first = middle(
         hidden, d, last, wide // 8, pieces, me_ref, d_gate, d_up, cols, *weights[:2], feat

time: 62.4 us -> 63.1 us (1.011)
  transfers between devices with their start and end apart: 10 -> 10, of which waited for: 1 -> 2; matrix products, arithmetic and copies ran while one was open for 0% -> 0% of each run, Pallas kernels for 40% -> 40%
where the time goes in v7:
time: 63.1 us; the launch traced here: 62.8 us
  Pallas kernels  31.7 us (50%)
  blocking collectives  17.6 us (28%)
  starting transfers between devices  11.2 us (18%)
  waiting for transfers between devices  1.32 us (2%)
  between operations  0.91 us (1%)
    all_to_all x1, blocking collectives, exchange(): lax.all_to_all(blocks, axis, split_axis=0, concat_axis=0, axis_index_grou...  17.6 us
    pallas_call x1, Pallas kernels, outer_rows(): pl.pallas_call(functools.partial(outer_rows_kernel, block, len(lefts)), o...  8.15 us
    pallas_call x1, Pallas kernels, load_early(): pl.pallas_call(lambda after_ref, *refs: load_early_kernel(*refs), out_sha...  7.44 us
    all_to_all x1, starting transfers between devices, exchange(): lax.all_to_all(blocks, axis, split_axis=0, concat_axis=0, axis_index_grou...  6.24 us
    pallas_call x1, Pallas kernels, middle(): pl.pallas_call(functools.partial(middle_kernel, block, pieces, feat), out...  5.53 us
    ppermute x9, starting transfers between devices, swap(): return lax.ppermute(value, axis, [(i, i ^ mask) for i in range(size)])  4.94 us
    pallas_call x2, Pallas kernels, partial(): pl.pallas_call(functools.partial(kernel, rels), out_shape=[jax.ShapeDtype...  2.59 us
    pallas_call x1, Pallas kernels, late(): pl.pallas_call(functools.partial(late_kernel, rels, feat), out_shape=[jax...  2.54 us
  transfers between devices with their start and end apart: 10, of which 2 were waited for; matrix products, arithmetic and copies ran while one was open for 0% of the time, Pallas kernels for 40%

profile of v7, /device:TPU:0, one launch (start us, length us, event | category | flops | bytes accessed | tf_op | source)
XLA Modules:
  0.0 62.8 jit_solution(17597213281954778243)
XLA Ops:
  0.6 1.7 %pack.1 = (bf16[8,16,1792]{2,1,0:T(8,128)(2,1)S(1)}, bf16[64,128]{1,0:T(8,128)(2,1)S(1)}, f32[2,128]{1,0:T(2,128)S(1)}) custom-call(s32[2,128]{1,0:T(2,128)} %bitcast.20, bf16[2,128]{1,0:T(2,128)(2,1)} %bitcast.21, bf16[128,1792]{1,0:T(8,128)(2,1)} %x_hbm.1, bf16[128,1792]{1,0:T(8,128)(2,1)} %d_hbm.1), custom_call_target="tpu_custom_call" | custom-call | flops 100000000 | bytes 2000000 | tf_op jit(solution)/shard_map/pack/pallas_call | solution.py:175
  2.3 17.6 %all_to_all.10.after_ref = bf16[8,16,1792]{2,1,0:T(8,128)(2,1)S(1)} all-to-all(bf16[8,16,1792]{2,1,0:T(8,128)(2,1)S(1)} %get-tuple-element.37), channel_id=1, replica_groups={{20,16,12,8,28,24,4,0},{21,17,13,9,29,25,5,1},{22,18,14,10,30,26,6,2},{..., dimensions={0} | all-to-all | bytes 917504 | tf_op jit(solution)/shard_map/all_to_all | solution.py:111
  19.9 1.6 %collective-permute-start = (bf16[64,1792]{1,0:T(8,128)(2,1)S(1)}, bf16[64,1792]{1,0:T(8,128)(2,1)S(1)}, u32[]{:S(2)}, u32[]{:S(2)}) collective-permute-start(bf16[64,1792]{1,0:T(8,128)(2,1)S(1)} %get-tuple-element.66.refs_0_), channel_id=1, source_target_pairs={{0,2},{1,3},{2,0},{3,1},{4,6},{5,7},{6,4},{7,5},{8,10},{9,11},{10,... | collective-permute-start | bytes 688136 | tf_op jit(solution)/shard_map/ppermute | solution.py:25
  21.5 0.0 collective-permute-start.3
  21.5 0.5 collective-permute-start.2
  22.0 0.2 collective-permute-start.5
  22.2 7.4 %load_early.1 = (bf16[7168,512]{1,0:T(8,128)(2,1)S(1)}, bf16[7168,512]{1,0:T(8,128)(2,1)S(1)}, bf16[512,7168]{1,0:T(8,128)(2,1)S(1)}, f32[64,512]{1,0:T(8,128)S(...) custom-call(bf16[8,16,1792]{2,1,0:T(8,128)(2,1)S(1)} %all_to_all.10.after_ref, ...), custom_call_target="tpu_custom_call" | custom-call | flops 352321536 | bytes 22020096 | tf_op jit(solution)/shard_map/load_early/pallas_call | solution.py:359
  29.7 0.0 collective-permute-done.refs_1_.refs_2_
  29.7 0.3 collective-permute-start.1
  30.1 0.0 collective-permute-done.3.refs_0_.refs_1_
  30.1 1.4 %partial.2 = (f32[64,512]{1,0:T(8,128)S(1)}, f32[64,512]{1,0:T(8,128)S(1)}) custom-call(s32[1]{0:T(128)} %bitcast.2.me_ref, f32[64,512]{1,0:T(8,128)S(1)} %get-tuple-element.42.after_ref.refs_5_, bf16[7168,512]{1,0:T(8,128)(2,1)S(1)} %get-tuple-element.43.gate_ref.refs_2_, bf16[7168,512]{1,0:T(8,128)(2,1)S(1)} %get-tuple-element.44.up_ref.refs_3_, ...), custom_call_target="tpu_custom_call" | custom-call | flops 469762048 | bytes 7340032 | tf_op jit(solution)/shard_map/partial/pallas_call | solution.py:297
  31.4 0.0 collective-permute-done.2.refs_1_.refs_2_
  31.4 0.3 collective-permute-start.4
  31.7 1.2 %partial.3.refs_10_ = f32[64,512]{1,0:T(8,128)S(1)} custom-call(s32[1]{0:T(128)} %bitcast.2.me_ref, f32[64,512]{1,0:T(8,128)S(1)} %get-tuple-element.51.after_ref.refs_8_, bf16[7168,512]{1,0:T(8,128)(2,1)S(1)} %get-tuple-element.43.gate_ref.refs_2_, bf16[7168,512]{1,0:T(8,128)(2,1)S(1)} %get-tuple-element.44.up_ref.refs_3_, ...), custom_call_target="tpu_custom_call" | custom-call | flops 234881024 | bytes 3670016 | tf_op jit(solution)/shard_map/partial/pallas_call | solution.py:297
  33.0 0.0 collective-permute-done.1.refs_0_.refs_3_
  33.0 0.0 collective-permute-done.4.refs_1_.refs_3_
  33.0 2.5 %late.1 = (bf16[64,512]{1,0:T(8,128)(2,1)S(1)}, bf16[64,512]{1,0:T(8,128)(2,1)S(1)}, bf16[64,512]{1,0:T(8,128)(2,1)S(1)}, bf16[64,128]{1,0:T(8,128)(2,1)S(1)}, bf16[64,1920]{1,0:T(8,128)(2,1)S(1)}) custom-call(s32[1]{0:T(128)} %bitcast.2.me_ref, bf16[64,1792]{1,0:T(8,128)(2,1)S(1)} %collective-permute-done.1.refs_0_.refs_3_, ...), custom_call_target="tpu_custom_call" | custom-call | flops 587202560 | bytes 9175040 | tf_op jit(solution)/shard_map/late/pallas_call | solution.py:416
  35.5 0.4 collective-permute-start.6
  35.9 1.2 %terms.2 = bf16[64,1920]{1,0:T(8,128)(2,1)S(1)} custom-call(s32[1]{0:T(128)} %bitcast.2.me_ref, bf16[64,128]{1,0:T(8,128)(2,1)S(1)} %get-tuple-element.53.after_ref.last_ref.cols_ref, bf16[64,128]{1,0:T(8,128)(2,1)S(1)} %get-tuple-element.53.after_ref.last_ref.cols_ref, bf16[64,512]{1,0:T(8,128)(2,1)S(1)} %get-tuple-element.54.d_gate_ref.refs_4_, ...), custom_call_target="tpu_custom_call" | custom-call | flops 1 | bytes 1 | tf_op jit(solution)/shard_map/terms/pallas_call | solution.py:451
  37.1 0.0 collective-permute-done.6
  37.1 0.1 add_convert_fusion.after_ref
  37.2 1.6 %collective-permute-start.7 = (bf16[64,1920]{1,0:T(8,128)(2,1)S(1)}, bf16[64,1920]{1,0:T(8,128)(2,1)S(1)}, u32[]{:S(2)}, u32[]{:S(2)}) collective-permute-start(bf16[64,1920]{1,0:T(8,128)(2,1)S(1)} %add_convert_fusion.after_ref), channel_id=1, source_target_pairs={{0,2},{1,3},{2,0},{3,1},{4,6},{5,7},{6,4},{7,5},{8,10},{9,11},{10,... | collective-permute-start | bytes 737288 | tf_op jit(solution)/shard_map/ppermute | solution.py:25
  38.8 5.5 %middle.1 = (bf16[512,7168]{1,0:T(8,128)(2,1)}, bf16[64,1920]{1,0:T(8,128)(2,1)S(1)}, bf16[64,1664]{1,0:T(8,128)(2,1)S(1)}) custom-call(s32[1]{0:T(128)} %bitcast.2.me_ref, bf16[64,1920]{1,0:T(8,128)(2,1)S(1)} %add_convert_fusion.after_ref, bf16[64,512]{1,0:T(8,128)(2,1)S(1)} %get-tuple-element.57.left_ref, ...), custom_call_target="tpu_custom_call" | custom-call | flops 939524096 | bytes 7340032 | tf_op jit(solution)/shard_map/middle/pallas_call | solution.py:573
  44.3 0.1 collective-permute-start.8
  44.4 1.0 %collective-permute-done.7.after_ref.refs_3_ = bf16[64,1920]{1,0:T(8,128)(2,1)S(1)} collective-permute-done((bf16[64,1920]{1,0:T(8,128)(2,1)S(1)}, bf16[64,1920]{1,0:T(8,128)(2,1)S(1)}, u32[]{:S(2)}, u32[]{:S(2)}) %collective-permute-start.7) | collective-permute-done | bytes 245792 | tf_op jit(solution)/shard_map/ppermute | solution.py:25
  45.4 0.2 terms.3.refs_1_
  45.6 0.2 collective-permute-done.8.refs_2_
  45.9 0.8 %settle.1.after_ref = bf16[8,8,1920]{2,1,0:T(8,128)(2,1)} custom-call(bf16[64,1664]{1,0:T(8,128)(2,1)S(1)} %get-tuple-element.58.refs_0_, bf16[64,256]{1,0:T(8,128)(2,1)S(1)} %terms.3.refs_1_, bf16[64,1920]{1,0:T(8,128)(2,1)S(1)} %collective-permute-done.8.refs_2_, bf16[64,1920]{1,0:T(8,128)(2,1)S(1)} %collective-permute-done.7.after_ref.refs_3_, ...), custom_call_target="tpu_custom_call" | custom-call | bytes 1000000 | tf_op jit(solution)/shard_map/settle/pallas_call | solution.py:611
  46.7 6.2 %all-to-all-start.1 = ((bf16[8,8,1920]{2,1,0:T(8,128)(2,1)}), bf16[8,8,1920]{2,1,0:T(8,128)(2,1)S(1)}, u32[]{:S(2)}, u32[]{:S(2)}) async-start(bf16[8,8,1920]{2,1,0:T(8,128)(2,1)} %settle.1.after_ref), calls=%async_computation.1 | async-start | bytes 491520 | tf_op jit(solution)/shard_map/all_to_all | solution.py:111
  52.9 8.1 %outer_rows.1 = (bf16[7168,512]{1,0:T(8,128)(2,1)}, bf16[7168,512]{1,0:T(8,128)(2,1)}) custom-call(bf16[8,8,1920]{2,1,0:T(8,128)(2,1)} %settle.1.after_ref, bf16[64,1792]{1,0:T(8,128)(2,1)S(1)} %get-tuple-element.66.refs_0_, bf16[64,1792]{1,0:T(8,128)(2,1)S(1)} %collective-permute-done.3.refs_0_.refs_1_, ...), custom_call_target="tpu_custom_call" | custom-call | flops 939524096 | bytes 14680064 | tf_op jit(solution)/shard_map/outer_rows/pallas_call | solution.py:524
  61.0 0.0 all-to-all-done.1
  61.1 1.6 %combine.1 = (bf16[128,1792]{1,0:T(8,128)(2,1)}, f32[2,128]{1,0:T(2,128)}) custom-call(bf16[64,128]{1,0:T(8,128)(2,1)S(1)} %get-tuple-element.35.pick_ref, f32[2,128]{1,0:T(2,128)S(1)} %get-tuple-element.36.gates_ref, bf16[64,1920]{1,0:T(8,128)(2,1)S(1)} %bitcast.15), custom_call_target="tpu_custom_call" | custom-call | flops 100000000 | bytes 1000000 | tf_op jit(solution)/shard_map/combine/pallas_call | solution.py:643
  (2 shorter events, 0.0 us)
Async XLA Ops:
  19.9 9.8 %collective-permute-start = (bf16[64,1792]{1,0:T(8,128)(2,1)S(1)}, bf16[64,1792]{1,0:T(8,128)(2,1)S(1)}, u32[]{:S(2)}, u32[]{:S(2)}) collective-permute-start(bf16[64,1792]{1,0:T(8,128)(2,1)S(1)} %get-tuple-element.66.refs_0_), channel_id=1, source_target_pairs={{0,2},{1,3},{2,0},{3,1},{4,6},{5,7},{6,4},{7,5},{8,10},{9,11},{10,... | collective-permute-start | bytes 688136 | tf_op jit(solution)/shard_map/ppermute | solution.py:25
  21.5 8.6 %collective-permute-start.3 = (bf16[64,1792]{1,0:T(8,128)(2,1)S(1)}, bf16[64,1792]{1,0:T(8,128)(2,1)S(1)}, u32[]{:S(2)}, u32[]{:S(2)}) collective-permute-start(bf16[64,1792]{1,0:T(8,128)(2,1)S(1)} %get-tuple-element.66.refs_0_), channel_id=1, source_target_pairs={{0,1},{1,0},{2,3},{3,2},{4,5},{5,4},{6,7},{7,6},{8,9},{9,8},{10,11... | collective-permute-start | bytes 688136 | tf_op jit(solution)/shard_map/ppermute | solution.py:25
  21.5 10.0 %collective-permute-start.2 = (bf16[64,1792]{1,0:T(8,128)(2,1)S(1)}, bf16[64,1792]{1,0:T(8,128)(2,1)S(1)}, u32[]{:S(2)}, u32[]{:S(2)}) collective-permute-start(bf16[64,1792]{1,0:T(8,128)(2,1)S(1)} %get-tuple-element.65.refs_1_.refs_0_), channel_id=1, source_target_pairs={{0,2},{1,3},{2,0},{3,1},{4,6},{5,7},{6,4},{7,5},{8,10},{9,11},{10,... | collective-permute-start | bytes 688136 | tf_op jit(solution)/shard_map/ppermute | solution.py:25
  22.0 9.7 %collective-permute-start.5 = (bf16[64,1792]{1,0:T(8,128)(2,1)S(1)}, bf16[64,1792]{1,0:T(8,128)(2,1)S(1)}, u32[]{:S(2)}, u32[]{:S(2)}) collective-permute-start(bf16[64,1792]{1,0:T(8,128)(2,1)S(1)} %get-tuple-element.65.refs_1_.refs_0_), channel_id=1, source_target_pairs={{0,1},{1,0},{2,3},{3,2},{4,5},{5,4},{6,7},{7,6},{8,9},{9,8},{10,11... | collective-permute-start | bytes 688136 | tf_op jit(solution)/shard_map/ppermute | solution.py:25
  29.7 3.3 %collective-permute-start.1 = (bf16[64,1792]{1,0:T(8,128)(2,1)S(1)}, bf16[64,1792]{1,0:T(8,128)(2,1)S(1)}, u32[]{:S(2)}, u32[]{:S(2)}) collective-permute-start(bf16[64,1792]{1,0:T(8,128)(2,1)S(1)} %collective-permute-done.refs_1_.refs_2_), channel_id=1, source_target_pairs={{0,1},{1,0},{2,3},{3,2},{4,5},{5,4},{6,7},{7,6},{8,9},{9,8},{10,11... | collective-permute-start | bytes 688136 | tf_op jit(solution)/shard_map/ppermute | solution.py:25
  31.4 1.6 %collective-permute-start.4 = (bf16[64,1792]{1,0:T(8,128)(2,1)S(1)}, bf16[64,1792]{1,0:T(8,128)(2,1)S(1)}, u32[]{:S(2)}, u32[]{:S(2)}) collective-permute-start(bf16[64,1792]{1,0:T(8,128)(2,1)S(1)} %collective-permute-done.2.refs_1_.refs_2_), channel_id=1, source_target_pairs={{0,1},{1,0},{2,3},{3,2},{4,5},{5,4},{6,7},{7,6},{8,9},{9,8},{10,11... | collective-permute-start | bytes 688136 | tf_op jit(solution)/shard_map/ppermute | solution.py:25
  35.5 1.6 %collective-permute-start.6 = (bf16[64,1920]{1,0:T(8,128)(2,1)S(1)}, bf16[64,1920]{1,0:T(8,128)(2,1)S(1)}, u32[]{:S(2)}, u32[]{:S(2)}) collective-permute-start(bf16[64,1920]{1,0:T(8,128)(2,1)S(1)} %get-tuple-element.56), channel_id=1, source_target_pairs={{0,1},{1,0},{2,3},{3,2},{4,5},{5,4},{6,7},{7,6},{8,9},{9,8},{10,11... | collective-permute-start | bytes 737288 | tf_op jit(solution)/shard_map/ppermute | solution.py:25
  37.2 8.2 %collective-permute-start.7 = (bf16[64,1920]{1,0:T(8,128)(2,1)S(1)}, bf16[64,1920]{1,0:T(8,128)(2,1)S(1)}, u32[]{:S(2)}, u32[]{:S(2)}) collective-permute-start(bf16[64,1920]{1,0:T(8,128)(2,1)S(1)} %add_convert_fusion.after_ref), channel_id=1, source_target_pairs={{0,2},{1,3},{2,0},{3,1},{4,6},{5,7},{6,4},{7,5},{8,10},{9,11},{10,... | collective-permute-start | bytes 737288 | tf_op jit(solution)/shard_map/ppermute | solution.py:25
  44.3 1.6 %collective-permute-start.8 = (bf16[64,1920]{1,0:T(8,128)(2,1)S(1)}, bf16[64,1920]{1,0:T(8,128)(2,1)S(1)}, u32[]{:S(2)}, u32[]{:S(2)}) collective-permute-start(bf16[64,1920]{1,0:T(8,128)(2,1)S(1)} %get-tuple-element.60), channel_id=1, source_target_pairs={{0,1},{1,0},{2,3},{3,2},{4,5},{5,4},{6,7},{7,6},{8,9},{9,8},{10,11... | collective-permute-start | bytes 737288 | tf_op jit(solution)/shard_map/ppermute | solution.py:25
  46.7 14.4 %all-to-all-start.1 = ((bf16[8,8,1920]{2,1,0:T(8,128)(2,1)}), bf16[8,8,1920]{2,1,0:T(8,128)(2,1)S(1)}, u32[]{:S(2)}, u32[]{:S(2)}) async-start(bf16[8,8,1920]{2,1,0:T(8,128)(2,1)} %settle.1.after_ref), calls=%async_computation.1 | async-start | bytes 491520 | tf_op jit(solution)/shard_map/all_to_all | solution.py:111

commit v8 on v5

--- a/solution.py
+++ b/solution.py
@@ -326,27 +326,30 @@
     def copies(rel):
         at = place(rel)
         return [
-            pltpu.make_async_copy(src.at[where], dst.at[where], sems.at[i, rel])
-            for i, (src, dst, where) in enumerate(
-                ((gate_in, gate, at), (up_in, up, at), (down_in, down, (slice(None), at)))
-            )
+            pltpu.make_async_copy(src.at[at], dst.at[at], sems.at[i, rel])
+            for i, (src, dst) in enumerate(((gate_in, gate), (up_in, up)))
         ]
 
+    height = down.shape[0] // shards
+    downs = [
+        pltpu.make_async_copy(
+            down_in.at[i * height:(i + 1) * height], down.at[i * height:(i + 1) * height], sems.at[2, i]
+        )
+        for i in range(shards)
+    ]
     first, *rest = [copies(rel) for rel in range(shards)]
-    for copy in first:
-        copy.start()
-    for group in rest:
+    for group in [first, downs] + rest:
         for copy in group:
             copy.start()
     at = place(0)
-    for i in range(3):
-        first[i].wait()
-        if i < 2:
-            sums[i][...] = jnp.dot(x0[...], (gate, up)[i][at, :], preferred_element_type=F32)
-        else:
-            sums[i][...] = lax.dot_general(
-                d0[...], down[:, at], (((1,), (1,)), ((), ())), preferred_element_type=F32
-            )
+    for copy, weight, out in zip(first, (gate, up), sums[:2]):
+        copy.wait()
+        out[...] = jnp.dot(x0[...], weight[at, :], preferred_element_type=F32)
+    for copy in downs:
+        copy.wait()
+    sums[2][...] = lax.dot_general(
+        d0[...], down[:, at], (((1,), (1,)), ((), ())), preferred_element_type=F32
+    )
     for group in rest:
         for copy in group:
             copy.wait()

time: 62.4 us -> 62.4 us (level)
  no operation moved by 1% of the time
where the time goes in v8:
time: 62.4 us; the launch traced here: 62.1 us
  Pallas kernels  31.1 us (50%)
  blocking collectives  17.6 us (28%)
  starting transfers between devices  11.2 us (18%)
  waiting for transfers between devices  1.37 us (2%)
  between operations  0.75 us (1%)
    all_to_all x1, blocking collectives, exchange(): lax.all_to_all(blocks, axis, split_axis=0, concat_axis=0, axis_index_grou...  17.6 us
    pallas_call x1, Pallas kernels, outer_rows(): pl.pallas_call(functools.partial(outer_rows_kernel, block, len(lefts)), o...  8.15 us
    pallas_call x1, Pallas kernels, load_early(): pl.pallas_call(lambda after_ref, *refs: load_early_kernel(*refs), out_sha...  7.43 us
    all_to_all x1, starting transfers between devices, exchange(): lax.all_to_all(blocks, axis, split_axis=0, concat_axis=0, axis_index_grou...  6.25 us
    pallas_call x1, Pallas kernels, middle(): pl.pallas_call(functools.partial(middle_kernel, block, pieces, feat), out...  5.23 us
    ppermute x9, starting transfers between devices, swap(): return lax.ppermute(value, axis, [(i, i ^ mask) for i in range(size)])  4.93 us
    pallas_call x2, Pallas kernels, partial(): pl.pallas_call(functools.partial(kernel, rels), out_shape=[jax.ShapeDtype...  2.6 us
    pallas_call x1, Pallas kernels, late(): pl.pallas_call(functools.partial(late_kernel, rels, feat), out_shape=[jax...  2.55 us
  transfers between devices with their start and end apart: 10, of which 1 were waited for; matrix products, arithmetic and copies ran while one was open for 0% of the time, Pallas kernels for 40%

profile of v8, /device:TPU:0, one launch (start us, length us, event | category | flops | bytes accessed | tf_op | source)
XLA Modules:
  0.0 62.1 jit_solution(13368657286548586556)
XLA Ops:
  0.6 1.7 %pack.1 = (bf16[8,16,1792]{2,1,0:T(8,128)(2,1)S(1)}, bf16[64,128]{1,0:T(8,128)(2,1)S(1)}, f32[2,128]{1,0:T(2,128)S(1)}) custom-call(s32[2,128]{1,0:T(2,128)} %bitcast.20, bf16[2,128]{1,0:T(2,128)(2,1)} %bitcast.21, bf16[128,1792]{1,0:T(8,128)(2,1)} %x_hbm.1, bf16[128,1792]{1,0:T(8,128)(2,1)} %d_hbm.1), custom_call_target="tpu_custom_call" | custom-call | flops 100000000 | bytes 2000000 | tf_op jit(solution)/shard_map/pack/pallas_call | solution.py:175
  2.3 17.6 %all_to_all.10.after_ref = bf16[8,16,1792]{2,1,0:T(8,128)(2,1)S(1)} all-to-all(bf16[8,16,1792]{2,1,0:T(8,128)(2,1)S(1)} %get-tuple-element.37), channel_id=1, replica_groups={{20,16,12,8,28,24,4,0},{21,17,13,9,29,25,5,1},{22,18,14,10,30,26,6,2},{..., dimensions={0} | all-to-all | bytes 917504 | tf_op jit(solution)/shard_map/all_to_all | solution.py:111
  19.9 1.6 %collective-permute-start = (bf16[64,1792]{1,0:T(8,128)(2,1)S(1)}, bf16[64,1792]{1,0:T(8,128)(2,1)S(1)}, u32[]{:S(2)}, u32[]{:S(2)}) collective-permute-start(bf16[64,1792]{1,0:T(8,128)(2,1)S(1)} %get-tuple-element.66.refs_0_), channel_id=1, source_target_pairs={{0,2},{1,3},{2,0},{3,1},{4,6},{5,7},{6,4},{7,5},{8,10},{9,11},{10,... | collective-permute-start | bytes 688136 | tf_op jit(solution)/shard_map/ppermute | solution.py:25
  21.5 0.0 collective-permute-start.3
  21.5 0.5 collective-permute-start.2
  22.0 0.2 collective-permute-start.5
  22.2 7.4 %load_early.1 = (bf16[7168,512]{1,0:T(8,128)(2,1)S(1)}, bf16[7168,512]{1,0:T(8,128)(2,1)S(1)}, bf16[512,7168]{1,0:T(8,128)(2,1)S(1)}, f32[64,512]{1,0:T(8,128)S(...) custom-call(bf16[8,16,1792]{2,1,0:T(8,128)(2,1)S(1)} %all_to_all.10.after_ref, ...), custom_call_target="tpu_custom_call" | custom-call | flops 352321536 | bytes 22020096 | tf_op jit(solution)/shard_map/load_early/pallas_call | solution.py:362
  29.7 0.0 collective-permute-done.refs_1_.refs_2_
  29.7 0.3 collective-permute-start.1
  30.0 0.0 collective-permute-done.3.refs_0_.refs_1_
  30.0 1.4 %partial.2 = (f32[64,512]{1,0:T(8,128)S(1)}, f32[64,512]{1,0:T(8,128)S(1)}) custom-call(s32[1]{0:T(128)} %bitcast.2.me_ref, f32[64,512]{1,0:T(8,128)S(1)} %get-tuple-element.42.after_ref.refs_5_, bf16[7168,512]{1,0:T(8,128)(2,1)S(1)} %get-tuple-element.43.gate_ref.refs_2_, bf16[7168,512]{1,0:T(8,128)(2,1)S(1)} %get-tuple-element.44.up_ref.refs_3_, ...), custom_call_target="tpu_custom_call" | custom-call | flops 469762048 | bytes 7340032 | tf_op jit(solution)/shard_map/partial/pallas_call | solution.py:297
  31.4 0.0 collective-permute-done.2.refs_1_.refs_2_
  31.4 0.3 collective-permute-start.4
  31.7 0.0 collective-permute-done.5.refs_0_.refs_1_
  31.7 1.2 %partial.3.refs_10_ = f32[64,512]{1,0:T(8,128)S(1)} custom-call(s32[1]{0:T(128)} %bitcast.2.me_ref, f32[64,512]{1,0:T(8,128)S(1)} %get-tuple-element.51.after_ref.refs_8_, bf16[7168,512]{1,0:T(8,128)(2,1)S(1)} %get-tuple-element.43.gate_ref.refs_2_, bf16[7168,512]{1,0:T(8,128)(2,1)S(1)} %get-tuple-element.44.up_ref.refs_3_, ...), custom_call_target="tpu_custom_call" | custom-call | flops 234881024 | bytes 3670016 | tf_op jit(solution)/shard_map/partial/pallas_call | solution.py:297
  33.0 0.0 collective-permute-done.1.refs_0_.refs_3_
  33.0 0.0 collective-permute-done.4.refs_1_.refs_3_
  33.0 2.5 %late.1 = (bf16[64,512]{1,0:T(8,128)(2,1)S(1)}, bf16[64,512]{1,0:T(8,128)(2,1)S(1)}, bf16[64,512]{1,0:T(8,128)(2,1)S(1)}, bf16[64,128]{1,0:T(8,128)(2,1)S(1)}, bf16[64,1920]{1,0:T(8,128)(2,1)S(1)}) custom-call(s32[1]{0:T(128)} %bitcast.2.me_ref, bf16[64,1792]{1,0:T(8,128)(2,1)S(1)} %collective-permute-done.1.refs_0_.refs_3_, ...), custom_call_target="tpu_custom_call" | custom-call | flops 587202560 | bytes 9175040 | tf_op jit(solution)/shard_map/late/pallas_call | solution.py:419
  35.5 0.3 collective-permute-start.6
  35.9 1.2 %terms.2 = bf16[64,1920]{1,0:T(8,128)(2,1)S(1)} custom-call(s32[1]{0:T(128)} %bitcast.2.me_ref, bf16[64,128]{1,0:T(8,128)(2,1)S(1)} %get-tuple-element.53.after_ref.last_ref.cols_ref, bf16[64,128]{1,0:T(8,128)(2,1)S(1)} %get-tuple-element.53.after_ref.last_ref.cols_ref, bf16[64,512]{1,0:T(8,128)(2,1)S(1)} %get-tuple-element.54.d_gate_ref.refs_4_, ...), custom_call_target="tpu_custom_call" | custom-call | flops 1 | bytes 1 | tf_op jit(solution)/shard_map/terms/pallas_call | solution.py:454
  37.1 0.0 collective-permute-done.6
  37.1 0.1 add_convert_fusion.after_ref
  37.2 1.6 %collective-permute-start.7 = (bf16[64,1920]{1,0:T(8,128)(2,1)S(1)}, bf16[64,1920]{1,0:T(8,128)(2,1)S(1)}, u32[]{:S(2)}, u32[]{:S(2)}) collective-permute-start(bf16[64,1920]{1,0:T(8,128)(2,1)S(1)} %add_convert_fusion.after_ref), channel_id=1, source_target_pairs={{0,2},{1,3},{2,0},{3,1},{4,6},{5,7},{6,4},{7,5},{8,10},{9,11},{10,... | collective-permute-start | bytes 737288 | tf_op jit(solution)/shard_map/ppermute | solution.py:25
  38.7 5.2 %middle.1 = (bf16[512,7168]{1,0:T(8,128)(2,1)}, bf16[64,1920]{1,0:T(8,128)(2,1)S(1)}, bf16[64,1536]{1,0:T(8,128)(2,1)S(1)}) custom-call(s32[1]{0:T(128)} %bitcast.2.me_ref, bf16[64,1920]{1,0:T(8,128)(2,1)S(1)} %add_convert_fusion.after_ref, bf16[64,512]{1,0:T(8,128)(2,1)S(1)} %get-tuple-element.57.left_ref, ...), custom_call_target="tpu_custom_call" | custom-call | flops 939524096 | bytes 7340032 | tf_op jit(solution)/shard_map/middle/pallas_call | solution.py:576
  44.0 0.1 collective-permute-start.8
  44.1 1.3 %collective-permute-done.7.after_ref.refs_3_ = bf16[64,1920]{1,0:T(8,128)(2,1)S(1)} collective-permute-done((bf16[64,1920]{1,0:T(8,128)(2,1)S(1)}, bf16[64,1920]{1,0:T(8,128)(2,1)S(1)}, u32[]{:S(2)}, u32[]{:S(2)}) %collective-permute-start.7) | collective-permute-done | bytes 245792 | tf_op jit(solution)/shard_map/ppermute | solution.py:25
  45.4 0.3 terms.3.refs_1_
  45.7 0.8 %settle.1.after_ref = bf16[8,8,1920]{2,1,0:T(8,128)(2,1)} custom-call(bf16[64,1536]{1,0:T(8,128)(2,1)S(1)} %get-tuple-element.58.refs_0_, bf16[64,384]{1,0:T(8,128)(2,1)S(1)} %terms.3.refs_1_, bf16[64,1920]{1,0:T(8,128)(2,1)S(1)} %collective-permute-done.8.refs_2_, bf16[64,1920]{1,0:T(8,128)(2,1)S(1)} %collective-permute-done.7.after_ref.refs_3_, ...), custom_call_target="tpu_custom_call" | custom-call | bytes 1000000 | tf_op jit(solution)/shard_map/settle/pallas_call | solution.py:614
  46.5 6.2 %all-to-all-start.1 = ((bf16[8,8,1920]{2,1,0:T(8,128)(2,1)}), bf16[8,8,1920]{2,1,0:T(8,128)(2,1)S(1)}, u32[]{:S(2)}, u32[]{:S(2)}) async-start(bf16[8,8,1920]{2,1,0:T(8,128)(2,1)} %settle.1.after_ref), calls=%async_computation.1 | async-start | bytes 491520 | tf_op jit(solution)/shard_map/all_to_all | solution.py:111
  52.7 8.1 %outer_rows.1 = (bf16[7168,512]{1,0:T(8,128)(2,1)}, bf16[7168,512]{1,0:T(8,128)(2,1)}) custom-call(bf16[8,8,1920]{2,1,0:T(8,128)(2,1)} %settle.1.after_ref, bf16[64,1792]{1,0:T(8,128)(2,1)S(1)} %get-tuple-element.66.refs_0_, bf16[64,1792]{1,0:T(8,128)(2,1)S(1)} %collective-permute-done.3.refs_0_.refs_1_, ...), custom_call_target="tpu_custom_call" | custom-call | flops 939524096 | bytes 14680064 | tf_op jit(solution)/shard_map/outer_rows/pallas_call | solution.py:527
  60.9 0.0 all-to-all-done.1
  60.9 1.2 %combine.1 = (bf16[128,1792]{1,0:T(8,128)(2,1)}, f32[2,128]{1,0:T(2,128)}) custom-call(bf16[64,128]{1,0:T(8,128)(2,1)S(1)} %get-tuple-element.35.pick_ref, f32[2,128]{1,0:T(2,128)S(1)} %get-tuple-element.36.gates_ref, bf16[64,1920]{1,0:T(8,128)(2,1)S(1)} %bitcast.15), custom_call_target="tpu_custom_call" | custom-call | flops 100000000 | bytes 1000000 | tf_op jit(solution)/shard_map/combine/pallas_call | solution.py:644
  (2 shorter events, 0.0 us)
Async XLA Ops:
  19.9 9.8 %collective-permute-start = (bf16[64,1792]{1,0:T(8,128)(2,1)S(1)}, bf16[64,1792]{1,0:T(8,128)(2,1)S(1)}, u32[]{:S(2)}, u32[]{:S(2)}) collective-permute-start(bf16[64,1792]{1,0:T(8,128)(2,1)S(1)} %get-tuple-element.66.refs_0_), channel_id=1, source_target_pairs={{0,2},{1,3},{2,0},{3,1},{4,6},{5,7},{6,4},{7,5},{8,10},{9,11},{10,... | collective-permute-start | bytes 688136 | tf_op jit(solution)/shard_map/ppermute | solution.py:25
  21.5 8.6 %collective-permute-start.3 = (bf16[64,1792]{1,0:T(8,128)(2,1)S(1)}, bf16[64,1792]{1,0:T(8,128)(2,1)S(1)}, u32[]{:S(2)}, u32[]{:S(2)}) collective-permute-start(bf16[64,1792]{1,0:T(8,128)(2,1)S(1)} %get-tuple-element.66.refs_0_), channel_id=1, source_target_pairs={{0,1},{1,0},{2,3},{3,2},{4,5},{5,4},{6,7},{7,6},{8,9},{9,8},{10,11... | collective-permute-start | bytes 688136 | tf_op jit(solution)/shard_map/ppermute | solution.py:25
  21.5 9.9 %collective-permute-start.2 = (bf16[64,1792]{1,0:T(8,128)(2,1)S(1)}, bf16[64,1792]{1,0:T(8,128)(2,1)S(1)}, u32[]{:S(2)}, u32[]{:S(2)}) collective-permute-start(bf16[64,1792]{1,0:T(8,128)(2,1)S(1)} %get-tuple-element.65.refs_1_.refs_0_), channel_id=1, source_target_pairs={{0,2},{1,3},{2,0},{3,1},{4,6},{5,7},{6,4},{7,5},{8,10},{9,11},{10,... | collective-permute-start | bytes 688136 | tf_op jit(solution)/shard_map/ppermute | solution.py:25
  22.0 9.7 %collective-permute-start.5 = (bf16[64,1792]{1,0:T(8,128)(2,1)S(1)}, bf16[64,1792]{1,0:T(8,128)(2,1)S(1)}, u32[]{:S(2)}, u32[]{:S(2)}) collective-permute-start(bf16[64,1792]{1,0:T(8,128)(2,1)S(1)} %get-tuple-element.65.refs_1_.refs_0_), channel_id=1, source_target_pairs={{0,1},{1,0},{2,3},{3,2},{4,5},{5,4},{6,7},{7,6},{8,9},{9,8},{10,11... | collective-permute-start | bytes 688136 | tf_op jit(solution)/shard_map/ppermute | solution.py:25
  29.7 3.3 %collective-permute-start.1 = (bf16[64,1792]{1,0:T(8,128)(2,1)S(1)}, bf16[64,1792]{1,0:T(8,128)(2,1)S(1)}, u32[]{:S(2)}, u32[]{:S(2)}) collective-permute-start(bf16[64,1792]{1,0:T(8,128)(2,1)S(1)} %collective-permute-done.refs_1_.refs_2_), channel_id=1, source_target_pairs={{0,1},{1,0},{2,3},{3,2},{4,5},{5,4},{6,7},{7,6},{8,9},{9,8},{10,11... | collective-permute-start | bytes 688136 | tf_op jit(solution)/shard_map/ppermute | solution.py:25
  31.4 1.6 %collective-permute-start.4 = (bf16[64,1792]{1,0:T(8,128)(2,1)S(1)}, bf16[64,1792]{1,0:T(8,128)(2,1)S(1)}, u32[]{:S(2)}, u32[]{:S(2)}) collective-permute-start(bf16[64,1792]{1,0:T(8,128)(2,1)S(1)} %collective-permute-done.2.refs_1_.refs_2_), channel_id=1, source_target_pairs={{0,1},{1,0},{2,3},{3,2},{4,5},{5,4},{6,7},{7,6},{8,9},{9,8},{10,11... | collective-permute-start | bytes 688136 | tf_op jit(solution)/shard_map/ppermute | solution.py:25
  35.5 1.6 %collective-permute-start.6 = (bf16[64,1920]{1,0:T(8,128)(2,1)S(1)}, bf16[64,1920]{1,0:T(8,128)(2,1)S(1)}, u32[]{:S(2)}, u32[]{:S(2)}) collective-permute-start(bf16[64,1920]{1,0:T(8,128)(2,1)S(1)} %get-tuple-element.56), channel_id=1, source_target_pairs={{0,1},{1,0},{2,3},{3,2},{4,5},{5,4},{6,7},{7,6},{8,9},{9,8},{10,11... | collective-permute-start | bytes 737288 | tf_op jit(solution)/shard_map/ppermute | solution.py:25
  37.2 8.2 %collective-permute-start.7 = (bf16[64,1920]{1,0:T(8,128)(2,1)S(1)}, bf16[64,1920]{1,0:T(8,128)(2,1)S(1)}, u32[]{:S(2)}, u32[]{:S(2)}) collective-permute-start(bf16[64,1920]{1,0:T(8,128)(2,1)S(1)} %add_convert_fusion.after_ref), channel_id=1, source_target_pairs={{0,2},{1,3},{2,0},{3,1},{4,6},{5,7},{6,4},{7,5},{8,10},{9,11},{10,... | collective-permute-start | bytes 737288 | tf_op jit(solution)/shard_map/ppermute | solution.py:25
  44.0 1.7 %collective-permute-start.8 = (bf16[64,1920]{1,0:T(8,128)(2,1)S(1)}, bf16[64,1920]{1,0:T(8,128)(2,1)S(1)}, u32[]{:S(2)}, u32[]{:S(2)}) collective-permute-start(bf16[64,1920]{1,0:T(8,128)(2,1)S(1)} %get-tuple-element.60), channel_id=1, source_target_pairs={{0,1},{1,0},{2,3},{3,2},{4,5},{5,4},{6,7},{7,6},{8,9},{9,8},{10,11... | collective-permute-start | bytes 737288 | tf_op jit(solution)/shard_map/ppermute | solution.py:25
  46.5 14.4 %all-to-all-start.1 = ((bf16[8,8,1920]{2,1,0:T(8,128)(2,1)}), bf16[8,8,1920]{2,1,0:T(8,128)(2,1)S(1)}, u32[]{:S(2)}, u32[]{:S(2)}) async-start(bf16[8,8,1920]{2,1,0:T(8,128)(2,1)} %settle.1.after_ref), calls=%async_computation.1 | async-start | bytes 491520 | tf_op jit(solution)/shard_map/all_to_all | solution.py:111
